TPU v7x, 32 devices: a whole 2x2x4 slice. The times are simulated.
32 devices in a mesh: pair: 8 (over z, x), tm: 4 (over y, core).
Axes of the slice: x: 2, y: 2, z: 4, core: 2. Of those that a mesh axis runs over, the one named last changes fastest.
Arguments:
- history: float32 [8192, 4096], P('tm', 'pair'), may hold values from -6 to 6
- round_index: int32 [1], replicated, may hold values from 0 to 14
Outputs:
- rotated: float32 [8192, 4096], P('tm', 'pair')
Inputs may be any that keep to these rules, and one draw needn't show every extreme that they name: `round_index`: the same value on every device.
All inputs are finite; a program needn't handle non-finite values.
Results may differ from a plain program's by a relative error of at most 0.0003.
Values sent between devices are 32-bit elements; how exact they have to be, the bound alone decides.
No kernel may reach another device: no remote copies, remote signals or barrier semaphores. Data moves between devices by JAX's collectives and lax.ppermute only.
A program may use at most 64 MiB of HBM per device.

v0:
```python
import jax
import jax.numpy as jnp
from jax import lax
from jax.sharding import PartitionSpec as P

STEPS = 4


epsilon = 1e-06


def shifted(shard, axis, by):
    size = lax.axis_size(axis)
    pairs = [(i, i + by) for i in range(size) if 0 <= i + by < size]
    return lax.ppermute(shard, axis, pairs)


def start_iterate(gram_full, orient):
    diag_sq = jnp.diagonal(gram_full)
    skew_part = orient * gram_full / (diag_sq[:, None] + diag_sq[None, :] + epsilon)
    scale_norm = jnp.sqrt(1.0 + jnp.sum(skew_part * skew_part))
    identity = jnp.eye(gram_full.shape[0], dtype=jnp.float32)
    return (identity + skew_part) / scale_norm


def shards(history, round_index):
    width = history.shape[1] // 2
    pair_count = lax.axis_size("pair")
    position = lax.axis_index("pair")
    cycle_len = 2 * pair_count - 1
    round_now = round_index[0]
    top_id = jnp.where(position == 0, 0, 1 + jnp.mod(position - 1 - round_now, cycle_len))
    bottom_id = 1 + jnp.mod(2 * pair_count - 2 - position - round_now, cycle_len)
    column = jnp.arange(2 * width, dtype=jnp.int32)
    global_id = jnp.where(
        column < width, top_id * width + column, bottom_id * width + column - width
    )
    orient = jnp.sign(global_id[None, :] - global_id[:, None]).astype(jnp.float32)
    partial_value = lax.dot_general(
        history,
        history,
        (((0,), (0,)), ((), ())),
        precision=lax.Precision.HIGHEST,
        preferred_element_type=jnp.float32,
    )
    gram_full = lax.psum(partial_value, "tm")
    factor = start_iterate(gram_full, orient)
    identity = jnp.eye(2 * width, dtype=jnp.float32)
    for step in range(STEPS):
        square = jnp.dot(
            factor.T, factor, precision=lax.Precision.HIGHEST, preferred_element_type=jnp.float32
        )
        factor = jnp.dot(
            factor,
            1.5 * identity - 0.5 * square,
            precision=lax.Precision.HIGHEST,
            preferred_element_type=jnp.float32,
        )
    rotated = jnp.dot(
        history, factor, precision=lax.Precision.HIGHEST, preferred_element_type=jnp.float32
    )
    top_out = rotated[:, :width]
    bottom_out = rotated[:, width:]
    from_right = shifted(bottom_out, "pair", -1)
    outgoing = jnp.where(position == 0, bottom_out, top_out)
    from_left = shifted(outgoing, "pair", 1)
    new_top = jnp.where(position == 0, top_out, from_left)
    new_bottom = jnp.where(position == pair_count - 1, top_out, from_right)
    return jnp.concatenate([new_top, new_bottom], axis=1)


def solution(mesh):
    in_specs = (P("tm", "pair"), P())
    out_specs = P("tm", "pair")
    return jax.shard_map(shards, mesh=mesh, in_specs=in_specs, out_specs=out_specs, check_vma=False)
```

profile of v0, /device:TPU:9, one launch (start us, length us, event | category | flops | bytes accessed | tf_op | source)
XLA Modules:
  0.0 215.3 jit_solution(6972016567903222417)
XLA Ops:
  6.5 11.2 %fusion.1 = f32[512,512]{1,0:T(8,128)} fusion(f32[2048,512]{1,0:T(8,128)} %param.2), kind=kOutput, calls=%fused_computation.22 | convolution fusion | flops 6442450944 | bytes 5242880 | tf_op jit(solution)/shard_map/dot_general | solution.py:39
  17.7 0.0 all-reduce.2.cloned.1.call-update
  18.5 36.2 %all-reduce.2.cloned.1.call-done = f32[512,512]{1,0:T(8,128)} async-done(((f32[512,512]{1,0:T(8,128)}), f32[512,512]{1,0:T(8,128)}) %all-reduce.2.cloned.1.call-update) | async-done | bytes 1048592 | tf_op jit(solution)/shard_map/psum | solution.py:46
  54.7 8.9 %gather_fusion = f32[512]{0:T(512)S(1)} fusion(f32[512,512]{1,0:T(8,128)} %all-reduce.2.cloned.1.call-done, s32[512]{0:T(512)S(1)} %bitcast.23), kind=kCustom, calls=%fused_computation | custom fusion | bytes 8192 | tf_op jit(solution)/shard_map/jit(diagonal)/cond/branch_0_fun/gather | solution.py:19
  63.6 2.5 %multiply_reduce_fusion = f32[]{:T(128)} fusion(f32[512]{0:T(512)S(1)} %gather_fusion, f32[512,512]{1,0:T(8,128)} %all-reduce.2.cloned.1.call-done, s32[512]{0:T(512)S(1)} %add_select_fusion), kind=kLoop, calls=%fused_computation.14 | loop fusion | flops 2359295 | bytes 1052676 | tf_op jit(solution)/shard_map/reduce_sum | solution.py:21
  66.8 4.5 %select_subtract_fusion.3 = f32[512,512]{1,0:T(8,128)S(1)} fusion(f32[]{:T(128)S(6)} %sqrt.3, f32[512,512]{1,0:T(8,128)} %all-reduce.2.cloned.1.call-done, f32[512]{0:T(512)S(1)} %gather_fusion, s32[512]{0:T(512)S(1)} %add_select_fusion), kind=kOutput, calls=%fused_computation.6 | convolution fusion | flops 1614544896 | bytes 2101252 | tf_op jit(solution)/shard_map/dot_general | solution.py:50
  71.4 2.3 %fusion = f32[512,512]{1,0:T(8,128)S(1)} fusion(f32[512,512]{1,0:T(8,128)S(1)} %select_subtract_fusion.3, f32[]{:T(128)S(6)} %sqrt.3, f32[512,512]{1,0:T(8,128)S(1)} %copy-done.2, f32[512]{0:T(512)S(1)} %gather_fusion, s32[512]{0:T(512)S(1)} %add_select_fusion), kind=kOutput, calls=%fused_computation.18 | convolution fusion | flops 1613496320 | bytes 3149828 | tf_op jit(solution)/shard_map/dot_general | solution.py:53
  73.6 1.9 select_subtract_fusion.2
  75.5 1.8 fusion.2
  77.4 1.9 select_subtract_fusion.1
  79.2 0.0 copy-start
  79.2 2.1 fusion.3
  81.3 1.9 select_subtract_fusion
  83.2 1.8 fusion.4
  85.1 13.6 %convolution_bitcast_fusion = f32[2048,512]{0,1:T(8,128)S(1)} fusion(f32[512,512]{1,0:T(8,128)S(1)} %fusion.4, f32[2048,512]{1,0:T(8,128)S(1)} %copy-done), kind=kOutput, calls=%fused_computation.2 | convolution fusion | flops 6442450944 | bytes 9437184 | tf_op jit(solution)/shard_map/dot_general | solution.py:59
  98.6 2.4 %slice_select_fusion.2 = (f32[2048,256]{0,1:T(8,128)}, f32[2048,256]{0,1:T(8,128)}) fusion(f32[2048,512]{0,1:T(8,128)S(1)} %convolution_bitcast_fusion, pred[]{:T(512)S(6)} %eq.23), kind=kLoop, calls=%fused_computation.9 | loop fusion | flops 524288 | bytes 8388609 | tf_op jit(solution)/shard_map/jit(_where)/select_n | solution.py:65
  101.1 0.8 copy-done.1
  101.9 3.1 %collective-permute-start = (f32[2048,256]{0,1:T(8,128)}, f32[2048,256]{0,1:T(8,128)S(1)}, u32[]{:S(2)}, u32[]{:S(2)}) collective-permute-start(f32[2048,256]{0,1:T(8,128)} %get-tuple-element.7), channel_id=1, source_target_pairs={{0,4},{4,8},{8,12},{12,16},{16,20},{20,24},{24,28},{1,5},{5,9},{9,... | collective-permute-start | bytes 6291464 | tf_op jit(solution)/shard_map/ppermute | solution.py:15
  105.0 3.1 %collective-permute-start.1 = (f32[2048,256]{0,1:T(8,128)}, f32[2048,256]{0,1:T(8,128)}, u32[]{:S(2)}, u32[]{:S(2)}) collective-permute-start(f32[2048,256]{0,1:T(8,128)} %get-tuple-element.8), channel_id=1, source_target_pairs={{4,0},{8,4},{12,8},{16,12},{20,16},{24,20},{28,24},{5,1},{9,5},{13... | collective-permute-start | bytes 6291464 | tf_op jit(solution)/shard_map/ppermute | solution.py:15
  108.1 85.9 %collective-permute-done = f32[2048,256]{0,1:T(8,128)S(1)} collective-permute-done((f32[2048,256]{0,1:T(8,128)}, f32[2048,256]{0,1:T(8,128)S(1)}, u32[]{:S(2)}, u32[]{:S(2)}) %collective-permute-start) | collective-permute-done | bytes 2097184 | tf_op jit(solution)/shard_map/ppermute | solution.py:15
  194.0 3.5 %collective-permute-done.1 = f32[2048,256]{0,1:T(8,128)} collective-permute-done((f32[2048,256]{0,1:T(8,128)}, f32[2048,256]{0,1:T(8,128)}, u32[]{:S(2)}, u32[]{:S(2)}) %collective-permute-start.1) | collective-permute-done | bytes 2097184 | tf_op jit(solution)/shard_map/ppermute | solution.py:15
  197.5 2.8 %slice_select_fusion.1 = (f32[2048,256]{0,1:T(8,128)S(1)}, f32[2048,256]{0,1:T(8,128)S(1)}) fusion(f32[2048,256]{0,1:T(8,128)S(1)} %collective-permute-done, f32[2048,512]{0,1:T(8,128)} %copy-done.1, pred[]{:T(512)S(6)} %eq.23, f32[2048,256]{0,1:T(8,128)} %collective-permute-done.1, pred[]{:T(512)S(6)} %eq.25), kind=kLoop, calls=%fused_computation.8 | loop fusion | flops 1048576 | bytes 10485762 | tf_op jit(solution)/shard_map/jit(_where)/select_n | solution.py:67
  200.3 2.4 %pad_maximum_fusion = f32[2048,512]{0,1:T(8,128)} fusion(f32[2048,256]{0,1:T(8,128)S(1)} %get-tuple-element.6, f32[2048,256]{0,1:T(8,128)S(1)} %get-tuple-element.5), kind=kLoop, calls=%fused_computation.1 | loop fusion | flops 1048576 | bytes 8388608 | tf_op jit(solution)/shard_map/concatenate | solution.py:69
  202.7 5.3 %copy.4 = f32[2048,512]{1,0:T(8,128)} copy(f32[2048,512]{0,1:T(8,128)} %pad_maximum_fusion) | data formatting | bytes 8388608 | tf_op jit(solution)/shard_map/concatenate | solution.py:69
  (7 shorter events, 0.0 us)
Async XLA Ops:
  6.5 48.2 %all-reduce.2.cloned.1.call-start = ((), (), s32[]{:S(2)}) async-start(), calls=%async_computation | async-start | bytes 2097152 | tf_op jit(solution)/shard_map/psum | solution.py:46
  66.8 4.6 %copy-start.2 = (f32[512,512]{1,0:T(8,128)S(1)}, f32[512,512]{1,0:T(8,128)}, u32[]{:S(2)}) copy-start(f32[512,512]{1,0:T(8,128)} %all-reduce.2.cloned.1.call-done) | copy-start | bytes 3145732
  79.2 5.8 %copy-start = (f32[2048,512]{1,0:T(8,128)S(1)}, f32[2048,512]{1,0:T(8,128)}, u32[]{:S(2)}) copy-start(f32[2048,512]{1,0:T(8,128)} %param.2) | copy-start | bytes 12582916
  98.6 3.3 %copy-start.1 = (f32[2048,512]{0,1:T(8,128)}, f32[2048,512]{0,1:T(8,128)S(1)}, u32[]{:S(2)}) copy-start(f32[2048,512]{0,1:T(8,128)S(1)} %convolution_bitcast_fusion) | copy-start | bytes 12582916
  101.9 92.1 %collective-permute-start = (f32[2048,256]{0,1:T(8,128)}, f32[2048,256]{0,1:T(8,128)S(1)}, u32[]{:S(2)}, u32[]{:S(2)}) collective-permute-start(f32[2048,256]{0,1:T(8,128)} %get-tuple-element.7), channel_id=1, source_target_pairs={{0,4},{4,8},{8,12},{12,16},{16,20},{20,24},{24,28},{1,5},{5,9},{9,... | collective-permute-start | bytes 6291464 | tf_op jit(solution)/shard_map/ppermute | solution.py:15
  105.0 92.5 %collective-permute-start.1 = (f32[2048,256]{0,1:T(8,128)}, f32[2048,256]{0,1:T(8,128)}, u32[]{:S(2)}, u32[]{:S(2)}) collective-permute-start(f32[2048,256]{0,1:T(8,128)} %get-tuple-element.8), channel_id=1, source_target_pairs={{4,0},{8,4},{12,8},{16,12},{20,16},{24,20},{28,24},{5,1},{9,5},{13... | collective-permute-start | bytes 6291464 | tf_op jit(solution)/shard_map/ppermute | solution.py:15
Sparse Core Ops, SparseCore 0:
  17.9 36.7 all-reduce.1
where the time goes:
time: 220 us; the launch traced here: 215 us
  waiting for transfers between devices  126 us (57%)
  matrix products  42.9 us (20%)
  between operations  15.4 us (7%)
  local copies, waits for them, and re-layouts  15.1 us (7%)
  other arithmetic  10.2 us (5%)
  starting transfers between devices  6.17 us (3%)
    ppermute x2, waiting for transfers between devices, shifted(): return lax.ppermute(shard, axis, pairs)  89.4 us
    psum x1, waiting for transfers between devices, shards(): gram_full = lax.psum(partial_value, 'tm')  36.2 us
    dot_general x1, matrix products, shards(): jnp.dot(history, factor, precision=lax.Precision.HIGHEST, preferred_eleme...  13.6 us
    dot_general x1, matrix products, shards(): lax.dot_general(history, history, (((0,), (0,)), ((), ())), precision=lax...  11.2 us
    dot_general x4, matrix products, shards(): jnp.dot(factor.T, factor, precision=lax.Precision.HIGHEST, preferred_elem...  10.1 us
    gather x1, local copies, waits for them, and re-layouts, start_iterate(): diag_sq = jnp.diagonal(gram_full)  8.89 us
    dot_general x4, matrix products, shards(): jnp.dot(factor, 1.5 * identity - 0.5 * square, precision=lax.Precision.HI...  8.04 us
    ppermute x2, starting transfers between devices, shifted(): return lax.ppermute(shard, axis, pairs)  6.17 us
  transfers between devices with their start and end apart: 3, of which 3 were waited for; matrix products, arithmetic and copies ran while one was open for 0% of the time, Pallas kernels for 0%

commit v1 on v0

v1 whole, which is shorter than its diff:
```python
import jax
import jax.numpy as jnp
from jax import lax
from jax.experimental import pallas as pl
from jax.experimental.pallas import tpu as pltpu
from jax.sharding import PartitionSpec as P

STEPS = 4
TILE = 128
F32, BF16 = jnp.float32, jnp.bfloat16

epsilon = 1e-06

PLAN = ((4, 0), (4, 0), (8, 4))

VMEM_BYTES = 48 << 20
IN_VMEM = pl.BlockSpec(memory_space=pltpu.VMEM)
IN_SMEM = pl.BlockSpec(memory_space=pltpu.SMEM)
ANYWHERE = pl.BlockSpec(memory_space=pl.ANY)


def split(x):
    high = x.astype(BF16)
    return high, (x - high.astype(F32)).astype(BF16)


def product(a, b):
    return jnp.dot(a, b, preferred_element_type=F32)


def inner(a, b):
    return lax.dot_general(a, b, (((0,), (0,)), ((), ())), preferred_element_type=F32)


def params(**more):
    return pltpu.CompilerParams(vmem_limit_bytes=VMEM_BYTES, **more)


def upper_tiles(width):
    n = width // TILE
    at = [slice(i * TILE, (i + 1) * TILE) for i in range(n)]
    return list(enumerate((at[i], at[j]) for i in range(n) for j in range(i, n)))


def gram_kernel(core_ref, b_ref, out_ref, high_ref, cross_ref):
    high, low = split(b_ref[...])
    high_ref[...] = inner(high, high)
    cross_ref[...] = inner(high, low)
    core = core_ref[0]
    tiles = upper_tiles(b_ref.shape[1])
    half = len(tiles) // 2
    for k, (i, j) in tiles:
        at = slice(k % half * TILE, (k % half + 1) * TILE)
        out_ref[core ^ (k // half), at, :] = high_ref[i, j] + cross_ref[i, j] + cross_ref[j, i].T


def gram(core, b):
    rows, width = b.shape
    packed = len(upper_tiles(width)) // 2 * TILE
    return pl.pallas_call(
        gram_kernel,
        in_specs=[IN_SMEM, IN_VMEM],
        out_specs=IN_VMEM,
        out_shape=jax.ShapeDtypeStruct((2, packed, TILE), F32),
        scratch_shapes=[pltpu.VMEM((width, width), F32)] * 2,
        compiler_params=params(),
        cost_estimate=pl.CostEstimate(flops=0, bytes_accessed=0, transcendentals=0),
        name="gram",
    )(core, b)


def polar_kernel(at_ref, mine_ref, other_ref, _, high_ref, low_ref, x_ref, one_ref, two_ref):
    width = x_ref.shape[0]
    half = width // 2
    core, top_id, bottom_id, swapped = (at_ref[i] for i in range(4))
    tiles = upper_tiles(width)
    for k, (i, j) in tiles:
        per = len(tiles) // 2
        at = slice(k % per * TILE, (k % per + 1) * TILE)
        tile = jnp.where(core == k // per, mine_ref[at], other_ref[at])
        one_ref[i, j] = tile
        if i != j:
            one_ref[j, i] = tile.T
    row = lax.broadcasted_iota(jnp.int32, (width, width), 0)
    column = lax.broadcasted_iota(jnp.int32, (width, width), 1)
    on_diagonal = row == column

    def global_id(c):
        return jnp.where(c < half, top_id * half + c, bottom_id * half + c - half)

    row_id = global_id(lax.broadcasted_iota(jnp.int32, (width, 1), 0))
    column_id = global_id(lax.broadcasted_iota(jnp.int32, (1, width), 1))
    gram_full = one_ref[...]
    diagonal = jnp.where(on_diagonal, gram_full, 0.0)
    across = jnp.sum(diagonal, axis=0, keepdims=True)
    down = jnp.sum(diagonal, axis=1, keepdims=True)
    skew = gram_full / (down + across + epsilon)
    skew = jnp.where(column_id > row_id, skew, jnp.where(column_id < row_id, -skew, 0.0))
    norm = jnp.sqrt(1.0 + jnp.sum(skew * skew))
    x_ref[...] = (jnp.where(on_diagonal, 1.0, 0.0) + skew) / norm
    for _ in range(STEPS):
        high, low = split(x_ref[...])
        one_ref[...] = inner(high, high)
        two_ref[...] = inner(high, low)
        square = one_ref[...] + two_ref[...] + two_ref[...].T
        turn_high, turn_low = split(jnp.where(on_diagonal, 1.5, 0.0) - 0.5 * square)
        x_ref[...] = product(high, turn_high)
        one_ref[...] = product(high, turn_low)
        two_ref[...] = product(low, turn_high)
        x_ref[...] = x_ref[...] + (one_ref[...] + two_ref[...])
    for flag, (first, second) in enumerate((((0, half), (half, width)), ((half, width), (0, half)))):

        @pl.when(swapped == flag)
        def _():
            for to, (begin, end) in ((0, first), (half, second)):
                high, low = split(x_ref[:, begin:end])
                high_ref[:, to : to + half] = high
                low_ref[:, to : to + half] = low


def polar(at, mine, other, after, width):
    return pl.pallas_call(
        polar_kernel,
        in_specs=[IN_SMEM, IN_VMEM, IN_VMEM, ANYWHERE],
        out_specs=[IN_VMEM, IN_VMEM],
        out_shape=[jax.ShapeDtypeStruct((width, width), BF16)] * 2,
        scratch_shapes=[pltpu.VMEM((width, width), F32)] * 3,
        compiler_params=params(),
        cost_estimate=pl.CostEstimate(flops=0, bytes_accessed=0, transcendentals=0),
        name="polar",
    )(at, mine, other, after)


def turn_kernel(start, b_ref, high_ref, low_ref, first_ref, second_ref, rows_ref, sem):
    load = pltpu.make_async_copy(b_ref.at[pl.ds(start, rows_ref.shape[0])], rows_ref, sem)
    load.start()
    load.wait()
    high, low = split(rows_ref[...])
    half = first_ref.shape[1]
    for out_ref, at in ((first_ref, slice(0, half)), (second_ref, slice(half, 2 * half))):
        w_high, w_low = high_ref[:, at], low_ref[:, at]
        out_ref[...] = product(high, w_high) + product(high, w_low) + product(low, w_high)


def turn(b, start, count, w):
    width = b.shape[1]

    def kernel(*refs):
        turn_kernel(start, *refs)

    return pl.pallas_call(
        kernel,
        in_specs=[ANYWHERE, IN_VMEM, IN_VMEM],
        out_specs=[IN_VMEM, IN_VMEM],
        out_shape=[jax.ShapeDtypeStruct((count, width // 2), F32)] * 2,
        scratch_shapes=[pltpu.VMEM((count, width), F32), pltpu.SemaphoreType.DMA],
        compiler_params=params(),
        cost_estimate=pl.CostEstimate(flops=0, bytes_accessed=0, transcendentals=0),
        name="turn",
    )(b, *w)


def take(b, start, count, after):
    width = b.shape[1]

    def kernel(b_ref, _, out_ref, sem):
        copy = pltpu.make_async_copy(b_ref.at[pl.ds(start, count)], out_ref, sem)
        copy.start()
        copy.wait()

    return pl.pallas_call(
        kernel,
        in_specs=[ANYWHERE, ANYWHERE],
        out_specs=IN_VMEM,
        out_shape=jax.ShapeDtypeStruct((count, width), F32),
        scratch_shapes=[pltpu.SemaphoreType.DMA],
        compiler_params=params(),
        cost_estimate=pl.CostEstimate(flops=0, bytes_accessed=0, transcendentals=0),
        name="take",
    )(b, after)


def own_kernel(start, end_ref, b_ref, high_ref, low_ref, out_ref, rows_ref, sem):
    half = out_ref.shape[1]
    for which, at in ((1, slice(half, 2 * half)), (2, slice(0, half))):

        @pl.when(end_ref[0] == which)
        def _():
            load = pltpu.make_async_copy(b_ref.at[pl.ds(start, rows_ref.shape[0])], rows_ref, sem)
            load.start()
            load.wait()
            high, low = split(rows_ref[...])
            w_high, w_low = high_ref[:, at], low_ref[:, at]
            out_ref[...] = product(high, w_high) + product(high, w_low) + product(low, w_high)


def own(end, b, start, count, w):
    width = b.shape[1]

    def kernel(*refs):
        own_kernel(start, *refs)

    return pl.pallas_call(
        kernel,
        in_specs=[IN_SMEM, ANYWHERE, IN_VMEM, IN_VMEM],
        out_specs=IN_VMEM,
        out_shape=jax.ShapeDtypeStruct((count, width // 2), F32),
        scratch_shapes=[pltpu.VMEM((count, width), F32), pltpu.SemaphoreType.DMA],
        compiler_params=params(),
        cost_estimate=pl.CostEstimate(flops=0, bytes_accessed=0, transcendentals=0),
        name="own",
    )(end, b, *w)


def join_kernel(places, choice_ref, *refs):
    out_ref, held_ref, load_sem, store_sem = refs[-4:]
    half = out_ref.shape[1] // 2
    loads, stores = [], []
    taken = 0
    for k, (start, count, sources) in enumerate(places):
        for side in (0, 1):
            n = sources[side]
            for s in range(n):
                into = held_ref.at[pl.ds(start, count), pl.ds(side * half, half)]
                copy = pltpu.make_async_copy(refs[taken + s], into, load_sem.at[2 * k + side])

                @pl.when(choice_ref[2 * k + side] == s)
                def _():
                    copy.start()

            loads.append(copy)
            taken += n
    for k, (start, count, _) in enumerate(places):
        loads[2 * k].wait()
        loads[2 * k + 1].wait()
        at = pl.ds(start, count)
        stores.append(pltpu.make_async_copy(held_ref.at[at], out_ref.at[at], store_sem.at[k]))
        stores[-1].start()
    for copy in stores:
        copy.wait()


def join(choice, chunks, rows, width):
    places = [(start, count, (len(left), len(right))) for start, count, left, right in chunks]
    arrays = [a for _, _, left, right in chunks for a in (*left, *right)]

    def kernel(*refs):
        join_kernel(places, *refs)

    return pl.pallas_call(
        kernel,
        in_specs=[IN_SMEM] + [ANYWHERE] * len(arrays),
        out_specs=ANYWHERE,
        out_shape=jax.ShapeDtypeStruct((rows, width), F32),
        scratch_shapes=[
            pltpu.VMEM((rows, width), F32),
            pltpu.SemaphoreType.DMA((2 * len(chunks),)),
            pltpu.SemaphoreType.DMA((len(chunks),)),
        ],
        compiler_params=params(),
        cost_estimate=pl.CostEstimate(flops=0, bytes_accessed=0, transcendentals=0),
        name="join",
    )(choice, *arrays)


def shards(history, round_index):
    rows, width = history.shape
    pairs = lax.axis_size("pair")
    levels = pairs // 2
    position = lax.axis_index("pair")
    partner = position ^ 1
    even = position % 2 == 0
    first, last = position == 0, position == pairs - 1
    core, row_half = lax.axis_index("tm") % 2, lax.axis_index("tm") // 2
    cycle_len = 2 * pairs - 1
    round_now = round_index[0]
    swap_pairs = [(p, p ^ 1) for p in range(pairs)]
    swap_cores = [(i, i ^ 1) for i in range(4)]
    swap_rows = [(i, i ^ 2) for i in range(4)]

    def ids(p):
        top_id = jnp.where(p == 0, 0, 1 + jnp.mod(p - 1 - round_now, cycle_len))
        bottom_id = 1 + jnp.mod(2 * pairs - 2 - p - round_now, cycle_len)
        return top_id, bottom_id

    def is_early(p, threshold):
        level = p // 2
        return (p % 2 == 0) & (level >= threshold) | (p % 2 == 1) & (level <= levels - 1 - threshold)

    chunks = []
    begin = 0
    for sixteenths, quarter in PLAN:
        count = rows * sixteenths // 16
        chunks.append((begin, count, quarter * levels // 4))
        begin += count

    def swap_early(k, after):
        begin, count, threshold = chunks[k]
        sent = [(p, p ^ 1) for p in range(pairs) if is_early(p, threshold)]
        return lax.ppermute(take(history, begin, count, after), "pair", sent)

    early = [k for k, chunk in enumerate(chunks) if chunk[2] < levels]
    from_partner = {0: swap_early(0, round_index)}

    packed = gram(jnp.stack([core]), history)
    summed = packed[0] + lax.ppermute(packed[1], "tm", swap_cores)
    mine = summed + lax.ppermute(summed, "tm", swap_rows)
    other = lax.ppermute(mine, "tm", swap_cores)

    piece = mine.shape[0] // 2
    part = lax.ppermute(lax.dynamic_slice_in_dim(mine, row_half * piece, piece), "pair", swap_pairs)
    for k in early[1:]:
        from_partner[k] = swap_early(k, other)
    part_2 = lax.ppermute(part, "tm", swap_rows)
    mine_q = jnp.where(row_half == 0, jnp.concatenate([part, part_2]), jnp.concatenate([part_2, part]))
    other_q = lax.ppermute(mine_q, "tm", swap_cores)

    flag = first.astype(jnp.int32)
    w = polar(jnp.stack([core, *ids(position), flag]), mine, other, from_partner[0], width)

    late = {}
    for k, (begin, count, threshold) in enumerate(chunks):
        if threshold > 0:
            right, left = turn(history, begin, count, w)
            to_right = [(p, p + 1) for p in range(pairs - 1) if not is_early(p, threshold)]
            to_left = [(p, p - 1) for p in range(1, pairs) if not is_early(p, threshold)]
            late[k] = (right, left, lax.ppermute(right, "pair", to_right), lax.ppermute(left, "pair", to_left))

    flag_q = (even | (partner == 0)).astype(jnp.int32)
    w_q = polar(jnp.stack([core, *ids(partner), flag_q]), mine_q, other_q, from_partner[early[-1]], width)
    end = jnp.stack([first + 2 * last]).astype(jnp.int32)

    joined, choice = [], []
    for k, (begin, count, threshold) in enumerate(chunks):
        left_from, right_from = [], []
        top_choice, bottom_choice = 0, 0
        if threshold < levels:
            near, far = turn(from_partner[k], 0, count, w_q)
            onward = [(p ^ 1, p - 1) for p in range(2, pairs, 2) if is_early(p, threshold)]
            onward += [(p ^ 1, p + 1) for p in range(1, pairs - 1, 2) if is_early(p, threshold)]
            passed = lax.ppermute(far, "pair", onward)
            left_from += [near, passed]
            right_from += [near, passed]
            top_choice = jnp.where(even, 1, 0)
            bottom_choice = jnp.where(even, 0, 1)
            if threshold == 0:
                alone = own(end, history, begin, count, w)
                left_from.append(alone)
                right_from.append(alone)
                top_choice = jnp.where(first, 2, top_choice)
                bottom_choice = jnp.where(last, 2, bottom_choice)
        if threshold > 0:
            n = len(left_from)
            right, left, from_left, from_right = late[k]
            left_from += [from_left, left]
            right_from += [from_right, right]
            top_choice = jnp.where(is_early(position - 1, threshold) & ~first, top_choice, n)
            bottom_choice = jnp.where(is_early(position + 1, threshold) & ~last, bottom_choice, n)
            top_choice = jnp.where(first, n + 1, top_choice)
            bottom_choice = jnp.where(last, n + 1, bottom_choice)
        joined.append((begin, count, left_from, right_from))
        choice += [top_choice, bottom_choice]
    return join(jnp.stack(choice).astype(jnp.int32), joined, rows, width)


def solution(mesh):
    in_specs = (P("tm", "pair"), P())
    out_specs = P("tm", "pair")
    return jax.shard_map(shards, mesh=mesh, in_specs=in_specs, out_specs=out_specs, check_vma=False)
```

time: 220 us -> 129 us (0.59); the launches traced: 215 us -> 129 us
  waiting for transfers between devices: 126 us -> 63.6 us
  matrix products: 42.9 us -> 0 us
  Pallas kernels: 0 us -> 33.5 us
  starting transfers between devices: 6.17 us -> 21.5 us
  between operations: 15.4 us -> 1.02 us
  other arithmetic: 10.2 us -> 1.41 us
  local copies, waits for them, and re-layouts: 15.1 us -> 7.63 us
    dot_general x10 -> x0, matrix products: 42.9 us -> none  [the longest x1 13.6 us: shards(): jnp.dot(history, factor, precision=lax.Precision.HIGHEST, preferred_eleme...]
    psum x1 -> x0, waiting for transfers between devices: 36.2 us -> none  [shards(): gram_full = lax.psum(partial_value, 'tm')]
    pallas_call x0 -> x11, Pallas kernels: none -> 33.5 us  [the longest x2 16.8 us: polar(): pl.pallas_call(polar_kernel, in_specs=[IN_SMEM, IN_VMEM, IN_VMEM, ANYWHER...]
    ppermute x2 -> x12, waiting for transfers between devices: 89.4 us -> 63.6 us  [the longest x1 36.8 us: shards(): lax.ppermute(lax.dynamic_slice_in_dim(mine, row_half * piece, piece), 'pa...]
    ppermute x2 -> x12, starting transfers between devices: 6.17 us -> 21.5 us  [the longest x2 6.4 us: shards(): passed = lax.ppermute(far, 'pair', onward)]
    gather x1 -> x0, local copies, waits for them, and re-layouts: 8.89 us -> none  [start_iterate(): diag_sq = jnp.diagonal(gram_full)]
    unnamed x6 -> x12, local copies, waits for them, and re-layouts: 0.84 us -> 6.86 us
    concatenate x1 -> x0, local copies, waits for them, and re-layouts: 5.34 us -> none  [shards(): return jnp.concatenate([new_top, new_bottom], axis=1)]
  transfers between devices with their start and end apart: 3 -> 12, of which waited for: 3 -> 7; matrix products, arithmetic and copies ran while one was open for 0% -> 2% of each run, Pallas kernels for 0% -> 21%
where the time goes in v1:
time: 129 us
  waiting for transfers between devices  63.6 us (49%)
  Pallas kernels  33.5 us (26%)
  starting transfers between devices  21.5 us (17%)
  local copies, waits for them, and re-layouts  7.63 us (6%)
  other arithmetic  1.41 us (1%)
    ppermute x1, waiting for transfers between devices, shards(): lax.ppermute(lax.dynamic_slice_in_dim(mine, row_half * piece, piece), 'pa...  36.8 us
    pallas_call x2, Pallas kernels, polar(): pl.pallas_call(polar_kernel, in_specs=[IN_SMEM, IN_VMEM, IN_VMEM, ANYWHER...  16.8 us
    ppermute x1, waiting for transfers between devices, shards(): lax.ppermute(right, 'pair', to_right)  13.2 us
    pallas_call x3, Pallas kernels, turn(): pl.pallas_call(kernel, in_specs=[ANYWHERE, IN_VMEM, IN_VMEM], out_specs=[...  8.43 us
    unnamed x12, local copies, waits for them, and re-layouts  6.86 us
    ppermute x2, starting transfers between devices, shards(): passed = lax.ppermute(far, 'pair', onward)  6.4 us
    ppermute x1, waiting for transfers between devices, shards(): mine = summed + lax.ppermute(summed, 'tm', swap_rows)  5.66 us
    pallas_call x1, Pallas kernels, join(): pl.pallas_call(kernel, in_specs=[IN_SMEM] + [ANYWHERE] * len(arrays), out...  4.58 us
  transfers between devices with their start and end apart: 12, of which 7 were waited for; matrix products, arithmetic and copies ran while one was open for 2% of the time, Pallas kernels for 21%

profile of v1, /device:TPU:9, one launch (start us, length us, event | category | flops | bytes accessed | tf_op | source)
XLA Modules:
  0.0 128.6 jit_solution(18330840538675196681)
XLA Ops:
  0.0 2.2 %copy-done = f32[2048,512]{1,0:T(8,128)S(1)} copy-done((f32[2048,512]{1,0:T(8,128)S(1)}, f32[2048,512]{1,0:T(8,128)}, u32[]{:S(2)}) %copy-start) | copy-done | bytes 4194328
  2.2 2.5 %gram.1 = f32[2,640,128]{2,1,0:T(8,128)S(1)} custom-call(s32[1]{0:T(128)} %bitcast.4.core_ref, f32[2048,512]{1,0:T(8,128)S(1)} %copy-done), custom_call_target="tpu_custom_call" | custom-call | tf_op jit(solution)/shard_map/gram/pallas_call | solution.py:60
  5.5 1.3 collective-permute-done.1
  6.8 1.3 %collective-permute-start.2 = (f32[640,128]{1,0:T(8,128)S(1)}, f32[640,128]{1,0:T(8,128)S(1)}, u32[]{:S(2)}, u32[]{:S(2)}) collective-permute-start(f32[640,128]{1,0:T(8,128)S(1)} %fusion), channel_id=1, source_target_pairs={{0,2},{1,3},{2,0},{3,1},{4,6},{5,7},{6,4},{7,5},{8,10},{9,11},{10,... | collective-permute-start | bytes 983048 | tf_op jit(solution)/shard_map/ppermute | solution.py:307
  8.8 1.3 collective-permute-start
  10.1 5.7 %collective-permute-done.2 = f32[640,128]{1,0:T(8,128)S(1)} collective-permute-done((f32[640,128]{1,0:T(8,128)S(1)}, f32[640,128]{1,0:T(8,128)S(1)}, u32[]{:S(2)}, u32[]{:S(2)}) %collective-permute-start.2) | collective-permute-done | bytes 327712 | tf_op jit(solution)/shard_map/ppermute | solution.py:307
  15.8 1.3 collective-permute-start.6
  17.1 1.3 collective-permute-done.6._.other_ref
  22.3 36.8 %collective-permute-done.3 = f32[320,128]{1,0:T(8,128)} collective-permute-done((f32[320,128]{1,0:T(8,128)}, f32[320,128]{1,0:T(8,128)}, u32[]{:S(2)}, u32[]{:S(2)}) %collective-permute-start.3) | collective-permute-done | bytes 163872 | tf_op jit(solution)/shard_map/ppermute | solution.py:311
  60.3 8.2 %polar.3 = (bf16[512,512]{1,0:T(8,128)(2,1)S(1)}, bf16[512,512]{1,0:T(8,128)(2,1)S(1)}) custom-call(s32[4]{0:T(128)S(1)} %pad_add_fusion.1.at_ref, f32[640,128]{1,0:T(8,128)S(1)} %add.60.mine_ref, f32[640,128]{1,0:T(8,128)S(1)} %copy-done.5, f32[512,512]{1,0:T(8,128)S(1)} %collective-permute-done.refs_0_._), custom_call_target="tpu_custom_call" | custom-call | tf_op jit(solution)/shard_map/polar/pallas_call | solution.py:122
  68.5 4.7 %turn.5 = (f32[1024,256]{1,0:T(8,128)}, f32[1024,256]{1,0:T(8,128)}) custom-call(f32[2048,512]{1,0:T(8,128)} %refs_0_.1, bf16[512,512]{1,0:T(8,128)(2,1)S(1)} %get-tuple-element.19.refs_2_.refs_1_, bf16[512,512]{1,0:T(8,128)(2,1)S(1)} %get-tuple-element.20.refs_3_.refs_2_), custom_call_target="tpu_custom_call" | custom-call | tf_op jit(solution)/shard_map/turn/pallas_call | solution.py:151
  73.2 3.1 %collective-permute-start.10 = (f32[1024,256]{1,0:T(8,128)}, f32[1024,256]{1,0:T(8,128)}, u32[]{:S(2)}, u32[]{:S(2)}) collective-permute-start(f32[1024,256]{1,0:T(8,128)} %get-tuple-element.23.refs_16_), channel_id=1, source_target_pairs={{0,4},{4,8},{8,12},{12,16},{16,20},{20,24},{24,28},{1,5},{5,9},{9,... | collective-permute-start | bytes 3145736 | tf_op jit(solution)/shard_map/ppermute | solution.py:327
  76.4 3.2 %collective-permute-start.11 = (f32[1024,256]{1,0:T(8,128)}, f32[1024,256]{1,0:T(8,128)}, u32[]{:S(2)}, u32[]{:S(2)}) collective-permute-start(f32[1024,256]{1,0:T(8,128)} %get-tuple-element.24.refs_14_), channel_id=1, source_target_pairs={{4,0},{8,4},{12,8},{16,12},{20,16},{24,20},{28,24},{5,1},{9,5},{13... | collective-permute-start | bytes 3145736 | tf_op jit(solution)/shard_map/ppermute | solution.py:327
  80.8 2.4 %collective-permute-start.5 = (f32[640,128]{1,0:T(8,128)S(1)}, f32[640,128]{1,0:T(8,128)}, u32[]{:S(2)}, u32[]{:S(2)}) collective-permute-start(f32[640,128]{1,0:T(8,128)S(1)} %maximum_select_fusion.mine_ref), channel_id=1, source_target_pairs={{0,1},{1,0},{2,3},{3,2},{4,5},{5,4},{6,7},{7,6},{8,9},{9,8},{10,11... | collective-permute-start | bytes 983048 | tf_op jit(solution)/shard_map/ppermute | solution.py:316
  83.3 1.3 %collective-permute-done.5.other_ref = f32[640,128]{1,0:T(8,128)} collective-permute-done((f32[640,128]{1,0:T(8,128)S(1)}, f32[640,128]{1,0:T(8,128)}, u32[]{:S(2)}, u32[]{:S(2)}) %collective-permute-start.5) | collective-permute-done | bytes 327712 | tf_op jit(solution)/shard_map/ppermute | solution.py:316
  84.6 8.6 %polar.2 = (bf16[512,512]{1,0:T(8,128)(2,1)S(1)}, bf16[512,512]{1,0:T(8,128)(2,1)S(1)}) custom-call(s32[4]{0:T(128)S(1)} %pad_add_fusion.at_ref, f32[640,128]{1,0:T(8,128)S(1)} %maximum_select_fusion.mine_ref, f32[640,128]{1,0:T(8,128)} %collective-permute-done.5.other_ref, f32[512,512]{1,0:T(8,128)S(1)} %collective-permute-done.7._.refs_0_), custom_call_target="tpu_custom_call" | custom-call | tf_op jit(solution)/shard_map/polar/pallas_call | solution.py:122
  93.3 1.9 %turn.4 = (f32[512,256]{1,0:T(8,128)S(1)}, f32[512,256]{1,0:T(8,128)}) custom-call(f32[512,512]{1,0:T(8,128)S(1)} %collective-permute-done.7._.refs_0_, bf16[512,512]{1,0:T(8,128)(2,1)S(1)} %get-tuple-element.15.refs_1_, bf16[512,512]{1,0:T(8,128)(2,1)S(1)} %get-tuple-element.16.refs_2_), custom_call_target="tpu_custom_call" | custom-call | tf_op jit(solution)/shard_map/turn/pallas_call | solution.py:151
  95.9 3.2 %collective-permute-start.9 = (f32[512,256]{1,0:T(8,128)}, f32[512,256]{1,0:T(8,128)S(1)}, u32[]{:S(2)}, u32[]{:S(2)}) collective-permute-start(f32[512,256]{1,0:T(8,128)} %get-tuple-element.22), channel_id=1, source_target_pairs={{12,4},{20,12},{28,20},{0,8},{8,16},{16,24},{13,5},{21,13},{29,21}... | collective-permute-start | bytes 1572872 | tf_op jit(solution)/shard_map/ppermute | solution.py:341
  99.1 1.9 %turn.3 = (f32[512,256]{1,0:T(8,128)S(1)}, f32[512,256]{1,0:T(8,128)}) custom-call(f32[512,512]{1,0:T(8,128)S(1)} %collective-permute-done.refs_0_._, bf16[512,512]{1,0:T(8,128)(2,1)S(1)} %get-tuple-element.15.refs_1_, bf16[512,512]{1,0:T(8,128)(2,1)S(1)} %get-tuple-element.16.refs_2_), custom_call_target="tpu_custom_call" | custom-call | tf_op jit(solution)/shard_map/turn/pallas_call | solution.py:151
  101.0 3.2 %collective-permute-start.8 = (f32[512,256]{1,0:T(8,128)}, f32[512,256]{1,0:T(8,128)S(1)}, u32[]{:S(2)}, u32[]{:S(2)}) collective-permute-start(f32[512,256]{1,0:T(8,128)} %get-tuple-element.18), channel_id=1, source_target_pairs={{12,4},{20,12},{28,20},{0,8},{8,16},{16,24},{13,5},{21,13},{29,21}... | collective-permute-start | bytes 1572872 | tf_op jit(solution)/shard_map/ppermute | solution.py:341
  104.3 2.2 %copy-done.1 = f32[2048,512]{1,0:T(8,128)S(1)} copy-done((f32[2048,512]{1,0:T(8,128)S(1)}, f32[2048,512]{1,0:T(8,128)}, u32[]{:S(2)}) %copy-start.1) | copy-done | bytes 4194328
  106.6 13.2 %collective-permute-done.10.refs_13_ = f32[1024,256]{1,0:T(8,128)} collective-permute-done((f32[1024,256]{1,0:T(8,128)}, f32[1024,256]{1,0:T(8,128)}, u32[]{:S(2)}, u32[]{:S(2)}) %collective-permute-start.10) | collective-permute-done | bytes 1048608 | tf_op jit(solution)/shard_map/ppermute | solution.py:327
  119.8 4.1 %collective-permute-done.11.refs_15_ = f32[1024,256]{1,0:T(8,128)} collective-permute-done((f32[1024,256]{1,0:T(8,128)}, f32[1024,256]{1,0:T(8,128)}, u32[]{:S(2)}, u32[]{:S(2)}) %collective-permute-start.11) | collective-permute-done | bytes 1048608 | tf_op jit(solution)/shard_map/ppermute | solution.py:327
  123.9 4.6 %join.1 = f32[2048,512]{1,0:T(8,128)} custom-call(s32[6]{0:T(128)S(1)} %stack.56.refs_0_, f32[512,256]{1,0:T(8,128)S(1)} %get-tuple-element.17.refs_1_.refs_4_, f32[512,256]{1,0:T(8,128)S(1)} %collective-permute-done.8.refs_2_.refs_5_, f32[512,256]{1,0:T(8,128)S(1)} %own.2.refs_3_.refs_6_, f32[512,256]{1,0:T(8,128)S(1)} %get-tuple-element.17.refs_1_.refs_4_, ...), custom_call_target="tpu_custom_call" | custom-call | tf_op jit(solution)/shard_map/join/pallas_call | solution.py:250
  (31 shorter events, 8.3 us)
Async XLA Ops:
  0.0 2.2 %copy-start = (f32[2048,512]{1,0:T(8,128)S(1)}, f32[2048,512]{1,0:T(8,128)}, u32[]{:S(2)}) copy-start(f32[2048,512]{1,0:T(8,128)} %refs_0_.1) | copy-start | bytes 12582916
  4.8 2.0 %collective-permute-start.1 = (f32[640,128]{1,0:T(8,128)S(1)}, f32[640,128]{1,0:T(8,128)S(1)}, u32[]{:S(2)}, u32[]{:S(2)}) collective-permute-start(f32[640,128]{1,0:T(8,128)S(1)} %slice_bitcast_fusion), channel_id=1, source_target_pairs={{0,1},{1,0},{2,3},{3,2},{4,5},{5,4},{6,7},{7,6},{8,9},{9,8},{10,11... | collective-permute-start | bytes 983048 | tf_op jit(solution)/shard_map/ppermute | solution.py:306
  6.8 9.0 %collective-permute-start.2 = (f32[640,128]{1,0:T(8,128)S(1)}, f32[640,128]{1,0:T(8,128)S(1)}, u32[]{:S(2)}, u32[]{:S(2)}) collective-permute-start(f32[640,128]{1,0:T(8,128)S(1)} %fusion), channel_id=1, source_target_pairs={{0,2},{1,3},{2,0},{3,1},{4,6},{5,7},{6,4},{7,5},{8,10},{9,11},{10,... | collective-permute-start | bytes 983048 | tf_op jit(solution)/shard_map/ppermute | solution.py:307
  8.8 50.5 %collective-permute-start = (f32[512,512]{1,0:T(8,128)S(1)}, f32[512,512]{1,0:T(8,128)S(1)}, u32[]{:S(2)}, u32[]{:S(2)}) collective-permute-start(f32[512,512]{1,0:T(8,128)S(1)} %take.2), channel_id=1, source_target_pairs={{0,4},{4,0},{8,12},{12,8},{16,20},{20,16},{24,28},{28,24},{1,5},{5... | collective-permute-start | bytes 3145736 | tf_op jit(solution)/shard_map/ppermute | solution.py:300
  15.8 2.5 %collective-permute-start.6 = (f32[640,128]{1,0:T(8,128)S(1)}, f32[640,128]{1,0:T(8,128)S(1)}, u32[]{:S(2)}, u32[]{:S(2)}) collective-permute-start(f32[640,128]{1,0:T(8,128)S(1)} %add.60.mine_ref), channel_id=1, source_target_pairs={{0,1},{1,0},{2,3},{3,2},{4,5},{5,4},{6,7},{7,6},{8,9},{9,8},{10,11... | collective-permute-start | bytes 983048 | tf_op jit(solution)/shard_map/ppermute | solution.py:308
  19.4 0.7 copy-start.4
  20.1 64.5 %collective-permute-start.7 = (f32[512,512]{1,0:T(8,128)}, f32[512,512]{1,0:T(8,128)S(1)}, u32[]{:S(2)}, u32[]{:S(2)}) collective-permute-start(f32[512,512]{1,0:T(8,128)} %take.3), channel_id=1, source_target_pairs={{0,4},{4,0},{8,12},{12,8},{16,20},{20,16},{24,28},{28,24},{1,5},{5... | collective-permute-start | bytes 3145736 | tf_op jit(solution)/shard_map/ppermute | solution.py:300
  22.0 37.0 %collective-permute-start.3 = (f32[320,128]{1,0:T(8,128)}, f32[320,128]{1,0:T(8,128)}, u32[]{:S(2)}, u32[]{:S(2)}) collective-permute-start(f32[320,128]{1,0:T(8,128)} %constant_dynamic-slice_fusion), channel_id=1, source_target_pairs={{0,4},{4,0},{8,12},{12,8},{16,20},{20,16},{24,28},{28,24},{1,5},{5... | collective-permute-start | bytes 491528 | tf_op jit(solution)/shard_map/ppermute | solution.py:311
  59.0 20.6 %collective-permute-start.4 = (f32[320,128]{1,0:T(8,128)}, f32[320,128]{1,0:T(8,128)}, u32[]{:S(2)}, u32[]{:S(2)}) collective-permute-start(f32[320,128]{1,0:T(8,128)} %collective-permute-done.3), channel_id=1, source_target_pairs={{0,2},{1,3},{2,0},{3,1},{4,6},{5,7},{6,4},{7,5},{8,10},{9,11},{10,... | collective-permute-start | bytes 491528 | tf_op jit(solution)/shard_map/ppermute | solution.py:314
  59.3 1.0 copy-start.5
  73.2 46.5 %collective-permute-start.10 = (f32[1024,256]{1,0:T(8,128)}, f32[1024,256]{1,0:T(8,128)}, u32[]{:S(2)}, u32[]{:S(2)}) collective-permute-start(f32[1024,256]{1,0:T(8,128)} %get-tuple-element.23.refs_16_), channel_id=1, source_target_pairs={{0,4},{4,8},{8,12},{12,16},{16,20},{20,24},{24,28},{1,5},{5,9},{9,... | collective-permute-start | bytes 3145736 | tf_op jit(solution)/shard_map/ppermute | solution.py:327
  76.4 47.5 %collective-permute-start.11 = (f32[1024,256]{1,0:T(8,128)}, f32[1024,256]{1,0:T(8,128)}, u32[]{:S(2)}, u32[]{:S(2)}) collective-permute-start(f32[1024,256]{1,0:T(8,128)} %get-tuple-element.24.refs_14_), channel_id=1, source_target_pairs={{4,0},{8,4},{12,8},{16,12},{20,16},{24,20},{28,24},{5,1},{9,5},{13... | collective-permute-start | bytes 3145736 | tf_op jit(solution)/shard_map/ppermute | solution.py:327
  80.8 3.8 %collective-permute-start.5 = (f32[640,128]{1,0:T(8,128)S(1)}, f32[640,128]{1,0:T(8,128)}, u32[]{:S(2)}, u32[]{:S(2)}) collective-permute-start(f32[640,128]{1,0:T(8,128)S(1)} %maximum_select_fusion.mine_ref), channel_id=1, source_target_pairs={{0,1},{1,0},{2,3},{3,2},{4,5},{5,4},{6,7},{7,6},{8,9},{9,8},{10,11... | collective-permute-start | bytes 983048 | tf_op jit(solution)/shard_map/ppermute | solution.py:316
  95.1 0.8 copy-start.2
  95.9 28.0 %collective-permute-start.9 = (f32[512,256]{1,0:T(8,128)}, f32[512,256]{1,0:T(8,128)S(1)}, u32[]{:S(2)}, u32[]{:S(2)}) collective-permute-start(f32[512,256]{1,0:T(8,128)} %get-tuple-element.22), channel_id=1, source_target_pairs={{12,4},{20,12},{28,20},{0,8},{8,16},{16,24},{13,5},{21,13},{29,21}... | collective-permute-start | bytes 1572872 | tf_op jit(solution)/shard_map/ppermute | solution.py:341
  101.0 22.9 %collective-permute-start.8 = (f32[512,256]{1,0:T(8,128)}, f32[512,256]{1,0:T(8,128)S(1)}, u32[]{:S(2)}, u32[]{:S(2)}) collective-permute-start(f32[512,256]{1,0:T(8,128)} %get-tuple-element.18), channel_id=1, source_target_pairs={{12,4},{20,12},{28,20},{0,8},{8,16},{16,24},{13,5},{21,13},{29,21}... | collective-permute-start | bytes 1572872 | tf_op jit(solution)/shard_map/ppermute | solution.py:341
  104.3 2.2 %copy-start.1 = (f32[2048,512]{1,0:T(8,128)S(1)}, f32[2048,512]{1,0:T(8,128)}, u32[]{:S(2)}) copy-start(f32[2048,512]{1,0:T(8,128)} %refs_0_.1) | copy-start | bytes 12582916
  106.5 17.4 %copy-start.3 = (f32[512,256]{1,0:T(8,128)S(1)}, f32[512,256]{1,0:T(8,128)}, u32[]{:S(2)}) copy-start(f32[512,256]{1,0:T(8,128)} %copy-done.2) | copy-start | bytes 1572868

commit v2 on v0

v2 whole, which is shorter than its diff:
```python
import jax
import jax.numpy as jnp
from jax import lax
from jax.experimental import pallas as pl
from jax.experimental.pallas import tpu as pltpu
from jax.sharding import PartitionSpec as P

STEPS = 4
TILE = 128
F32, BF16 = jnp.float32, jnp.bfloat16

epsilon = 1e-06

PLAN = ((0, (6, 9)), (0, (13,)), (4, (36,)))

MIB = 1 << 20
LONG = 10**12
WHOLE = pl.BlockSpec()
IN_VMEM = pl.BlockSpec(memory_space=pltpu.VMEM)
IN_SMEM = pl.BlockSpec(memory_space=pltpu.SMEM)
ANYWHERE = pl.BlockSpec(memory_space=pl.ANY)


def call(kernel, name, operands, in_specs, outs, out_specs, scratch=(), after=(), vmem=56, flops=0, **more):
    given, late = len(operands), len(after)

    def body(*refs):
        kernel(*refs[:given], *refs[given + late :])

    return pl.pallas_call(
        body,
        in_specs=[*in_specs, *[ANYWHERE] * late],
        out_specs=out_specs,
        out_shape=outs,
        scratch_shapes=scratch,
        compiler_params=pltpu.CompilerParams(vmem_limit_bytes=vmem * MIB),
        cost_estimate=pl.CostEstimate(flops=flops, bytes_accessed=0, transcendentals=0),
        name=name,
        **more,
    )(*operands, *after)


def shape(*dims, dtype=F32):
    return jax.ShapeDtypeStruct(dims, dtype)


def split(x):
    high = x.astype(BF16)
    return high, (x - high.astype(F32)).astype(BF16)


def product(a, b):
    return jnp.dot(a, b, preferred_element_type=F32)


def inner(a, b):
    return lax.dot_general(a, b, (((0,), (0,)), ((), ())), preferred_element_type=F32)


def upper_tiles(width):
    n = width // TILE
    at = [slice(i * TILE, (i + 1) * TILE) for i in range(n)]
    return list(enumerate((at[i], at[j]) for i in range(n) for j in range(i, n)))


def gram(core, b, pieces, after, parts=4):
    rows, width = b.shape
    tiles = upper_tiles(width)
    half = len(tiles) // 2

    def kernel(core_ref, b_ref, *refs):
        mine_ref, other_ref, *copies = refs[:-5]
        rows_ref, high_ref, cross_ref, load_sem, store_sem = refs[-5:]
        loads = [
            pltpu.make_async_copy(b_ref.at[pl.ds(p * (rows // parts), rows // parts)], at, load_sem.at[p])
            for p, at in enumerate(rows_ref.at[pl.ds(p * (rows // parts), rows // parts)] for p in range(parts))
        ]
        stores = [
            pltpu.make_async_copy(rows_ref.at[pl.ds(*piece)], copies[k], store_sem.at[k])
            for k, piece in enumerate(pieces)
        ]
        for load in loads:
            load.start()
        for p, load in enumerate(loads):
            load.wait()
            high, low = split(rows_ref[p * (rows // parts) : (p + 1) * (rows // parts)])
            high_ref[p] = inner(high, high)
            cross_ref[p] = inner(high, low)
        for store in stores:
            store.start()

        for flag, outs in enumerate(((mine_ref, other_ref), (other_ref, mine_ref))):

            @pl.when(core_ref[0] == flag)
            def _():
                for k, (i, j) in tiles:
                    tile = sum(high_ref[p, i, j] + cross_ref[p, i, j] for p in range(parts))
                    at = slice(k % half * TILE, (k % half + 1) * TILE)
                    outs[k // half][at, :] = tile + sum(cross_ref[p, j, i] for p in range(parts)).T

        for store in stores:
            store.wait()

    outs = [shape(half * TILE, TILE)] * 2 + [shape(count, width) for _, count in pieces]
    scratch = [
        pltpu.VMEM((rows, width), F32),
        *[pltpu.VMEM((parts, width, width), F32)] * 2,
        pltpu.SemaphoreType.DMA((parts,)),
        pltpu.SemaphoreType.DMA((max(1, len(pieces)),)),
    ]
    specs = [IN_VMEM] * 2 + [ANYWHERE] * len(pieces)
    return call(kernel, "gram", (core, b), [IN_SMEM, ANYWHERE], outs, specs, scratch, after, flops=LONG)


def add(a, b, after):
    def kernel(a_ref, b_ref, out_ref):
        out_ref[...] = a_ref[...] + b_ref[...]

    return call(kernel, "add", (a, b), [IN_VMEM] * 2, shape(*a.shape), IN_VMEM, after=after, vmem=8)


def add_and_cut(second, a, b, after):
    n = a.shape[0] // 2

    def kernel(second_ref, a_ref, b_ref, out_ref, part_ref):
        out_ref[...] = a_ref[...] + b_ref[...]
        for flag, at in ((0, slice(0, n)), (1, slice(n, 2 * n))):

            @pl.when(second_ref[0] == flag)
            def _():
                part_ref[...] = a_ref[at, :] + b_ref[at, :]

    outs = [shape(*a.shape), shape(n, a.shape[1])]
    specs = [IN_SMEM, IN_VMEM, IN_VMEM]
    return call(kernel, "add", (second, a, b), specs, outs, [IN_VMEM] * 2, after=after, vmem=8)


def merge_kernel(second_ref, a_ref, b_ref, out_ref):
    n = a_ref.shape[0]
    for flag, (x_ref, y_ref) in enumerate(((a_ref, b_ref), (b_ref, a_ref))):

        @pl.when(second_ref[0] == flag)
        def _():
            out_ref[:n] = x_ref[...]
            out_ref[n:] = y_ref[...]


def merge(second, a, b, after):
    out = shape(2 * a.shape[0], a.shape[1])
    return call(merge_kernel, "merge", (second, a, b), [IN_SMEM, IN_VMEM, IN_VMEM], out, IN_VMEM, after=after, vmem=8)


def polar_kernel(at_ref, mine_ref, other_ref, high_ref, low_ref, x_ref, one_ref, two_ref):
    width = x_ref.shape[0]
    half = width // 2
    core, top_id, bottom_id, swapped = (at_ref[i] for i in range(4))
    tiles = upper_tiles(width)
    for k, (i, j) in tiles:
        per = len(tiles) // 2
        at = slice(k % per * TILE, (k % per + 1) * TILE)
        tile = jnp.where(core == k // per, mine_ref[at], other_ref[at])
        one_ref[i, j] = tile
        if i != j:
            one_ref[j, i] = tile.T
    row = lax.broadcasted_iota(jnp.int32, (width, width), 0)
    column = lax.broadcasted_iota(jnp.int32, (width, width), 1)
    on_diagonal = row == column

    def global_id(c):
        return jnp.where(c < half, top_id * half + c, bottom_id * half + c - half)

    row_id = global_id(lax.broadcasted_iota(jnp.int32, (width, 1), 0))
    column_id = global_id(lax.broadcasted_iota(jnp.int32, (1, width), 1))
    gram_full = one_ref[...]
    diagonal = jnp.where(on_diagonal, gram_full, 0.0)
    across = jnp.sum(diagonal, axis=0, keepdims=True)
    down = jnp.sum(diagonal, axis=1, keepdims=True)
    skew = gram_full / (down + across + epsilon)
    skew = jnp.where(column_id > row_id, skew, jnp.where(column_id < row_id, -skew, 0.0))
    norm = jnp.sqrt(1.0 + jnp.sum(skew * skew))
    x_ref[...] = (jnp.where(on_diagonal, 1.0, 0.0) + skew) / norm
    for _ in range(STEPS):
        high, low = split(x_ref[...])
        one_ref[...] = inner(high, high)
        two_ref[...] = inner(high, low)
        square = one_ref[...] + two_ref[...] + two_ref[...].T
        turn_high, turn_low = split(jnp.where(on_diagonal, 1.5, 0.0) - 0.5 * square)
        x_ref[...] = product(high, turn_high)
        one_ref[...] = product(high, turn_low)
        two_ref[...] = product(low, turn_high)
        x_ref[...] = x_ref[...] + (one_ref[...] + two_ref[...])
    for flag, (first, second) in enumerate((((0, half), (half, width)), ((half, width), (0, half)))):

        @pl.when(swapped == flag)
        def _():
            for to, (begin, end) in ((0, first), (half, second)):
                high, low = split(x_ref[:, begin:end])
                high_ref[:, to : to + half] = high
                low_ref[:, to : to + half] = low


def polar(at, mine, other, width, after=()):
    specs = [IN_SMEM, IN_VMEM, IN_VMEM]
    outs = [shape(width, width, dtype=BF16)] * 2
    scratch = [pltpu.VMEM((width, width), F32)] * 3
    return call(polar_kernel, "polar", (at, mine, other), specs, outs, [IN_VMEM] * 2, scratch, after, 24, LONG)


def times(rows, w_high, w_low):
    high, low = split(rows)
    return product(high, w_high) + product(high, w_low) + product(low, w_high)


def turn_kernel(b_ref, high_ref, low_ref, first_ref, second_ref):
    half = first_ref.shape[1]
    for out_ref, at in ((first_ref, slice(0, half)), (second_ref, slice(half, 2 * half))):
        out_ref[...] = times(b_ref[...], high_ref[:, at], low_ref[:, at])


def row_blocks(count):
    return next(count // n for n in range(1, count) if count % n == 0 and count // n <= 512 and count // n % 16 == 0)


def turn(b, start, count, w, after=()):
    width = b.shape[1]
    rows = row_blocks(count)
    part = pl.BlockSpec((pl.Element(rows), pl.Element(width)), lambda i: (pl.multiple_of(start + i * rows, 16), 0))
    whole = pl.BlockSpec((width, width), lambda i: (0, 0))
    out = pl.BlockSpec((rows, width // 2), lambda i: (i, 0))
    outs = [shape(count, width // 2)] * 2
    return call(turn_kernel, "turn", (b, *w), [part, whole, whole], outs, [out, out], after=after, vmem=24, grid=(count // rows,))


def turn_all(arrays, w, after=()):
    width = w[0].shape[0]
    half = width // 2

    def kernel(*refs):
        (high_ref, low_ref), parts, outs = refs[:2], refs[2:-2], refs[-2:]
        begin = 0
        for b_ref in parts:
            rows = pl.ds(begin, b_ref.shape[0])
            for out_ref, at in zip(outs, (slice(0, half), slice(half, width)), strict=True):
                out_ref[rows, :] = times(b_ref[...], high_ref[:, at], low_ref[:, at])
            begin += b_ref.shape[0]

    outs = [shape(sum(b.shape[0] for b in arrays), half)] * 2
    return call(kernel, "turn", (*w, *arrays), [WHOLE] * (2 + len(arrays)), outs, [WHOLE] * 2, after=after, vmem=24)


def take(b, pieces):
    n = len(pieces)

    def kernel(b_ref, *refs):
        copies = [
            pltpu.make_async_copy(b_ref.at[pl.ds(*piece)], refs[k], refs[n].at[k]) for k, piece in enumerate(pieces)
        ]
        for copy in copies:
            copy.start()
        for copy in copies:
            copy.wait()

    outs = [shape(count, b.shape[1]) for _, count in pieces]
    return call(kernel, "take", (b,), [ANYWHERE], outs, [IN_VMEM] * n, [pltpu.SemaphoreType.DMA((n,))])


def own(end, b, start, count, w, after=()):
    width = b.shape[1]
    half = width // 2

    def kernel(end_ref, b_ref, high_ref, low_ref, out_ref, rows_ref, sem):
        for which, at in ((1, slice(half, width)), (2, slice(0, half))):

            @pl.when(end_ref[0] == which)
            def _():
                load = pltpu.make_async_copy(b_ref.at[pl.ds(start, count)], rows_ref, sem)
                load.start()
                load.wait()
                out_ref[...] = times(rows_ref[...], high_ref[:, at], low_ref[:, at])

    specs = [IN_SMEM, ANYWHERE, WHOLE, WHOLE]
    scratch = [pltpu.VMEM((count, width), F32), pltpu.SemaphoreType.DMA]
    return call(kernel, "own", (end, b, *w), specs, shape(count, half), WHOLE, scratch, after)


def join(choice, groups, rows, width, into=None):
    sources = [s if isinstance(s, tuple) else (s, 0) for _, _, left, right in groups for s in (*left, *right)]
    arrays = [array for array, _ in sources]
    half = width // 2
    lowest = min(group[0] for group in groups)
    held_rows = max(group[0] + group[1] for group in groups) - lowest

    def kernel(choice_ref, *refs):
        out_ref, held_ref, load_sem, store_sem = refs[-4:]
        loads, stores, taken = [], [], 0
        for k, (start, count, *sides) in enumerate(groups):
            for side, n in enumerate(len(one) for one in sides):
                place = held_ref.at[pl.ds(start - lowest, count), pl.ds(side * half, half)]
                for s in range(n):
                    rows_of_s = refs[taken + s].at[pl.ds(sources[taken + s][1], count)]
                    copy = pltpu.make_async_copy(rows_of_s, place, load_sem.at[2 * k + side])

                    @pl.when(choice_ref[2 * k + side] == s)
                    def _():
                        copy.start()

                loads.append(copy)
                taken += n
        for k, (start, count, *_) in enumerate(groups):
            loads[2 * k].wait()
            loads[2 * k + 1].wait()
            place = held_ref.at[pl.ds(start - lowest, count)]
            stores.append(pltpu.make_async_copy(place, out_ref.at[pl.ds(start, count)], store_sem.at[k]))
            stores[-1].start()
        for copy in stores:
            copy.wait()

    scratch = [
        pltpu.VMEM((held_rows, width), F32),
        pltpu.SemaphoreType.DMA((2 * len(groups),)),
        pltpu.SemaphoreType.DMA((len(groups),)),
    ]
    operands = (choice, *arrays)
    more = {}
    if into is not None:
        operands += (into,)
        more["input_output_aliases"] = {len(operands) - 1: 0}
    specs = [IN_SMEM] + [ANYWHERE] * (len(operands) - 1)
    return call(kernel, "join", operands, specs, shape(rows, width), ANYWHERE, scratch, vmem=8, **more)


def shards(history, round_index):
    rows, width = history.shape
    pairs = lax.axis_size("pair")
    levels = pairs // 2
    position = lax.axis_index("pair")
    partner = position ^ 1
    even = position % 2 == 0
    first, last = position == 0, position == pairs - 1
    core, row_half = lax.axis_index("tm") % 2, lax.axis_index("tm") // 2
    cycle_len = 2 * pairs - 1
    round_now = round_index[0]
    swap_pairs = [(p, p ^ 1) for p in range(pairs)]
    swap_cores = [(i, i ^ 1) for i in range(4)]
    swap_rows = [(i, i ^ 2) for i in range(4)]

    def ids(p):
        top_id = jnp.where(p == 0, 0, 1 + jnp.mod(p - 1 - round_now, cycle_len))
        bottom_id = 1 + jnp.mod(2 * pairs - 2 - p - round_now, cycle_len)
        return top_id, bottom_id

    def is_early(p, threshold):
        level = p // 2
        return (p % 2 == 0) & (level >= threshold) | (p % 2 == 1) & (level <= levels - 1 - threshold)

    groups, pieces = [], []
    begin = 0
    for quarter, parts in PLAN:
        counts = [rows * part // 64 for part in parts]
        groups.append((begin, sum(counts), quarter * levels // 4))
        pieces.append([(begin + sum(counts[:i]), count) for i, count in enumerate(counts)])
        begin += sum(counts)
    early = [k for k, group in enumerate(groups) if group[2] < levels]

    def sent_early(k, rows_of_k):
        return lax.ppermute(rows_of_k, "pair", [(p, p ^ 1) for p in range(pairs) if is_early(p, groups[k][2])])

    from_partner = {k: [] for k in early}
    taken = take(history, pieces[early[0]])
    from_partner[early[0]] = [sent_early(early[0], a) for a in taken]

    later = [(k, piece) for k in early[1:] for piece in pieces[k]]
    keep, give, *copies = gram(jnp.stack([core]), history, [piece for _, piece in later], taken)
    summed = add(keep, lax.ppermute(give, "tm", swap_cores), from_partner[early[0]][:1])
    from_row = lax.ppermute(summed, "tm", swap_rows)
    second = jnp.stack([row_half])
    mine, part = add_and_cut(second, summed, from_row, from_partner[early[0]][1:])
    other = lax.ppermute(mine, "tm", swap_cores)
    part = lax.ppermute(part, "pair", swap_pairs)
    for (k, _), a in zip(later, copies, strict=True):
        from_partner[k].append(sent_early(k, a))

    w = polar(jnp.stack([core, *ids(position), first.astype(jnp.int32)]), mine, other, width, (part,))
    late = {}
    for k, (begin, count, threshold) in enumerate(groups):
        if threshold > 0:
            right, left = turn(history, begin, count, w)
            to_right = [(p, p + 1) for p in range(pairs - 1) if not is_early(p, threshold)]
            to_left = [(p, p - 1) for p in range(1, pairs) if not is_early(p, threshold)]
            late[k] = (right, left, lax.ppermute(right, "pair", to_right), lax.ppermute(left, "pair", to_left))

    part_2 = lax.ppermute(part, "tm", swap_rows)
    mine_q = merge(second, part, part_2, [late[k][0] for k in late])
    other_q = lax.ppermute(mine_q, "tm", swap_cores)
    flag_q = (even | (partner == 0)).astype(jnp.int32)
    w_q = polar(jnp.stack([core, *ids(partner), flag_q]), mine_q, other_q, width, from_partner[early[1]])
    end = jnp.stack([first + 2 * last]).astype(jnp.int32)
    near, passed = {}, {}
    always = [k for k in early if groups[k][2] == 0]
    after = ()
    for k in early:
        threshold = groups[k][2]
        near[k], far = turn_all(from_partner[k], w_q, after)
        onward = [(p ^ 1, p - 1) for p in range(2, pairs, 2) if is_early(p, threshold)]
        onward += [(p ^ 1, p + 1) for p in range(1, pairs - 1, 2) if is_early(p, threshold)]
        passed[k] = lax.ppermute(far, "pair", onward)
        if k == early[0]:
            alone = own(end, history, groups[always[0]][0], sum(groups[k][1] for k in always), w, (far,))
            after = (alone, passed[k])

    ready, joined = {}, None
    for k, (begin, count, threshold) in enumerate(groups):
        left_from, right_from = [], []
        top_choice, bottom_choice = 0, 0
        if k in near:
            left_from += [near[k], passed[k]]
            right_from += [near[k], passed[k]]
            top_choice = jnp.where(even, 1, 0)
            bottom_choice = jnp.where(even, 0, 1)
        if k in always:
            left_from.append((alone, begin))
            right_from.append((alone, begin))
            top_choice = jnp.where(first, 2, top_choice)
            bottom_choice = jnp.where(last, 2, bottom_choice)
        if k in late:
            n = len(left_from)
            right, left, from_left, from_right = late[k]
            left_from += [from_left, left]
            right_from += [from_right, right]
            top_choice = jnp.where(is_early(position - 1, threshold) & ~first, top_choice, n)
            bottom_choice = jnp.where(is_early(position + 1, threshold) & ~last, bottom_choice, n)
            top_choice = jnp.where(first, n + 1, top_choice)
            bottom_choice = jnp.where(last, n + 1, bottom_choice)
        ready[k] = (begin, count, left_from, right_from), [top_choice, bottom_choice]
    for which in (early, [k for k in ready if k not in early]):
        choice = [c for k in which for c in ready[k][1]]
        joined = join(jnp.stack(choice).astype(jnp.int32), [ready[k][0] for k in which], rows, width, joined)
    return joined


def solution(mesh):
    in_specs = (P("tm", "pair"), P())
    out_specs = P("tm", "pair")
    return jax.shard_map(shards, mesh=mesh, in_specs=in_specs, out_specs=out_specs, check_vma=False)
```

time: 220 us -> 111 us (0.50); the launches traced: 215 us -> 111 us
  waiting for transfers between devices: 126 us -> 41.4 us
  matrix products: 42.9 us -> 0 us
  Pallas kernels: 0 us -> 41.4 us
  starting transfers between devices: 6.17 us -> 21.9 us
  between operations: 15.4 us -> 1.07 us
  local copies, waits for them, and re-layouts: 15.1 us -> 4.73 us
  other arithmetic: 10.2 us -> 0.31 us
    ppermute x2 -> x13, waiting for transfers between devices: 89.4 us -> 41.4 us  [the longest x2 17.5 us: shards(): passed[k] = lax.ppermute(far, 'pair', onward)]
    dot_general x10 -> x0, matrix products: 42.9 us -> none  [the longest x1 13.6 us: shards(): jnp.dot(history, factor, precision=lax.Precision.HIGHEST, preferred_eleme...]
    pallas_call x0 -> x13, Pallas kernels: none -> 41.4 us  [call(): pl.pallas_call(body, in_specs=[*in_specs, *[ANYWHERE] * late], out_specs=...]
    psum x1 -> x0, waiting for transfers between devices: 36.2 us -> none  [shards(): gram_full = lax.psum(partial_value, 'tm')]
    ppermute x2 -> x13, starting transfers between devices: 6.17 us -> 21.9 us  [the longest x2 6.4 us: shards(): passed[k] = lax.ppermute(far, 'pair', onward)]
    gather x1 -> x0, local copies, waits for them, and re-layouts: 8.89 us -> none  [start_iterate(): diag_sq = jnp.diagonal(gram_full)]
    concatenate x1 -> x0, local copies, waits for them, and re-layouts: 5.34 us -> none  [shards(): return jnp.concatenate([new_top, new_bottom], axis=1)]
    select_n x3 -> x0, other arithmetic: 5.23 us -> none  [the longest x1 2.78 us: shards(): new_top = jnp.where(position == 0, top_out, from_left)]
  transfers between devices with their start and end apart: 3 -> 13, of which waited for: 3 -> 7; matrix products, arithmetic and copies ran while one was open for 0% -> 0% of each run, Pallas kernels for 0% -> 32%
where the time goes in v2:
time: 111 us
  Pallas kernels  41.4 us (37%)
  waiting for transfers between devices  41.4 us (37%)
  starting transfers between devices  21.9 us (20%)
  local copies, waits for them, and re-layouts  4.73 us (4%)
    pallas_call x13, Pallas kernels, call(): pl.pallas_call(body, in_specs=[*in_specs, *[ANYWHERE] * late], out_specs=...  41.4 us
    ppermute x2, waiting for transfers between devices, shards(): passed[k] = lax.ppermute(far, 'pair', onward)  17.5 us
    ppermute x3, waiting for transfers between devices, sent_early(): lax.ppermute(rows_of_k, 'pair', [(p, p ^ 1) for p in range(pairs) if is_e...  11.6 us
    ppermute x1, waiting for transfers between devices, shards(): lax.ppermute(left, 'pair', to_left)  7.46 us
    ppermute x2, starting transfers between devices, shards(): passed[k] = lax.ppermute(far, 'pair', onward)  6.4 us
    unnamed x16, local copies, waits for them, and re-layouts  4.73 us
    ppermute x1, waiting for transfers between devices, shards(): part = lax.ppermute(part, 'pair', swap_pairs)  3.64 us
    ppermute x1, starting transfers between devices, shards(): lax.ppermute(left, 'pair', to_left)  3.25 us
  transfers between devices with their start and end apart: 13, of which 7 were waited for; matrix products, arithmetic and copies ran while one was open for 0% of the time, Pallas kernels for 32%

profile of v2, /device:TPU:9, one launch (start us, length us, event | category | flops | bytes accessed | tf_op | source)
XLA Modules:
  0.0 110.9 jit_solution(537323276572026413)
XLA Ops:
  0.0 2.2 %take.1 = (f32[192,512]{1,0:T(8,128)}, f32[288,512]{1,0:T(8,128)}) custom-call(f32[2048,512]{1,0:T(8,128)} %refs_1_.3), custom_call_target="tpu_custom_call" | custom-call | tf_op jit(solution)/shard_map/take/pallas_call | solution.py:30
  2.2 1.3 %collective-permute-start.1 = (f32[192,512]{1,0:T(8,128)}, f32[192,512]{1,0:T(8,128)}, u32[]{:S(2)}, u32[]{:S(2)}) collective-permute-start(f32[192,512]{1,0:T(8,128)} %get-tuple-element.22.refs_2_), channel_id=1, source_target_pairs={{0,4},{4,0},{8,12},{12,8},{16,20},{20,16},{24,28},{28,24},{1,5},{5... | collective-permute-start | bytes 1179656 | tf_op jit(solution)/shard_map/ppermute | solution.py:366
  3.5 5.9 %gram.1 = (f32[640,128]{1,0:T(8,128)}, f32[640,128]{1,0:T(8,128)}, f32[416,512]{1,0:T(8,128)}) custom-call(s32[1]{0:T(128)} %bitcast.2.refs_0_, f32[2048,512]{1,0:T(8,128)} %refs_1_.3, f32[192,512]{1,0:T(8,128)} %get-tuple-element.22.refs_2_, f32[288,512]{1,0:T(8,128)} %get-tuple-element.23.refs_3_), custom_call_target="tpu_custom_call" | custom-call | flops 999999995904 | tf_op jit(solution)/shard_map/gram/pallas_call | solution.py:30
  13.6 1.3 %collective-permute-start.2 = (f32[640,128]{1,0:T(8,128)S(1)}, f32[640,128]{1,0:T(8,128)S(1)}, u32[]{:S(2)}, u32[]{:S(2)}) collective-permute-start(f32[640,128]{1,0:T(8,128)S(1)} %add.77.refs_1_), channel_id=1, source_target_pairs={{0,2},{1,3},{2,0},{3,1},{4,6},{5,7},{6,4},{7,5},{8,10},{9,11},{10,... | collective-permute-start | bytes 983048 | tf_op jit(solution)/shard_map/ppermute | solution.py:375
  14.9 10.9 %collective-permute-done.3.refs_3_ = f32[288,512]{1,0:T(8,128)S(1)} collective-permute-done((f32[288,512]{1,0:T(8,128)S(1)}, f32[288,512]{1,0:T(8,128)S(1)}, u32[]{:S(2)}, u32[]{:S(2)}) %collective-permute-start.3) | collective-permute-done | bytes 589856 | tf_op jit(solution)/shard_map/ppermute | solution.py:366
  29.0 3.6 %collective-permute-done.5.refs_3_.refs_1_ = f32[320,128]{1,0:T(8,128)} collective-permute-done((f32[320,128]{1,0:T(8,128)S(1)}, f32[320,128]{1,0:T(8,128)}, u32[]{:S(2)}, u32[]{:S(2)}) %collective-permute-start.5) | collective-permute-done | bytes 163872 | tf_op jit(solution)/shard_map/ppermute | solution.py:379
  32.7 1.2 %collective-permute-start.8 = (f32[320,128]{1,0:T(8,128)}, f32[320,128]{1,0:T(8,128)}, u32[]{:S(2)}, u32[]{:S(2)}) collective-permute-start(f32[320,128]{1,0:T(8,128)} %collective-permute-done.5.refs_3_.refs_1_), channel_id=1, source_target_pairs={{0,2},{1,3},{2,0},{3,1},{4,6},{5,7},{6,4},{7,5},{8,10},{9,11},{10,... | collective-permute-start | bytes 491528 | tf_op jit(solution)/shard_map/ppermute | solution.py:392
  33.9 8.2 %polar.2 = (bf16[512,512]{1,0:T(8,128)(2,1)S(1)}, bf16[512,512]{1,0:T(8,128)(2,1)S(1)}) custom-call(s32[4]{0:T(128)S(1)} %pad_add_fusion.1.refs_0_, f32[640,128]{1,0:T(8,128)S(1)} %get-tuple-element.26.refs_1_, f32[640,128]{1,0:T(8,128)S(1)} %collective-permute-done.4.refs_2_, f32[320,128]{1,0:T(8,128)} %collective-permute-done.5.refs_3_.refs_1_), custom_call_target="tpu_custom_call" | custom-call | flops 999999995904 | tf_op jit(solution)/shard_map/polar/pallas_call | solution.py:30
  42.1 2.6 %copy-done = f32[2048,512]{1,0:T(8,128)S(1)} copy-done((f32[2048,512]{1,0:T(8,128)S(1)}, f32[2048,512]{1,0:T(8,128)}, u32[]{:S(2)}) %copy-start) | copy-done | bytes 4194328
  44.7 3.3 %turn.3 = (f32[1152,256]{1,0:T(8,128)}, f32[1152,256]{1,0:T(8,128)}) custom-call(f32[2048,512]{1,0:T(8,128)S(1)} %copy-done, bf16[512,512]{1,0:T(8,128)(2,1)S(1)} %get-tuple-element.28.refs_1_.refs_2_, bf16[512,512]{1,0:T(8,128)(2,1)S(1)} %get-tuple-element.29.refs_2_.refs_3_), custom_call_target="tpu_custom_call" | custom-call | tf_op jit(solution)/shard_map/turn/pallas_call | solution.py:30
  49.1 1.6 %collective-permute-start.9 = (f32[640,128]{1,0:T(8,128)S(1)}, f32[640,128]{1,0:T(8,128)S(1)}, u32[]{:S(2)}, u32[]{:S(2)}) collective-permute-start(f32[640,128]{1,0:T(8,128)S(1)} %merge.1.refs_1_), channel_id=1, source_target_pairs={{0,1},{1,0},{2,3},{3,2},{4,5},{5,4},{6,7},{7,6},{8,9},{9,8},{10,11... | collective-permute-start | bytes 983048 | tf_op jit(solution)/shard_map/ppermute | solution.py:394
  50.8 3.1 %collective-permute-start.6 = (f32[1152,256]{1,0:T(8,128)}, f32[1152,256]{1,0:T(8,128)}, u32[]{:S(2)}, u32[]{:S(2)}) collective-permute-start(f32[1152,256]{1,0:T(8,128)} %get-tuple-element.30.refs_3_.refs_4_), channel_id=1, source_target_pairs={{0,4},{4,8},{8,12},{12,16},{16,20},{20,24},{24,28},{1,5},{5,9},{9,... | collective-permute-start | bytes 3538952 | tf_op jit(solution)/shard_map/ppermute | solution.py:390
  53.9 3.2 %collective-permute-start.7 = (f32[1152,256]{1,0:T(8,128)}, f32[1152,256]{1,0:T(8,128)}, u32[]{:S(2)}, u32[]{:S(2)}) collective-permute-start(f32[1152,256]{1,0:T(8,128)} %get-tuple-element.31.refs_2_), channel_id=1, source_target_pairs={{4,0},{8,4},{12,8},{16,12},{20,16},{24,20},{28,24},{5,1},{9,5},{13... | collective-permute-start | bytes 3538952 | tf_op jit(solution)/shard_map/ppermute | solution.py:390
  57.2 8.2 %polar.3 = (bf16[512,512]{1,0:T(8,128)(2,1)S(1)}, bf16[512,512]{1,0:T(8,128)(2,1)S(1)}) custom-call(s32[4]{0:T(128)S(1)} %pad_add_fusion.3.refs_0_, f32[640,128]{1,0:T(8,128)S(1)} %merge.1.refs_1_, f32[640,128]{1,0:T(8,128)S(1)} %collective-permute-done.9.refs_2_, f32[416,512]{1,0:T(8,128)} %collective-permute-done.10.refs_3_.refs_2_), custom_call_target="tpu_custom_call" | custom-call | flops 999999995904 | tf_op jit(solution)/shard_map/polar/pallas_call | solution.py:30
  65.4 1.9 %turn.4 = (f32[480,256]{1,0:T(8,128)S(1)}, f32[480,256]{1,0:T(8,128)S(1)}) custom-call(bf16[512,512]{1,0:T(8,128)(2,1)S(1)} %get-tuple-element.33.refs_0_, bf16[512,512]{1,0:T(8,128)(2,1)S(1)} %get-tuple-element.34.refs_1_, f32[192,512]{1,0:T(8,128)} %collective-permute-done.1.refs_2_, f32[288,512]{1,0:T(8,128)S(1)} %collective-permute-done.3.refs_3_), custom_call_target="tpu_custom_call" | custom-call | tf_op jit(solution)/shard_map/turn/pallas_call | solution.py:30
  67.3 3.2 %collective-permute-start.11 = (f32[480,256]{1,0:T(8,128)S(1)}, f32[480,256]{1,0:T(8,128)S(1)}, u32[]{:S(2)}, u32[]{:S(2)}) collective-permute-start(f32[480,256]{1,0:T(8,128)S(1)} %get-tuple-element.36.refs_4_), channel_id=1, source_target_pairs={{12,4},{20,12},{28,20},{0,8},{8,16},{16,24},{13,5},{21,13},{29,21}... | collective-permute-start | bytes 1474568 | tf_op jit(solution)/shard_map/ppermute | solution.py:406
  70.6 2.1 %own.1.refs_3_.refs_6_.refs_9_.refs_12_ = f32[896,256]{1,0:T(8,128)} custom-call(s32[1]{0:T(128)} %bitcast.13.refs_0_, f32[2048,512]{1,0:T(8,128)} %refs_1_.3, bf16[512,512]{1,0:T(8,128)(2,1)} %copy-done.3, bf16[512,512]{1,0:T(8,128)(2,1)} %copy-done.4, f32[480,256]{1,0:T(8,128)} %copy-done.5), custom_call_target="tpu_custom_call" | custom-call | tf_op jit(solution)/shard_map/own/pallas_call | solution.py:30
  72.7 8.8 %collective-permute-done.11.refs_4_.refs_2_.refs_5_ = f32[480,256]{1,0:T(8,128)S(1)} collective-permute-done((f32[480,256]{1,0:T(8,128)S(1)}, f32[480,256]{1,0:T(8,128)S(1)}, u32[]{:S(2)}, u32[]{:S(2)}) %collective-permute-start.11) | collective-permute-done | bytes 491552 | tf_op jit(solution)/shard_map/ppermute | solution.py:406
  82.7 2.8 %turn.5 = (f32[416,256]{1,0:T(8,128)S(1)}, f32[416,256]{1,0:T(8,128)}) custom-call(bf16[512,512]{1,0:T(8,128)(2,1)S(1)} %get-tuple-element.33.refs_0_, bf16[512,512]{1,0:T(8,128)(2,1)S(1)} %get-tuple-element.34.refs_1_, f32[416,512]{1,0:T(8,128)} %collective-permute-done.10.refs_3_.refs_2_, f32[896,256]{1,0:T(8,128)S(1)} %copy-done.1, ...), custom_call_target="tpu_custom_call" | custom-call | tf_op jit(solution)/shard_map/turn/pallas_call | solution.py:30
  85.5 3.2 %collective-permute-start.12 = (f32[416,256]{1,0:T(8,128)}, f32[416,256]{1,0:T(8,128)S(1)}, u32[]{:S(2)}, u32[]{:S(2)}) collective-permute-start(f32[416,256]{1,0:T(8,128)} %get-tuple-element.38), channel_id=1, source_target_pairs={{12,4},{20,12},{28,20},{0,8},{8,16},{16,24},{13,5},{21,13},{29,21}... | collective-permute-start | bytes 1277960 | tf_op jit(solution)/shard_map/ppermute | solution.py:406
  88.8 8.7 %collective-permute-done.12.refs_8_.refs_11_ = f32[416,256]{1,0:T(8,128)S(1)} collective-permute-done((f32[416,256]{1,0:T(8,128)}, f32[416,256]{1,0:T(8,128)S(1)}, u32[]{:S(2)}, u32[]{:S(2)}) %collective-permute-start.12) | collective-permute-done | bytes 426016 | tf_op jit(solution)/shard_map/ppermute | solution.py:406
  97.6 2.0 %join.2.refs_5_ = f32[2048,512]{1,0:T(8,128)} custom-call(s32[4]{0:T(128)S(1)} %pad_add_fusion.2.refs_0_, f32[480,256]{1,0:T(8,128)S(1)} %get-tuple-element.35.refs_1_.refs_4_, f32[480,256]{1,0:T(8,128)S(1)} %collective-permute-done.11.refs_4_.refs_2_.refs_5_, f32[896,256]{1,0:T(8,128)S(1)} %copy-done.2, f32[480,256]{1,0:T(8,128)S(1)} %get-tuple-element.35.refs_1_.refs_4_, ...), custom_call_target="tpu_custom_call" | custom-call | tf_op jit(solution)/shard_map/join/pallas_call | solution.py:30
  99.6 7.5 %collective-permute-done.7.refs_3_ = f32[1152,256]{1,0:T(8,128)} collective-permute-done((f32[1152,256]{1,0:T(8,128)}, f32[1152,256]{1,0:T(8,128)}, u32[]{:S(2)}, u32[]{:S(2)}) %collective-permute-start.7) | collective-permute-done | bytes 1179680 | tf_op jit(solution)/shard_map/ppermute | solution.py:390
  107.1 3.6 %join.3 = f32[2048,512]{1,0:T(8,128)} custom-call(s32[2]{0:T(128)S(1)} %pad_add_fusion.refs_0_, f32[1152,256]{1,0:T(8,128)} %collective-permute-done.6.refs_1_, f32[1152,256]{1,0:T(8,128)} %get-tuple-element.31.refs_2_, f32[1152,256]{1,0:T(8,128)} %collective-permute-done.7.refs_3_, ...), custom_call_target="tpu_custom_call", output_to_operand_aliasing={{}: (5, {})} | custom-call | tf_op jit(solution)/shard_map/join/pallas_call | solution.py:30
  (35 shorter events, 9.2 us)
Async XLA Ops:
  2.2 10.4 %collective-permute-start.1 = (f32[192,512]{1,0:T(8,128)}, f32[192,512]{1,0:T(8,128)}, u32[]{:S(2)}, u32[]{:S(2)}) collective-permute-start(f32[192,512]{1,0:T(8,128)} %get-tuple-element.22.refs_2_), channel_id=1, source_target_pairs={{0,4},{4,0},{8,12},{12,8},{16,20},{20,16},{24,28},{28,24},{1,5},{5... | collective-permute-start | bytes 1179656 | tf_op jit(solution)/shard_map/ppermute | solution.py:366
  3.5 6.9 %copy-start.7 = (f32[288,512]{1,0:T(8,128)S(1)}, f32[288,512]{1,0:T(8,128)}, u32[]{:S(2)}) copy-start(f32[288,512]{1,0:T(8,128)} %get-tuple-element.23.refs_3_) | copy-start | bytes 1769476
  9.4 2.5 %collective-permute-start = (f32[640,128]{1,0:T(8,128)}, f32[640,128]{1,0:T(8,128)S(1)}, u32[]{:S(2)}, u32[]{:S(2)}) collective-permute-start(f32[640,128]{1,0:T(8,128)} %get-tuple-element.25), channel_id=1, source_target_pairs={{0,1},{1,0},{2,3},{3,2},{4,5},{5,4},{6,7},{7,6},{8,9},{9,8},{10,11... | collective-permute-start | bytes 983048 | tf_op jit(solution)/shard_map/ppermute | solution.py:374
  10.4 15.4 %collective-permute-start.3 = (f32[288,512]{1,0:T(8,128)S(1)}, f32[288,512]{1,0:T(8,128)S(1)}, u32[]{:S(2)}, u32[]{:S(2)}) collective-permute-start(f32[288,512]{1,0:T(8,128)S(1)} %copy-done.7), channel_id=1, source_target_pairs={{0,4},{4,0},{8,12},{12,8},{16,20},{20,16},{24,28},{28,24},{1,5},{5... | collective-permute-start | bytes 1769480 | tf_op jit(solution)/shard_map/ppermute | solution.py:366
  12.6 1.0 copy-start.6
  13.6 12.2 %collective-permute-start.2 = (f32[640,128]{1,0:T(8,128)S(1)}, f32[640,128]{1,0:T(8,128)S(1)}, u32[]{:S(2)}, u32[]{:S(2)}) collective-permute-start(f32[640,128]{1,0:T(8,128)S(1)} %add.77.refs_1_), channel_id=1, source_target_pairs={{0,2},{1,3},{2,0},{3,1},{4,6},{5,7},{6,4},{7,5},{8,10},{9,11},{10,... | collective-permute-start | bytes 983048 | tf_op jit(solution)/shard_map/ppermute | solution.py:375
  25.9 8.0 %collective-permute-start.4 = (f32[640,128]{1,0:T(8,128)S(1)}, f32[640,128]{1,0:T(8,128)S(1)}, u32[]{:S(2)}, u32[]{:S(2)}) collective-permute-start(f32[640,128]{1,0:T(8,128)S(1)} %get-tuple-element.26.refs_1_), channel_id=1, source_target_pairs={{0,1},{1,0},{2,3},{3,2},{4,5},{5,4},{6,7},{7,6},{8,9},{9,8},{10,11... | collective-permute-start | bytes 983048 | tf_op jit(solution)/shard_map/ppermute | solution.py:378
  26.8 5.9 %collective-permute-start.5 = (f32[320,128]{1,0:T(8,128)S(1)}, f32[320,128]{1,0:T(8,128)}, u32[]{:S(2)}, u32[]{:S(2)}) collective-permute-start(f32[320,128]{1,0:T(8,128)S(1)} %get-tuple-element.27), channel_id=1, source_target_pairs={{0,4},{4,0},{8,12},{12,8},{16,20},{20,16},{24,28},{28,24},{1,5},{5... | collective-permute-start | bytes 491528 | tf_op jit(solution)/shard_map/ppermute | solution.py:379
  28.0 29.2 %collective-permute-start.10 = (f32[416,512]{1,0:T(8,128)}, f32[416,512]{1,0:T(8,128)}, u32[]{:S(2)}, u32[]{:S(2)}) collective-permute-start(f32[416,512]{1,0:T(8,128)} %get-tuple-element.32), channel_id=1, source_target_pairs={{0,4},{4,0},{8,12},{12,8},{16,20},{20,16},{24,28},{28,24},{1,5},{5... | collective-permute-start | bytes 2555912 | tf_op jit(solution)/shard_map/ppermute | solution.py:366
  32.7 15.4 %collective-permute-start.8 = (f32[320,128]{1,0:T(8,128)}, f32[320,128]{1,0:T(8,128)}, u32[]{:S(2)}, u32[]{:S(2)}) collective-permute-start(f32[320,128]{1,0:T(8,128)} %collective-permute-done.5.refs_3_.refs_1_), channel_id=1, source_target_pairs={{0,2},{1,3},{2,0},{3,1},{4,6},{5,7},{6,4},{7,5},{8,10},{9,11},{10,... | collective-permute-start | bytes 491528 | tf_op jit(solution)/shard_map/ppermute | solution.py:392
  42.1 5.9 %copy-start.3 = (bf16[512,512]{1,0:T(8,128)(2,1)}, bf16[512,512]{1,0:T(8,128)(2,1)S(1)}, u32[]{:S(2)}) copy-start(bf16[512,512]{1,0:T(8,128)(2,1)S(1)} %get-tuple-element.28.refs_1_.refs_2_) | copy-start | bytes 1572868
  42.1 5.9 %copy-start.4 = (bf16[512,512]{1,0:T(8,128)(2,1)}, bf16[512,512]{1,0:T(8,128)(2,1)S(1)}, u32[]{:S(2)}) copy-start(bf16[512,512]{1,0:T(8,128)(2,1)S(1)} %get-tuple-element.29.refs_2_.refs_3_) | copy-start | bytes 1572868
  42.1 2.6 %copy-start = (f32[2048,512]{1,0:T(8,128)S(1)}, f32[2048,512]{1,0:T(8,128)}, u32[]{:S(2)}) copy-start(f32[2048,512]{1,0:T(8,128)} %refs_1_.3) | copy-start | bytes 12582916
  49.1 8.1 %collective-permute-start.9 = (f32[640,128]{1,0:T(8,128)S(1)}, f32[640,128]{1,0:T(8,128)S(1)}, u32[]{:S(2)}, u32[]{:S(2)}) collective-permute-start(f32[640,128]{1,0:T(8,128)S(1)} %merge.1.refs_1_), channel_id=1, source_target_pairs={{0,1},{1,0},{2,3},{3,2},{4,5},{5,4},{6,7},{7,6},{8,9},{9,8},{10,11... | collective-permute-start | bytes 983048 | tf_op jit(solution)/shard_map/ppermute | solution.py:394
  50.8 56.3 %collective-permute-start.6 = (f32[1152,256]{1,0:T(8,128)}, f32[1152,256]{1,0:T(8,128)}, u32[]{:S(2)}, u32[]{:S(2)}) collective-permute-start(f32[1152,256]{1,0:T(8,128)} %get-tuple-element.30.refs_3_.refs_4_), channel_id=1, source_target_pairs={{0,4},{4,8},{8,12},{12,16},{16,20},{20,24},{24,28},{1,5},{5,9},{9,... | collective-permute-start | bytes 3538952 | tf_op jit(solution)/shard_map/ppermute | solution.py:390
  53.9 53.2 %collective-permute-start.7 = (f32[1152,256]{1,0:T(8,128)}, f32[1152,256]{1,0:T(8,128)}, u32[]{:S(2)}, u32[]{:S(2)}) collective-permute-start(f32[1152,256]{1,0:T(8,128)} %get-tuple-element.31.refs_2_), channel_id=1, source_target_pairs={{4,0},{8,4},{12,8},{16,12},{20,16},{24,20},{28,24},{5,1},{9,5},{13... | collective-permute-start | bytes 3538952 | tf_op jit(solution)/shard_map/ppermute | solution.py:390
  67.3 3.2 %copy-start.5 = (f32[480,256]{1,0:T(8,128)}, f32[480,256]{1,0:T(8,128)S(1)}, u32[]{:S(2)}) copy-start(f32[480,256]{1,0:T(8,128)S(1)} %get-tuple-element.36.refs_4_) | copy-start | bytes 1474564
  67.3 14.1 %collective-permute-start.11 = (f32[480,256]{1,0:T(8,128)S(1)}, f32[480,256]{1,0:T(8,128)S(1)}, u32[]{:S(2)}, u32[]{:S(2)}) collective-permute-start(f32[480,256]{1,0:T(8,128)S(1)} %get-tuple-element.36.refs_4_), channel_id=1, source_target_pairs={{12,4},{20,12},{28,20},{0,8},{8,16},{16,24},{13,5},{21,13},{29,21}... | collective-permute-start | bytes 1474568 | tf_op jit(solution)/shard_map/ppermute | solution.py:406
  81.5 1.2 %copy-start.1 = (f32[896,256]{1,0:T(8,128)S(1)}, f32[896,256]{1,0:T(8,128)}, u32[]{:S(2)}) copy-start(f32[896,256]{1,0:T(8,128)} %own.1.refs_3_.refs_6_.refs_9_.refs_12_) | copy-start | bytes 2752516
  82.6 14.9 %copy-start.2 = (f32[896,256]{1,0:T(8,128)S(1)}, f32[896,256]{1,0:T(8,128)}, u32[]{:S(2)}) copy-start(f32[896,256]{1,0:T(8,128)} %own.1.refs_3_.refs_6_.refs_9_.refs_12_) | copy-start | bytes 2752516
  85.5 12.1 %collective-permute-start.12 = (f32[416,256]{1,0:T(8,128)}, f32[416,256]{1,0:T(8,128)S(1)}, u32[]{:S(2)}, u32[]{:S(2)}) collective-permute-start(f32[416,256]{1,0:T(8,128)} %get-tuple-element.38), channel_id=1, source_target_pairs={{12,4},{20,12},{28,20},{0,8},{8,16},{16,24},{13,5},{21,13},{29,21}... | collective-permute-start | bytes 1277960 | tf_op jit(solution)/shard_map/ppermute | solution.py:406

commit v3 on v2

--- a/solution.py
+++ b/solution.py
@@ -11,7 +11,7 @@
 
 epsilon = 1e-06
 
-PLAN = ((0, (6, 9)), (0, (13,)), (4, (36,)))
+PLAN = ((0, (6, 12)), (0, (14,)), (4, (32,)))
 
 MIB = 1 << 20
 LONG = 10**12
@@ -63,7 +63,7 @@
     return list(enumerate((at[i], at[j]) for i in range(n) for j in range(i, n)))
 
 
-def gram(core, b, pieces, after, parts=4):
+def gram(core, b, pieces, kept, after, parts=4):
     rows, width = b.shape
     tiles = upper_tiles(width)
     half = len(tiles) // 2
@@ -77,7 +77,7 @@
         ]
         stores = [
             pltpu.make_async_copy(rows_ref.at[pl.ds(*piece)], copies[k], store_sem.at[k])
-            for k, piece in enumerate(pieces)
+            for k, piece in enumerate((*pieces, *kept))
         ]
         for load in loads:
             load.start()
@@ -101,15 +101,15 @@
         for store in stores:
             store.wait()
 
-    outs = [shape(half * TILE, TILE)] * 2 + [shape(count, width) for _, count in pieces]
+    outs = [shape(half * TILE, TILE)] * 2 + [shape(count, width) for _, count in (*pieces, *kept)]
     scratch = [
         pltpu.VMEM((rows, width), F32),
         *[pltpu.VMEM((parts, width, width), F32)] * 2,
         pltpu.SemaphoreType.DMA((parts,)),
-        pltpu.SemaphoreType.DMA((max(1, len(pieces)),)),
+        pltpu.SemaphoreType.DMA((len(outs) - 2,)),
     ]
-    specs = [IN_VMEM] * 2 + [ANYWHERE] * len(pieces)
-    return call(kernel, "gram", (core, b), [IN_SMEM, ANYWHERE], outs, specs, scratch, after, flops=LONG)
+    specs = [IN_VMEM] * 2 + [ANYWHERE] * len(pieces) + [IN_VMEM] * len(kept)
+    return call(kernel, "gram", (core, b), [IN_SMEM, ANYWHERE], outs, specs, scratch, after, 57, LONG)
 
 
 def add(a, b, after):
@@ -211,27 +211,7 @@
     return product(high, w_high) + product(high, w_low) + product(low, w_high)
 
 
-def turn_kernel(b_ref, high_ref, low_ref, first_ref, second_ref):
-    half = first_ref.shape[1]
-    for out_ref, at in ((first_ref, slice(0, half)), (second_ref, slice(half, 2 * half))):
-        out_ref[...] = times(b_ref[...], high_ref[:, at], low_ref[:, at])
-
-
-def row_blocks(count):
-    return next(count // n for n in range(1, count) if count % n == 0 and count // n <= 512 and count // n % 16 == 0)
-
-
-def turn(b, start, count, w, after=()):
-    width = b.shape[1]
-    rows = row_blocks(count)
-    part = pl.BlockSpec((pl.Element(rows), pl.Element(width)), lambda i: (pl.multiple_of(start + i * rows, 16), 0))
-    whole = pl.BlockSpec((width, width), lambda i: (0, 0))
-    out = pl.BlockSpec((rows, width // 2), lambda i: (i, 0))
-    outs = [shape(count, width // 2)] * 2
-    return call(turn_kernel, "turn", (b, *w), [part, whole, whole], outs, [out, out], after=after, vmem=24, grid=(count // rows,))
-
-
-def turn_all(arrays, w, after=()):
+def turn(arrays, w, after=(), spec=WHOLE):
     width = w[0].shape[0]
     half = width // 2
 
@@ -245,88 +225,89 @@
             begin += b_ref.shape[0]
 
     outs = [shape(sum(b.shape[0] for b in arrays), half)] * 2
-    return call(kernel, "turn", (*w, *arrays), [WHOLE] * (2 + len(arrays)), outs, [WHOLE] * 2, after=after, vmem=24)
-
-
-def take(b, pieces):
-    n = len(pieces)
-
-    def kernel(b_ref, *refs):
+    return call(kernel, "turn", (*w, *arrays), [WHOLE] * 2 + [spec] * len(arrays), outs, [WHOLE] * 2, after=after, vmem=24)
+
+
+def take(b, start, count, parts=4):
+    rows = count // parts
+
+    def kernel(b_ref, out_ref, sem):
         copies = [
-            pltpu.make_async_copy(b_ref.at[pl.ds(*piece)], refs[k], refs[n].at[k]) for k, piece in enumerate(pieces)
+            pltpu.make_async_copy(
+                b_ref.at[pl.ds(start + p * rows, rows)], out_ref.at[pl.ds(p * rows, rows)], sem.at[p]
+            )
+            for p in range(parts)
         ]
         for copy in copies:
             copy.start()
         for copy in copies:
             copy.wait()
 
-    outs = [shape(count, b.shape[1]) for _, count in pieces]
-    return call(kernel, "take", (b,), [ANYWHERE], outs, [IN_VMEM] * n, [pltpu.SemaphoreType.DMA((n,))])
-
-
-def own(end, b, start, count, w, after=()):
+    scratch = [pltpu.SemaphoreType.DMA((parts,))]
+    return call(kernel, "take", (b,), [ANYWHERE], shape(count, b.shape[1]), IN_VMEM, scratch)
+
+
+def own(at_end, b, start, count, w, after=()):
     width = b.shape[1]
     half = width // 2
 
-    def kernel(end_ref, b_ref, high_ref, low_ref, out_ref, rows_ref, sem):
-        for which, at in ((1, slice(half, width)), (2, slice(0, half))):
-
-            @pl.when(end_ref[0] == which)
-            def _():
-                load = pltpu.make_async_copy(b_ref.at[pl.ds(start, count)], rows_ref, sem)
-                load.start()
-                load.wait()
-                out_ref[...] = times(rows_ref[...], high_ref[:, at], low_ref[:, at])
+    def kernel(at_end_ref, b_ref, high_ref, low_ref, out_ref, rows_ref, sem):
+        @pl.when(at_end_ref[0] == 1)
+        def _():
+            load = pltpu.make_async_copy(b_ref.at[pl.ds(start, count)], rows_ref, sem)
+            load.start()
+            load.wait()
+            out_ref[...] = times(rows_ref[...], high_ref[:, half:], low_ref[:, half:])
 
     specs = [IN_SMEM, ANYWHERE, WHOLE, WHOLE]
     scratch = [pltpu.VMEM((count, width), F32), pltpu.SemaphoreType.DMA]
-    return call(kernel, "own", (end, b, *w), specs, shape(count, half), WHOLE, scratch, after)
-
-
-def join(choice, groups, rows, width, into=None):
-    sources = [s if isinstance(s, tuple) else (s, 0) for _, _, left, right in groups for s in (*left, *right)]
-    arrays = [array for array, _ in sources]
+    return call(kernel, "own", (at_end, b, *w), specs, shape(count, half), IN_VMEM, scratch, after, 24)
+
+
+def join(choice, groups, rows, width, into=None, after=()):
+    places = []
+    for start, count, sources in groups:
+        for s, source in enumerate(sources):
+            if source is not None:
+                array, begin = source if isinstance(source, tuple) else (source, 0)
+                places.append((start, count, s, array, begin))
     half = width // 2
-    lowest = min(group[0] for group in groups)
-    held_rows = max(group[0] + group[1] for group in groups) - lowest
 
     def kernel(choice_ref, *refs):
-        out_ref, held_ref, load_sem, store_sem = refs[-4:]
-        loads, stores, taken = [], [], 0
-        for k, (start, count, *sides) in enumerate(groups):
-            for side, n in enumerate(len(one) for one in sides):
-                place = held_ref.at[pl.ds(start - lowest, count), pl.ds(side * half, half)]
-                for s in range(n):
-                    rows_of_s = refs[taken + s].at[pl.ds(sources[taken + s][1], count)]
-                    copy = pltpu.make_async_copy(rows_of_s, place, load_sem.at[2 * k + side])
-
-                    @pl.when(choice_ref[2 * k + side] == s)
+        out_ref, sem = refs[-2:]
+
+        def each(act):
+            for k, (start, count, s, _, begin) in enumerate(places):
+                for side in (0, 1):
+                    store = pltpu.make_async_copy(
+                        refs[k].at[pl.ds(begin, count)],
+                        out_ref.at[pl.ds(start, count), pl.ds(side * half, half)],
+                        sem.at[k],
+                    )
+
+                    @pl.when(choice_ref[side] == s)
                     def _():
-                        copy.start()
-
-                loads.append(copy)
-                taken += n
-        for k, (start, count, *_) in enumerate(groups):
-            loads[2 * k].wait()
-            loads[2 * k + 1].wait()
-            place = held_ref.at[pl.ds(start - lowest, count)]
-            stores.append(pltpu.make_async_copy(place, out_ref.at[pl.ds(start, count)], store_sem.at[k]))
-            stores[-1].start()
-        for copy in stores:
-            copy.wait()
-
-    scratch = [
-        pltpu.VMEM((held_rows, width), F32),
-        pltpu.SemaphoreType.DMA((2 * len(groups),)),
-        pltpu.SemaphoreType.DMA((len(groups),)),
-    ]
-    operands = (choice, *arrays)
+                        act(store)
+
+        each(lambda store: store.start())
+        each(lambda store: store.wait())
+
+    operands = (choice, *[array for _, _, _, array, _ in places])
+    specs = [IN_SMEM] + [IN_VMEM] * len(places)
     more = {}
     if into is not None:
+        more["input_output_aliases"] = {len(operands): 0}
         operands += (into,)
-        more["input_output_aliases"] = {len(operands) - 1: 0}
-    specs = [IN_SMEM] + [ANYWHERE] * (len(operands) - 1)
-    return call(kernel, "join", operands, specs, shape(rows, width), ANYWHERE, scratch, vmem=8, **more)
+        specs.append(ANYWHERE)
+    scratch = [pltpu.SemaphoreType.DMA((len(places),))]
+    return call(kernel, "join", operands, specs, shape(rows, width), ANYWHERE, scratch, after, 8, **more)
+
+
+def mark(after):
+    def kernel(out_ref):
+        out_ref[...] = jnp.zeros_like(out_ref)
+
+    return call(kernel, "mark", (), [], shape(8, TILE), WHOLE, after=(after,))
 
 
 def shards(history, round_index):
@@ -366,76 +347,61 @@
         return lax.ppermute(rows_of_k, "pair", [(p, p ^ 1) for p in range(pairs) if is_early(p, groups[k][2])])
 
     from_partner = {k: [] for k in early}
-    taken = take(history, pieces[early[0]])
+    taken = [history[begin : begin + count] for begin, count in pieces[early[0]]]
     from_partner[early[0]] = [sent_early(early[0], a) for a in taken]
 
     later = [(k, piece) for k in early[1:] for piece in pieces[k]]
-    keep, give, *copies = gram(jnp.stack([core]), history, [piece for _, piece in later], taken)
+    kept = [k for k in range(len(groups)) if groups[k][2] > 0]
+    at_once, then = [piece for _, piece in later], [groups[k][:2] for k in kept]
+    keep, give, *copies = gram(jnp.stack([core]), history, at_once, then, taken)
+    kept = dict(zip(kept, copies[len(later) :]))
     summed = add(keep, lax.ppermute(give, "tm", swap_cores), from_partner[early[0]][:1])
     from_row = lax.ppermute(summed, "tm", swap_rows)
     second = jnp.stack([row_half])
-    mine, part = add_and_cut(second, summed, from_row, from_partner[early[0]][1:])
+    mine, part = add_and_cut(second, summed, from_row, ())
     other = lax.ppermute(mine, "tm", swap_cores)
     part = lax.ppermute(part, "pair", swap_pairs)
-    for (k, _), a in zip(later, copies, strict=True):
+    for (k, _), a in zip(later, copies):
         from_partner[k].append(sent_early(k, a))
 
-    w = polar(jnp.stack([core, *ids(position), first.astype(jnp.int32)]), mine, other, width, (part,))
+    flag = (~even | first).astype(jnp.int32)
+    w = polar(jnp.stack([core, *ids(position), flag]), mine, other, width, (part, *from_partner[early[0]]))
     late = {}
-    for k, (begin, count, threshold) in enumerate(groups):
+    for k, (_, _, threshold) in enumerate(groups):
         if threshold > 0:
-            right, left = turn(history, begin, count, w)
-            to_right = [(p, p + 1) for p in range(pairs - 1) if not is_early(p, threshold)]
-            to_left = [(p, p - 1) for p in range(1, pairs) if not is_early(p, threshold)]
-            late[k] = (right, left, lax.ppermute(right, "pair", to_right), lax.ppermute(left, "pair", to_left))
+            near, far = turn([kept[k]], w, spec=IN_VMEM)
+            to_partner = [(p, p ^ 1) for p in range(pairs) if not is_early(p, threshold)]
+            onward = [(p, p - 1) for p in range(2, pairs, 2) if not is_early(p, threshold)]
+            onward += [(p, p + 1) for p in range(1, pairs - 1, 2) if not is_early(p, threshold)]
+            late[k] = lax.ppermute(near, "pair", to_partner), lax.ppermute(far, "pair", onward), far
 
     part_2 = lax.ppermute(part, "tm", swap_rows)
-    mine_q = merge(second, part, part_2, [late[k][0] for k in late])
+    mine_q = merge(second, part, part_2, [late[k][2] for k in late])
     other_q = lax.ppermute(mine_q, "tm", swap_cores)
     flag_q = (even | (partner == 0)).astype(jnp.int32)
     w_q = polar(jnp.stack([core, *ids(partner), flag_q]), mine_q, other_q, width, from_partner[early[1]])
-    end = jnp.stack([first + 2 * last]).astype(jnp.int32)
+    at_end = jnp.stack([first | last]).astype(jnp.int32)
     near, passed = {}, {}
     always = [k for k in early if groups[k][2] == 0]
     after = ()
     for k in early:
         threshold = groups[k][2]
-        near[k], far = turn_all(from_partner[k], w_q, after)
+        near[k], far = turn(from_partner[k], w_q, after)
         onward = [(p ^ 1, p - 1) for p in range(2, pairs, 2) if is_early(p, threshold)]
         onward += [(p ^ 1, p + 1) for p in range(1, pairs - 1, 2) if is_early(p, threshold)]
         passed[k] = lax.ppermute(far, "pair", onward)
         if k == early[0]:
-            alone = own(end, history, groups[always[0]][0], sum(groups[k][1] for k in always), w, (far,))
-            after = (alone, passed[k])
-
-    ready, joined = {}, None
-    for k, (begin, count, threshold) in enumerate(groups):
-        left_from, right_from = [], []
-        top_choice, bottom_choice = 0, 0
-        if k in near:
-            left_from += [near[k], passed[k]]
-            right_from += [near[k], passed[k]]
-            top_choice = jnp.where(even, 1, 0)
-            bottom_choice = jnp.where(even, 0, 1)
-        if k in always:
-            left_from.append((alone, begin))
-            right_from.append((alone, begin))
-            top_choice = jnp.where(first, 2, top_choice)
-            bottom_choice = jnp.where(last, 2, bottom_choice)
-        if k in late:
-            n = len(left_from)
-            right, left, from_left, from_right = late[k]
-            left_from += [from_left, left]
-            right_from += [from_right, right]
-            top_choice = jnp.where(is_early(position - 1, threshold) & ~first, top_choice, n)
-            bottom_choice = jnp.where(is_early(position + 1, threshold) & ~last, bottom_choice, n)
-            top_choice = jnp.where(first, n + 1, top_choice)
-            bottom_choice = jnp.where(last, n + 1, bottom_choice)
-        ready[k] = (begin, count, left_from, right_from), [top_choice, bottom_choice]
-    for which in (early, [k for k in ready if k not in early]):
-        choice = [c for k in which for c in ready[k][1]]
-        joined = join(jnp.stack(choice).astype(jnp.int32), [ready[k][0] for k in which], rows, width, joined)
-    return joined
+            alone = own(at_end, history, groups[always[0]][0], sum(groups[k][1] for k in always), w, (far,))
+            after = (alone,)
+
+    sources = {k: (near[k], passed[k], (alone, groups[k][0])) for k in early} | late
+    choice = jnp.stack([jnp.where(even, 1 + first, 0), jnp.where(even, 0, 1 + last)]).astype(jnp.int32)
+    near_late = {k: (sources[k][0], None, None) for k in late}
+    far_late = {k: (None, *sources[k][1:]) for k in late}
+    first_part, last_part = {k: sources[k] for k in early} | far_late, near_late
+    joined = join(choice, [(*groups[k][:2], first_part[k]) for k in first_part], rows, width)
+    last_groups = [(*groups[k][:2], last_part[k]) for k in last_part]
+    return join(choice, last_groups, rows, width, joined, (mark(joined),))
 
 
 def solution(mesh):

time: 111 us -> 106 us (0.955)
  waiting for transfers between devices: 41.4 us -> 35.4 us
  local copies, waits for them, and re-layouts: 4.73 us -> 9.63 us
  Pallas kernels: 41.4 us -> 38.8 us
  starting transfers between devices: 21.9 us -> 19.9 us
    ppermute x3, waiting for transfers between devices: 11.6 us -> 0.01 us  [sent_early(): lax.ppermute(rows_of_k, 'pair', [(p, p ^ 1) for p in range(pairs) if is_e...]
    ppermute x1, waiting for transfers between devices: 0.01 us -> 7.69 us  [shards(): from_row = lax.ppermute(summed, 'tm', swap_rows)]
    ppermute x2, waiting for transfers between devices: 7.46 us -> 2.87 us  [the longest x1 2.87 us: shards(): lax.ppermute(near, 'pair', to_partner)]
    ppermute x1, waiting for transfers between devices: 3.64 us -> 7.67 us  [shards(): part = lax.ppermute(part, 'pair', swap_pairs)]
    slice x0 -> x2, local copies, waits for them, and re-layouts: none -> 3.86 us  [shards(): taken = [history[begin:begin + count] for begin, count in pieces[early[0]]]]
    pallas_call x13, Pallas kernels: 41.4 us -> 38.8 us  [call(): pl.pallas_call(body, in_specs=[*in_specs, *[ANYWHERE] * late], out_specs=...]
    ppermute x2, starting transfers between devices: 6.35 us -> 4.43 us  [the longest x1 2.41 us: shards(): lax.ppermute(near, 'pair', to_partner)]
    ppermute x2, waiting for transfers between devices: 17.5 us -> 15.9 us  [shards(): passed[k] = lax.ppermute(far, 'pair', onward)]
  transfers between devices with their start and end apart: 13 -> 13, of which waited for: 7 -> 5; matrix products, arithmetic and copies ran while one was open for 0% -> 2% of each run, Pallas kernels for 32% -> 35%
where the time goes in v3:
time: 106 us; the launch traced here: 105 us
  Pallas kernels  38.8 us (37%)
  waiting for transfers between devices  35.4 us (33%)
  starting transfers between devices  19.9 us (19%)
  local copies, waits for them, and re-layouts  9.63 us (9%)
  between operations  1.1 us (1%)
    pallas_call x13, Pallas kernels, call(): pl.pallas_call(body, in_specs=[*in_specs, *[ANYWHERE] * late], out_specs=...  38.8 us
    ppermute x2, waiting for transfers between devices, shards(): passed[k] = lax.ppermute(far, 'pair', onward)  15.9 us
    ppermute x1, waiting for transfers between devices, shards(): from_row = lax.ppermute(summed, 'tm', swap_rows)  7.69 us
    ppermute x1, waiting for transfers between devices, shards(): part = lax.ppermute(part, 'pair', swap_pairs)  7.67 us
    ppermute x2, starting transfers between devices, shards(): passed[k] = lax.ppermute(far, 'pair', onward)  5.96 us
    unnamed x26, local copies, waits for them, and re-layouts  5.77 us
    slice x2, local copies, waits for them, and re-layouts, shards(): taken = [history[begin:begin + count] for begin, count in pieces[early[0]]]  3.86 us
    ppermute x1, waiting for transfers between devices, shards(): lax.ppermute(near, 'pair', to_partner)  2.87 us
  transfers between devices with their start and end apart: 13, of which 5 were waited for; matrix products, arithmetic and copies ran while one was open for 2% of the time, Pallas kernels for 35%

profile of v3, /device:TPU:9, one launch (start us, length us, event | category | flops | bytes accessed | tf_op | source)
XLA Modules:
  0.0 105.0 jit_solution(3780491953080680955)
XLA Ops:
  0.0 1.8 %slice.6.refs_2_ = f32[192,512]{1,0:T(8,128)} slice(f32[2048,512]{1,0:T(8,128)} %refs_1_.3), slice={[0:192], [0:512]} | slice | bytes 786432 | tf_op jit(solution)/shard_map/slice | solution.py:350
  3.0 2.1 %slice.7.refs_3_ = f32[384,512]{1,0:T(8,128)} slice(f32[2048,512]{1,0:T(8,128)} %refs_1_.3), slice={[192:576], [0:512]} | slice | bytes 1572864 | tf_op jit(solution)/shard_map/slice | solution.py:350
  5.1 6.7 %gram.1 = (f32[640,128]{1,0:T(8,128)}, f32[640,128]{1,0:T(8,128)}, f32[448,512]{1,0:T(8,128)}, f32[1024,512]{1,0:T(8,128)}) custom-call(s32[1]{0:T(128)} %bitcast.2.refs_0_, f32[2048,512]{1,0:T(8,128)} %refs_1_.3, f32[192,512]{1,0:T(8,128)} %slice.6.refs_2_, f32[384,512]{1,0:T(8,128)} %slice.7.refs_3_), custom_call_target="tpu_custom_call" | custom-call | flops 999999995904 | tf_op jit(solution)/shard_map/gram/pallas_call | solution.py:30
  15.3 1.3 %collective-permute-start.2 = (f32[640,128]{1,0:T(8,128)S(1)}, f32[640,128]{1,0:T(8,128)S(1)}, u32[]{:S(2)}, u32[]{:S(2)}) collective-permute-start(f32[640,128]{1,0:T(8,128)S(1)} %add.68.refs_1_), channel_id=1, source_target_pairs={{0,2},{1,3},{2,0},{3,1},{4,6},{5,7},{6,4},{7,5},{8,10},{9,11},{10,... | collective-permute-start | bytes 983048 | tf_op jit(solution)/shard_map/ppermute | solution.py:359
  16.6 7.7 %collective-permute-done.2.refs_2_ = f32[640,128]{1,0:T(8,128)S(1)} collective-permute-done((f32[640,128]{1,0:T(8,128)S(1)}, f32[640,128]{1,0:T(8,128)S(1)}, u32[]{:S(2)}, u32[]{:S(2)}) %collective-permute-start.2) | collective-permute-done | bytes 327712 | tf_op jit(solution)/shard_map/ppermute | solution.py:359
  24.4 1.3 %collective-permute-start.3 = (f32[640,128]{1,0:T(8,128)S(1)}, f32[640,128]{1,0:T(8,128)S(1)}, u32[]{:S(2)}, u32[]{:S(2)}) collective-permute-start(f32[640,128]{1,0:T(8,128)S(1)} %get-tuple-element.23.refs_1_), channel_id=1, source_target_pairs={{0,1},{1,0},{2,3},{3,2},{4,5},{5,4},{6,7},{7,6},{8,9},{9,8},{10,11... | collective-permute-start | bytes 983048 | tf_op jit(solution)/shard_map/ppermute | solution.py:362
  25.9 1.2 %collective-permute-start.9 = (f32[448,512]{1,0:T(8,128)}, f32[448,512]{1,0:T(8,128)}, u32[]{:S(2)}, u32[]{:S(2)}) collective-permute-start(f32[448,512]{1,0:T(8,128)} %get-tuple-element.30), channel_id=1, source_target_pairs={{0,4},{4,0},{8,12},{12,8},{16,20},{20,16},{24,28},{28,24},{1,5},{5... | collective-permute-start | bytes 2752520 | tf_op jit(solution)/shard_map/ppermute | solution.py:347
  27.9 7.7 %collective-permute-done.4.refs_3_.refs_1_ = f32[320,128]{1,0:T(8,128)} collective-permute-done((f32[320,128]{1,0:T(8,128)S(1)}, f32[320,128]{1,0:T(8,128)}, u32[]{:S(2)}, u32[]{:S(2)}) %collective-permute-start.4) | collective-permute-done | bytes 163872 | tf_op jit(solution)/shard_map/ppermute | solution.py:363
  35.5 1.2 %collective-permute-start.7 = (f32[320,128]{1,0:T(8,128)}, f32[320,128]{1,0:T(8,128)}, u32[]{:S(2)}, u32[]{:S(2)}) collective-permute-start(f32[320,128]{1,0:T(8,128)} %collective-permute-done.4.refs_3_.refs_1_), channel_id=1, source_target_pairs={{0,2},{1,3},{2,0},{3,1},{4,6},{5,7},{6,4},{7,5},{8,10},{9,11},{10,... | collective-permute-start | bytes 491528 | tf_op jit(solution)/shard_map/ppermute | solution.py:378
  36.8 8.4 %polar.2 = (bf16[512,512]{1,0:T(8,128)(2,1)S(1)}, bf16[512,512]{1,0:T(8,128)(2,1)S(1)}) custom-call(s32[4]{0:T(128)S(1)} %pad_add_fusion.1.refs_0_, f32[640,128]{1,0:T(8,128)S(1)} %get-tuple-element.23.refs_1_, f32[640,128]{1,0:T(8,128)S(1)} %collective-permute-done.3.refs_2_, f32[320,128]{1,0:T(8,128)} %collective-permute-done.4.refs_3_.refs_1_, ...), custom_call_target="tpu_custom_call" | custom-call | flops 999999995904 | tf_op jit(solution)/shard_map/polar/pallas_call | solution.py:30
  45.2 3.2 %turn.3 = (f32[1024,256]{1,0:T(8,128)}, f32[1024,256]{1,0:T(8,128)}) custom-call(bf16[512,512]{1,0:T(8,128)(2,1)S(1)} %get-tuple-element.25.refs_0_.refs_2_, bf16[512,512]{1,0:T(8,128)(2,1)S(1)} %get-tuple-element.26.refs_1_.refs_3_, f32[1024,512]{1,0:T(8,128)S(1)} %copy-done.1), custom_call_target="tpu_custom_call" | custom-call | tf_op jit(solution)/shard_map/turn/pallas_call | solution.py:30
  49.4 1.7 %collective-permute-start.8 = (f32[640,128]{1,0:T(8,128)S(1)}, f32[640,128]{1,0:T(8,128)S(1)}, u32[]{:S(2)}, u32[]{:S(2)}) collective-permute-start(f32[640,128]{1,0:T(8,128)S(1)} %merge.1.refs_1_), channel_id=1, source_target_pairs={{0,1},{1,0},{2,3},{3,2},{4,5},{5,4},{6,7},{7,6},{8,9},{9,8},{10,11... | collective-permute-start | bytes 983048 | tf_op jit(solution)/shard_map/ppermute | solution.py:380
  51.2 2.0 %collective-permute-start.12 = (f32[1024,256]{1,0:T(8,128)}, f32[1024,256]{1,0:T(8,128)}, u32[]{:S(2)}, u32[]{:S(2)}) collective-permute-start(f32[1024,256]{1,0:T(8,128)} %get-tuple-element.29.refs_3_.refs_8_), channel_id=1, source_target_pairs={{8,4},{16,12},{24,20},{4,8},{12,16},{20,24},{9,5},{17,13},{25,21},... | collective-permute-start | bytes 3145736 | tf_op jit(solution)/shard_map/ppermute | solution.py:376
  53.2 2.4 %collective-permute-start.6 = (f32[1024,256]{1,0:T(8,128)}, f32[1024,256]{1,0:T(8,128)}, u32[]{:S(2)}, u32[]{:S(2)}) collective-permute-start(f32[1024,256]{1,0:T(8,128)} %get-tuple-element.28), channel_id=1, source_target_pairs={{0,4},{4,0},{8,12},{12,8},{16,20},{20,16},{24,28},{28,24},{1,5},{5... | collective-permute-start | bytes 3145736 | tf_op jit(solution)/shard_map/ppermute | solution.py:376
  55.7 8.2 %polar.3 = (bf16[512,512]{1,0:T(8,128)(2,1)S(1)}, bf16[512,512]{1,0:T(8,128)(2,1)S(1)}) custom-call(s32[4]{0:T(128)S(1)} %pad_add_fusion.2.refs_0_, f32[640,128]{1,0:T(8,128)S(1)} %merge.1.refs_1_, f32[640,128]{1,0:T(8,128)S(1)} %collective-permute-done.8.refs_2_, f32[448,512]{1,0:T(8,128)} %collective-permute-done.9.refs_3_.refs_2_), custom_call_target="tpu_custom_call" | custom-call | flops 999999995904 | tf_op jit(solution)/shard_map/polar/pallas_call | solution.py:30
  63.9 2.9 %turn.4 = (f32[576,256]{1,0:T(8,128)S(1)}, f32[576,256]{1,0:T(8,128)}) custom-call(bf16[512,512]{1,0:T(8,128)(2,1)S(1)} %get-tuple-element.31.refs_0_, bf16[512,512]{1,0:T(8,128)(2,1)S(1)} %get-tuple-element.32.refs_1_, f32[192,512]{1,0:T(8,128)} %collective-permute-done.1.refs_2_.refs_4_, f32[384,512]{1,0:T(8,128)S(1)} %copy-done.7), custom_call_target="tpu_custom_call" | custom-call | tf_op jit(solution)/shard_map/turn/pallas_call | solution.py:30
  67.6 3.2 %collective-permute-start.10 = (f32[576,256]{1,0:T(8,128)}, f32[576,256]{1,0:T(8,128)}, u32[]{:S(2)}, u32[]{:S(2)}) collective-permute-start(f32[576,256]{1,0:T(8,128)} %get-tuple-element.34.refs_4_), channel_id=1, source_target_pairs={{12,4},{20,12},{28,20},{0,8},{8,16},{16,24},{13,5},{21,13},{29,21}... | collective-permute-start | bytes 1769480 | tf_op jit(solution)/shard_map/ppermute | solution.py:392
  70.9 2.2 %copy-done = f32[2048,512]{1,0:T(8,128)S(1)} copy-done((f32[2048,512]{1,0:T(8,128)S(1)}, f32[2048,512]{1,0:T(8,128)}, u32[]{:S(2)}) %copy-start) | copy-done | bytes 4194328
  73.1 2.0 %turn.5 = (f32[448,256]{1,0:T(8,128)S(1)}, f32[448,256]{1,0:T(8,128)S(1)}) custom-call(bf16[512,512]{1,0:T(8,128)(2,1)S(1)} %get-tuple-element.31.refs_0_, bf16[512,512]{1,0:T(8,128)(2,1)S(1)} %get-tuple-element.32.refs_1_, f32[448,512]{1,0:T(8,128)} %collective-permute-done.9.refs_3_.refs_2_, f32[1024,256]{1,0:T(8,128)S(1)} %own.1.refs_3_.refs_6_), custom_call_target="tpu_custom_call" | custom-call | tf_op jit(solution)/shard_map/turn/pallas_call | solution.py:30
  75.1 2.8 %collective-permute-start.11 = (f32[448,256]{1,0:T(8,128)S(1)}, f32[448,256]{1,0:T(8,128)S(1)}, u32[]{:S(2)}, u32[]{:S(2)}) collective-permute-start(f32[448,256]{1,0:T(8,128)S(1)} %get-tuple-element.36), channel_id=1, source_target_pairs={{12,4},{20,12},{28,20},{0,8},{8,16},{16,24},{13,5},{21,13},{29,21}... | collective-permute-start | bytes 1376264 | tf_op jit(solution)/shard_map/ppermute | solution.py:392
  78.0 15.9 %collective-permute-done.11.refs_5_ = f32[448,256]{1,0:T(8,128)S(1)} collective-permute-done((f32[448,256]{1,0:T(8,128)S(1)}, f32[448,256]{1,0:T(8,128)S(1)}, u32[]{:S(2)}, u32[]{:S(2)}) %collective-permute-start.11) | collective-permute-done | bytes 458784 | tf_op jit(solution)/shard_map/ppermute | solution.py:392
  95.0 3.5 %join.2.refs_0_.refs_2_ = f32[2048,512]{1,0:T(8,128)} custom-call(s32[2]{0:T(128)S(1)} %pad_add_fusion.refs_0_, f32[576,256]{1,0:T(8,128)S(1)} %copy-done.9, f32[576,256]{1,0:T(8,128)} %collective-permute-done.10.refs_2_, f32[1024,256]{1,0:T(8,128)S(1)} %own.1.refs_3_.refs_6_, f32[448,256]{1,0:T(8,128)S(1)} %get-tuple-element.35.refs_4_, ...), custom_call_target="tpu_custom_call" | custom-call | tf_op jit(solution)/shard_map/join/pallas_call | solution.py:30
  99.0 2.9 %collective-permute-done.6.refs_1_ = f32[1024,256]{1,0:T(8,128)} collective-permute-done((f32[1024,256]{1,0:T(8,128)}, f32[1024,256]{1,0:T(8,128)}, u32[]{:S(2)}, u32[]{:S(2)}) %collective-permute-start.6) | collective-permute-done | bytes 1048608 | tf_op jit(solution)/shard_map/ppermute | solution.py:376
  102.6 2.2 %join.3 = f32[2048,512]{1,0:T(8,128)} custom-call(s32[2]{0:T(128)S(1)} %pad_add_fusion.refs_0_, f32[1024,256]{1,0:T(8,128)} %collective-permute-done.6.refs_1_, f32[2048,512]{1,0:T(8,128)} %join.2.refs_0_.refs_2_, f32[8,128]{1,0:T(8,128)S(1)} %copy-done.11), custom_call_target="tpu_custom_call", output_to_operand_aliasing={{}: (2, {})} | custom-call | tf_op jit(solution)/shard_map/join/pallas_call | solution.py:30
  (46 shorter events, 9.5 us)
Async XLA Ops:
  1.8 12.5 %collective-permute-start.1 = (f32[192,512]{1,0:T(8,128)}, f32[192,512]{1,0:T(8,128)}, u32[]{:S(2)}, u32[]{:S(2)}) collective-permute-start(f32[192,512]{1,0:T(8,128)} %slice.6.refs_2_), channel_id=1, source_target_pairs={{0,4},{4,0},{8,12},{12,8},{16,20},{20,16},{24,28},{28,24},{1,5},{5... | collective-permute-start | bytes 1179656 | tf_op jit(solution)/shard_map/ppermute | solution.py:347
  5.1 7.7 %copy-start.12 = (f32[384,512]{1,0:T(8,128)S(1)}, f32[384,512]{1,0:T(8,128)}, u32[]{:S(2)}) copy-start(f32[384,512]{1,0:T(8,128)} %slice.7.refs_3_) | copy-start | bytes 2359300
  11.8 2.5 %collective-permute-start = (f32[640,128]{1,0:T(8,128)}, f32[640,128]{1,0:T(8,128)S(1)}, u32[]{:S(2)}, u32[]{:S(2)}) collective-permute-start(f32[640,128]{1,0:T(8,128)} %get-tuple-element.22), channel_id=1, source_target_pairs={{0,1},{1,0},{2,3},{3,2},{4,5},{5,4},{6,7},{7,6},{8,9},{9,8},{10,11... | collective-permute-start | bytes 983048 | tf_op jit(solution)/shard_map/ppermute | solution.py:358
  12.8 24.0 %collective-permute-start.5 = (f32[384,512]{1,0:T(8,128)S(1)}, f32[384,512]{1,0:T(8,128)S(1)}, u32[]{:S(2)}, u32[]{:S(2)}) collective-permute-start(f32[384,512]{1,0:T(8,128)S(1)} %copy-done.12), channel_id=1, source_target_pairs={{0,4},{4,0},{8,12},{12,8},{16,20},{20,16},{24,28},{28,24},{1,5},{5... | collective-permute-start | bytes 2359304 | tf_op jit(solution)/shard_map/ppermute | solution.py:347
  14.3 1.0 copy-start.10
  15.3 9.0 %collective-permute-start.2 = (f32[640,128]{1,0:T(8,128)S(1)}, f32[640,128]{1,0:T(8,128)S(1)}, u32[]{:S(2)}, u32[]{:S(2)}) collective-permute-start(f32[640,128]{1,0:T(8,128)S(1)} %add.68.refs_1_), channel_id=1, source_target_pairs={{0,2},{1,3},{2,0},{3,1},{4,6},{5,7},{6,4},{7,5},{8,10},{9,11},{10,... | collective-permute-start | bytes 983048 | tf_op jit(solution)/shard_map/ppermute | solution.py:359
  24.4 12.4 %collective-permute-start.3 = (f32[640,128]{1,0:T(8,128)S(1)}, f32[640,128]{1,0:T(8,128)S(1)}, u32[]{:S(2)}, u32[]{:S(2)}) collective-permute-start(f32[640,128]{1,0:T(8,128)S(1)} %get-tuple-element.23.refs_1_), channel_id=1, source_target_pairs={{0,1},{1,0},{2,3},{3,2},{4,5},{5,4},{6,7},{7,6},{8,9},{9,8},{10,11... | collective-permute-start | bytes 983048 | tf_op jit(solution)/shard_map/ppermute | solution.py:362
  25.6 9.9 %collective-permute-start.4 = (f32[320,128]{1,0:T(8,128)S(1)}, f32[320,128]{1,0:T(8,128)}, u32[]{:S(2)}, u32[]{:S(2)}) collective-permute-start(f32[320,128]{1,0:T(8,128)S(1)} %get-tuple-element.24), channel_id=1, source_target_pairs={{0,4},{4,0},{8,12},{12,8},{16,20},{20,16},{24,28},{28,24},{1,5},{5... | collective-permute-start | bytes 491528 | tf_op jit(solution)/shard_map/ppermute | solution.py:363
  25.9 29.8 %collective-permute-start.9 = (f32[448,512]{1,0:T(8,128)}, f32[448,512]{1,0:T(8,128)}, u32[]{:S(2)}, u32[]{:S(2)}) collective-permute-start(f32[448,512]{1,0:T(8,128)} %get-tuple-element.30), channel_id=1, source_target_pairs={{0,4},{4,0},{8,12},{12,8},{16,20},{20,16},{24,28},{28,24},{1,5},{5... | collective-permute-start | bytes 2752520 | tf_op jit(solution)/shard_map/ppermute | solution.py:347
  35.5 12.9 %collective-permute-start.7 = (f32[320,128]{1,0:T(8,128)}, f32[320,128]{1,0:T(8,128)}, u32[]{:S(2)}, u32[]{:S(2)}) collective-permute-start(f32[320,128]{1,0:T(8,128)} %collective-permute-done.4.refs_3_.refs_1_), channel_id=1, source_target_pairs={{0,2},{1,3},{2,0},{3,1},{4,6},{5,7},{6,4},{7,5},{8,10},{9,11},{10,... | collective-permute-start | bytes 491528 | tf_op jit(solution)/shard_map/ppermute | solution.py:378
  36.8 8.4 %copy-start.6 = (f32[384,512]{1,0:T(8,128)}, f32[384,512]{1,0:T(8,128)S(1)}, u32[]{:S(2)}) copy-start(f32[384,512]{1,0:T(8,128)S(1)} %collective-permute-done.5.refs_5_.refs_3_) | copy-start | bytes 2359300
  36.8 8.4 %copy-start.1 = (f32[1024,512]{1,0:T(8,128)S(1)}, f32[1024,512]{1,0:T(8,128)}, u32[]{:S(2)}) copy-start(f32[1024,512]{1,0:T(8,128)} %get-tuple-element.27.refs_2_) | copy-start | bytes 6291460
  45.2 3.2 %copy-start.2 = (bf16[512,512]{1,0:T(8,128)(2,1)}, bf16[512,512]{1,0:T(8,128)(2,1)S(1)}, u32[]{:S(2)}) copy-start(bf16[512,512]{1,0:T(8,128)(2,1)S(1)} %get-tuple-element.25.refs_0_.refs_2_) | copy-start | bytes 1572868
  45.2 3.2 %copy-start.4 = (bf16[512,512]{1,0:T(8,128)(2,1)}, bf16[512,512]{1,0:T(8,128)(2,1)S(1)}, u32[]{:S(2)}) copy-start(bf16[512,512]{1,0:T(8,128)(2,1)S(1)} %get-tuple-element.26.refs_1_.refs_3_) | copy-start | bytes 1572868
  49.4 6.2 %collective-permute-start.8 = (f32[640,128]{1,0:T(8,128)S(1)}, f32[640,128]{1,0:T(8,128)S(1)}, u32[]{:S(2)}, u32[]{:S(2)}) collective-permute-start(f32[640,128]{1,0:T(8,128)S(1)} %merge.1.refs_1_), channel_id=1, source_target_pairs={{0,1},{1,0},{2,3},{3,2},{4,5},{5,4},{6,7},{7,6},{8,9},{9,8},{10,11... | collective-permute-start | bytes 983048 | tf_op jit(solution)/shard_map/ppermute | solution.py:380
  51.2 42.7 %collective-permute-start.12 = (f32[1024,256]{1,0:T(8,128)}, f32[1024,256]{1,0:T(8,128)}, u32[]{:S(2)}, u32[]{:S(2)}) collective-permute-start(f32[1024,256]{1,0:T(8,128)} %get-tuple-element.29.refs_3_.refs_8_), channel_id=1, source_target_pairs={{8,4},{16,12},{24,20},{4,8},{12,16},{20,24},{9,5},{17,13},{25,21},... | collective-permute-start | bytes 3145736 | tf_op jit(solution)/shard_map/ppermute | solution.py:376
  53.2 48.7 %collective-permute-start.6 = (f32[1024,256]{1,0:T(8,128)}, f32[1024,256]{1,0:T(8,128)}, u32[]{:S(2)}, u32[]{:S(2)}) collective-permute-start(f32[1024,256]{1,0:T(8,128)} %get-tuple-element.28), channel_id=1, source_target_pairs={{0,4},{4,0},{8,12},{12,8},{16,20},{20,16},{24,28},{28,24},{1,5},{5... | collective-permute-start | bytes 3145736 | tf_op jit(solution)/shard_map/ppermute | solution.py:376
  55.6 8.2 %copy-start.7 = (f32[384,512]{1,0:T(8,128)S(1)}, f32[384,512]{1,0:T(8,128)}, u32[]{:S(2)}) copy-start(f32[384,512]{1,0:T(8,128)} %copy-done.6) | copy-start | bytes 2359300
  55.6 15.2 %copy-start.3 = (bf16[512,512]{1,0:T(8,128)(2,1)S(1)}, bf16[512,512]{1,0:T(8,128)(2,1)}, u32[]{:S(2)}) copy-start(bf16[512,512]{1,0:T(8,128)(2,1)} %copy-done.2) | copy-start | bytes 1572868
  55.7 15.2 %copy-start.5 = (bf16[512,512]{1,0:T(8,128)(2,1)S(1)}, bf16[512,512]{1,0:T(8,128)(2,1)}, u32[]{:S(2)}) copy-start(bf16[512,512]{1,0:T(8,128)(2,1)} %copy-done.4) | copy-start | bytes 1572868
  67.6 26.3 %collective-permute-start.10 = (f32[576,256]{1,0:T(8,128)}, f32[576,256]{1,0:T(8,128)}, u32[]{:S(2)}, u32[]{:S(2)}) collective-permute-start(f32[576,256]{1,0:T(8,128)} %get-tuple-element.34.refs_4_), channel_id=1, source_target_pairs={{12,4},{20,12},{28,20},{0,8},{8,16},{16,24},{13,5},{21,13},{29,21}... | collective-permute-start | bytes 1769480 | tf_op jit(solution)/shard_map/ppermute | solution.py:392
  70.8 2.2 %copy-start = (f32[2048,512]{1,0:T(8,128)S(1)}, f32[2048,512]{1,0:T(8,128)}, u32[]{:S(2)}) copy-start(f32[2048,512]{1,0:T(8,128)} %refs_1_.3) | copy-start | bytes 12582916
  75.1 18.8 %collective-permute-start.11 = (f32[448,256]{1,0:T(8,128)S(1)}, f32[448,256]{1,0:T(8,128)S(1)}, u32[]{:S(2)}, u32[]{:S(2)}) collective-permute-start(f32[448,256]{1,0:T(8,128)S(1)} %get-tuple-element.36), channel_id=1, source_target_pairs={{12,4},{20,12},{28,20},{0,8},{8,16},{16,24},{13,5},{21,13},{29,21}... | collective-permute-start | bytes 1376264 | tf_op jit(solution)/shard_map/ppermute | solution.py:392
  93.9 1.1 %copy-start.9 = (f32[576,256]{1,0:T(8,128)S(1)}, f32[576,256]{1,0:T(8,128)}, u32[]{:S(2)}) copy-start(f32[576,256]{1,0:T(8,128)} %copy-done.8) | copy-start | bytes 1769476
  (2 other events, 1.5 us)

commit v4 on v3

--- a/solution.py
+++ b/solution.py
@@ -11,7 +11,8 @@
 
 epsilon = 1e-06
 
-PLAN = ((0, (6, 12)), (0, (14,)), (4, (32,)))
+PLAN = ((0, (6, 12, 13)), (4, (33,)))
+FIRST = 2
 
 MIB = 1 << 20
 LONG = 10**12
@@ -19,9 +20,10 @@
 IN_VMEM = pl.BlockSpec(memory_space=pltpu.VMEM)
 IN_SMEM = pl.BlockSpec(memory_space=pltpu.SMEM)
 ANYWHERE = pl.BlockSpec(memory_space=pl.ANY)
-
-
-def call(kernel, name, operands, in_specs, outs, out_specs, scratch=(), after=(), vmem=56, flops=0, **more):
+IN_HBM = pl.BlockSpec(memory_space=pltpu.HBM)
+
+
+def call(kernel, name, operands, in_specs, outs, out_specs, scratch=(), after=(), vmem=56, flops=0, after_spec=ANYWHERE, **more):
     given, late = len(operands), len(after)
 
     def body(*refs):
@@ -29,7 +31,7 @@
 
     return pl.pallas_call(
         body,
-        in_specs=[*in_specs, *[ANYWHERE] * late],
+        in_specs=[*in_specs, *[after_spec] * late],
         out_specs=out_specs,
         out_shape=outs,
         scratch_shapes=scratch,
@@ -203,7 +205,7 @@
     specs = [IN_SMEM, IN_VMEM, IN_VMEM]
     outs = [shape(width, width, dtype=BF16)] * 2
     scratch = [pltpu.VMEM((width, width), F32)] * 3
-    return call(polar_kernel, "polar", (at, mine, other), specs, outs, [IN_VMEM] * 2, scratch, after, 24, LONG)
+    return call(polar_kernel, "polar", (at, mine, other), specs, outs, [IN_VMEM] * 2, scratch, after, 24, LONG, IN_HBM)
 
 
 def times(rows, w_high, w_low):
@@ -211,40 +213,25 @@
     return product(high, w_high) + product(high, w_low) + product(low, w_high)
 
 
-def turn(arrays, w, after=(), spec=WHOLE):
-    width = w[0].shape[0]
-    half = width // 2
+def turn(arrays, w, wanted, after=(), spec=WHOLE):
+    half = w[0].shape[0] // 2
 
     def kernel(*refs):
-        (high_ref, low_ref), parts, outs = refs[:2], refs[2:-2], refs[-2:]
-        begin = 0
-        for b_ref in parts:
-            rows = pl.ds(begin, b_ref.shape[0])
-            for out_ref, at in zip(outs, (slice(0, half), slice(half, width)), strict=True):
-                out_ref[rows, :] = times(b_ref[...], high_ref[:, at], low_ref[:, at])
-            begin += b_ref.shape[0]
-
-    outs = [shape(sum(b.shape[0] for b in arrays), half)] * 2
-    return call(kernel, "turn", (*w, *arrays), [WHOLE] * 2 + [spec] * len(arrays), outs, [WHOLE] * 2, after=after, vmem=24)
-
-
-def take(b, start, count, parts=4):
-    rows = count // parts
-
-    def kernel(b_ref, out_ref, sem):
-        copies = [
-            pltpu.make_async_copy(
-                b_ref.at[pl.ds(start + p * rows, rows)], out_ref.at[pl.ds(p * rows, rows)], sem.at[p]
-            )
-            for p in range(parts)
-        ]
-        for copy in copies:
-            copy.start()
-        for copy in copies:
-            copy.wait()
-
-    scratch = [pltpu.SemaphoreType.DMA((parts,))]
-    return call(kernel, "take", (b,), [ANYWHERE], shape(count, b.shape[1]), IN_VMEM, scratch)
+        (high_ref, low_ref), parts, outs = refs[:2], refs[2 : 2 + len(arrays)], refs[2 + len(arrays) :]
+        for out_ref, (side, begin, end) in zip(outs, wanted):
+            columns = slice(side * half, (side + 1) * half)
+            w_high, w_low = high_ref[:, columns], low_ref[:, columns]
+            at = 0
+            for b_ref in parts:
+                size = b_ref.shape[0]
+                lower, upper = max(begin, at), min(end, at + size)
+                if lower < upper:
+                    out_ref[lower - begin : upper - begin, :] = times(b_ref[lower - at : upper - at, :], w_high, w_low)
+                at += size
+
+    outs = [shape(end - begin, half) for _, begin, end in wanted]
+    specs = [WHOLE] * 2 + [spec] * len(arrays)
+    return call(kernel, "turn", (*w, *arrays), specs, outs, [WHOLE] * len(outs), after=after, vmem=24)
 
 
 def own(at_end, b, start, count, w, after=()):
@@ -264,7 +251,7 @@
     return call(kernel, "own", (at_end, b, *w), specs, shape(count, half), IN_VMEM, scratch, after, 24)
 
 
-def join(choice, groups, rows, width, into=None, after=()):
+def join(choice, groups, rows, width, into=None, token=None, vmem=8):
     places = []
     for start, count, sources in groups:
         for s, source in enumerate(sources):
@@ -297,10 +284,10 @@
     more = {}
     if into is not None:
         more["input_output_aliases"] = {len(operands): 0}
-        operands += (into,)
-        specs.append(ANYWHERE)
+        operands += (into, token)
+        specs += [ANYWHERE, ANYWHERE]
     scratch = [pltpu.SemaphoreType.DMA((len(places),))]
-    return call(kernel, "join", operands, specs, shape(rows, width), ANYWHERE, scratch, after, 8, **more)
+    return call(kernel, "join", operands, specs, shape(rows, width), ANYWHERE, scratch, vmem=vmem, **more)
 
 
 def mark(after):
@@ -346,62 +333,62 @@
     def sent_early(k, rows_of_k):
         return lax.ppermute(rows_of_k, "pair", [(p, p ^ 1) for p in range(pairs) if is_early(p, groups[k][2])])
 
-    from_partner = {k: [] for k in early}
-    taken = [history[begin : begin + count] for begin, count in pieces[early[0]]]
-    from_partner[early[0]] = [sent_early(early[0], a) for a in taken]
-
-    later = [(k, piece) for k in early[1:] for piece in pieces[k]]
+    (e,) = early
+    taken = [history[begin : begin + count] for begin, count in pieces[e][:FIRST]]
+    from_partner = [sent_early(e, a) for a in taken]
+
     kept = [k for k in range(len(groups)) if groups[k][2] > 0]
-    at_once, then = [piece for _, piece in later], [groups[k][:2] for k in kept]
-    keep, give, *copies = gram(jnp.stack([core]), history, at_once, then, taken)
+    later = pieces[e][FIRST:]
+    keep, give, *copies = gram(jnp.stack([core]), history, later, [groups[k][:2] for k in kept], taken)
     kept = dict(zip(kept, copies[len(later) :]))
-    summed = add(keep, lax.ppermute(give, "tm", swap_cores), from_partner[early[0]][:1])
+    summed = add(keep, lax.ppermute(give, "tm", swap_cores), from_partner[:1])
     from_row = lax.ppermute(summed, "tm", swap_rows)
     second = jnp.stack([row_half])
     mine, part = add_and_cut(second, summed, from_row, ())
     other = lax.ppermute(mine, "tm", swap_cores)
     part = lax.ppermute(part, "pair", swap_pairs)
-    for (k, _), a in zip(later, copies):
-        from_partner[k].append(sent_early(k, a))
+    from_partner += [sent_early(e, a) for a in copies[: len(later)]]
 
     flag = (~even | first).astype(jnp.int32)
-    w = polar(jnp.stack([core, *ids(position), flag]), mine, other, width, (part, *from_partner[early[0]]))
-    late = {}
+    w = polar(jnp.stack([core, *ids(position), flag]), mine, other, width, (part, *from_partner[:FIRST]))
+    to_partner, onward = {}, {}
     for k, (_, _, threshold) in enumerate(groups):
-        if threshold > 0:
-            near, far = turn([kept[k]], w, spec=IN_VMEM)
-            to_partner = [(p, p ^ 1) for p in range(pairs) if not is_early(p, threshold)]
-            onward = [(p, p - 1) for p in range(2, pairs, 2) if not is_early(p, threshold)]
-            onward += [(p, p + 1) for p in range(1, pairs - 1, 2) if not is_early(p, threshold)]
-            late[k] = lax.ppermute(near, "pair", to_partner), lax.ppermute(far, "pair", onward), far
+        to_partner[k] = [(p, p ^ 1) for p in range(pairs) if not is_early(p, threshold)]
+        onward[k] = [(p, p - 1) for p in range(2, pairs, 2) if not is_early(p, threshold)]
+        onward[k] += [(p, p + 1) for p in range(1, pairs - 1, 2) if not is_early(p, threshold)]
+    late_near, late_far = {}, {}
+    for k in kept:
+        count = groups[k][1]
+        (a,) = turn([kept[k]], w, [(0, 0, count)], spec=IN_VMEM)
+        late_near[k] = a, lax.ppermute(a, "pair", to_partner[k])
+        cut = count // 32 * 16
+        both = turn([kept[k]], w, [(1, 0, cut), (1, cut, count)], [a], IN_VMEM)
+        late_far[k] = [(at, a, lax.ppermute(a, "pair", onward[k])) for at, a in zip((0, cut), both)]
 
     part_2 = lax.ppermute(part, "tm", swap_rows)
-    mine_q = merge(second, part, part_2, [late[k][2] for k in late])
+    mine_q = merge(second, part, part_2, [late_far[k][0][1] for k in kept])
     other_q = lax.ppermute(mine_q, "tm", swap_cores)
     flag_q = (even | (partner == 0)).astype(jnp.int32)
-    w_q = polar(jnp.stack([core, *ids(partner), flag_q]), mine_q, other_q, width, from_partner[early[1]])
+    w_q = polar(jnp.stack([core, *ids(partner), flag_q]), mine_q, other_q, width, from_partner[FIRST:])
     at_end = jnp.stack([first | last]).astype(jnp.int32)
-    near, passed = {}, {}
-    always = [k for k in early if groups[k][2] == 0]
-    after = ()
-    for k in early:
-        threshold = groups[k][2]
-        near[k], far = turn(from_partner[k], w_q, after)
-        onward = [(p ^ 1, p - 1) for p in range(2, pairs, 2) if is_early(p, threshold)]
-        onward += [(p ^ 1, p + 1) for p in range(1, pairs - 1, 2) if is_early(p, threshold)]
-        passed[k] = lax.ppermute(far, "pair", onward)
-        if k == early[0]:
-            alone = own(at_end, history, groups[always[0]][0], sum(groups[k][1] for k in always), w, (far,))
-            after = (alone,)
-
-    sources = {k: (near[k], passed[k], (alone, groups[k][0])) for k in early} | late
+    begin, count, threshold = groups[e]
+    near, far = turn(from_partner, w_q, [(0, 0, count), (1, 0, count)])
+    passes = [(p ^ 1, p - 1) for p in range(2, pairs, 2) if is_early(p, threshold)]
+    passes += [(p ^ 1, p + 1) for p in range(1, pairs - 1, 2) if is_early(p, threshold)]
+    passed = lax.ppermute(far, "pair", passes)
+    alone = own(at_end, history, begin, count, w, (far,))
+
     choice = jnp.stack([jnp.where(even, 1 + first, 0), jnp.where(even, 0, 1 + last)]).astype(jnp.int32)
-    near_late = {k: (sources[k][0], None, None) for k in late}
-    far_late = {k: (None, *sources[k][1:]) for k in late}
-    first_part, last_part = {k: sources[k] for k in early} | far_late, near_late
-    joined = join(choice, [(*groups[k][:2], first_part[k]) for k in first_part], rows, width)
-    last_groups = [(*groups[k][:2], last_part[k]) for k in last_part]
-    return join(choice, last_groups, rows, width, joined, (mark(joined),))
+    parts = [[(begin, count, (near, None, alone))], [(begin, count, (None, passed, None))], []]
+    for k in kept:
+        begin, count = groups[k][:2]
+        for at, a, from_far in late_far[k]:
+            parts[1].append((begin + at, a.shape[0], (None, from_far, a)))
+        parts[2].append((begin, count, (late_near[k][1], None, None)))
+    joined = join(choice, parts[0], rows, width)
+    for part in parts[1:]:
+        joined = join(choice, part, rows, width, joined, mark(joined), 56)
+    return joined
 
 
 def solution(mesh):

time: 106 us -> 105 us (level)
  waiting for transfers between devices: 35.4 us -> 34.2 us
    ppermute x5, waiting for transfers between devices: 20 us -> 17.3 us  [the longest x2 15.4 us: shards(): lax.ppermute(a, 'pair', onward[k])]
    ppermute x3, waiting for transfers between devices: 0.01 us -> 1.57 us  [sent_early(): lax.ppermute(rows_of_k, 'pair', [(p, p ^ 1) for p in range(pairs) if is_e...]
    unnamed x26 -> x32, local copies, waits for them, and re-layouts: 5.77 us -> 6.15 us
    pallas_call x13 -> x15, Pallas kernels: 38.8 us -> 38.8 us  [call(): pl.pallas_call(body, in_specs=[*in_specs, *[after_spec] * late], out_spec...]
  transfers between devices with their start and end apart: 13 -> 13, of which waited for: 5 -> 7; matrix products, arithmetic and copies ran while one was open for 2% -> 2% of each run, Pallas kernels for 35% -> 35%
where the time goes in v4:
time: 105 us; the launch traced here: 103 us
  Pallas kernels  38.8 us (37%)
  waiting for transfers between devices  34.2 us (33%)
  starting transfers between devices  19 us (18%)
  local copies, waits for them, and re-layouts  10 us (10%)
  between operations  1.14 us (1%)
    pallas_call x15, Pallas kernels, call(): pl.pallas_call(body, in_specs=[*in_specs, *[after_spec] * late], out_spec...  38.8 us
    ppermute x2, waiting for transfers between devices, shards(): lax.ppermute(a, 'pair', onward[k])  15.4 us
    ppermute x1, waiting for transfers between devices, shards(): from_row = lax.ppermute(summed, 'tm', swap_rows)  7.69 us
    ppermute x1, waiting for transfers between devices, shards(): part = lax.ppermute(part, 'pair', swap_pairs)  7.67 us
    ppermute x2, starting transfers between devices, shards(): lax.ppermute(a, 'pair', onward[k])  6.18 us
    unnamed x32, local copies, waits for them, and re-layouts  6.15 us
    slice x2, local copies, waits for them, and re-layouts, shards(): taken = [history[begin:begin + count] for begin, count in pieces[e][:FIRST]]  3.89 us
    ppermute x1, starting transfers between devices, shards(): passed = lax.ppermute(far, 'pair', passes)  3.19 us
  transfers between devices with their start and end apart: 13, of which 7 were waited for; matrix products, arithmetic and copies ran while one was open for 2% of the time, Pallas kernels for 35%

profile of v4, /device:TPU:9, one launch (start us, length us, event | category | flops | bytes accessed | tf_op | source)
XLA Modules:
  0.0 103.5 jit_solution(12398033172091320439)
XLA Ops:
  0.0 1.8 %slice.6.refs_2_ = f32[192,512]{1,0:T(8,128)} slice(f32[2048,512]{1,0:T(8,128)} %refs_1_.3), slice={[0:192], [0:512]} | slice | bytes 786432 | tf_op jit(solution)/shard_map/slice | solution.py:337
  3.0 2.1 %slice.7.refs_3_ = f32[384,512]{1,0:T(8,128)} slice(f32[2048,512]{1,0:T(8,128)} %refs_1_.3), slice={[192:576], [0:512]} | slice | bytes 1572864 | tf_op jit(solution)/shard_map/slice | solution.py:337
  5.1 6.8 %gram.1 = (f32[640,128]{1,0:T(8,128)}, f32[640,128]{1,0:T(8,128)}, f32[416,512]{1,0:T(8,128)}, f32[1056,512]{1,0:T(8,128)}) custom-call(s32[1]{0:T(128)} %bitcast.2.refs_0_, f32[2048,512]{1,0:T(8,128)} %refs_1_.3, f32[192,512]{1,0:T(8,128)} %slice.6.refs_2_, f32[384,512]{1,0:T(8,128)} %slice.7.refs_3_), custom_call_target="tpu_custom_call" | custom-call | flops 999999995904 | tf_op jit(solution)/shard_map/gram/pallas_call | solution.py:32
  15.4 1.3 %collective-permute-start.2 = (f32[640,128]{1,0:T(8,128)S(1)}, f32[640,128]{1,0:T(8,128)S(1)}, u32[]{:S(2)}, u32[]{:S(2)}) collective-permute-start(f32[640,128]{1,0:T(8,128)S(1)} %add.68.refs_1_), channel_id=1, source_target_pairs={{0,2},{1,3},{2,0},{3,1},{4,6},{5,7},{6,4},{7,5},{8,10},{9,11},{10,... | collective-permute-start | bytes 983048 | tf_op jit(solution)/shard_map/ppermute | solution.py:345
  16.7 7.7 %collective-permute-done.2.refs_2_ = f32[640,128]{1,0:T(8,128)S(1)} collective-permute-done((f32[640,128]{1,0:T(8,128)S(1)}, f32[640,128]{1,0:T(8,128)S(1)}, u32[]{:S(2)}, u32[]{:S(2)}) %collective-permute-start.2) | collective-permute-done | bytes 327712 | tf_op jit(solution)/shard_map/ppermute | solution.py:345
  24.5 1.3 %collective-permute-start.3 = (f32[640,128]{1,0:T(8,128)S(1)}, f32[640,128]{1,0:T(8,128)S(1)}, u32[]{:S(2)}, u32[]{:S(2)}) collective-permute-start(f32[640,128]{1,0:T(8,128)S(1)} %get-tuple-element.21.refs_1_), channel_id=1, source_target_pairs={{0,1},{1,0},{2,3},{3,2},{4,5},{5,4},{6,7},{7,6},{8,9},{9,8},{10,11... | collective-permute-start | bytes 983048 | tf_op jit(solution)/shard_map/ppermute | solution.py:348
  28.0 7.7 %collective-permute-done.4.refs_3_.refs_1_ = f32[320,128]{1,0:T(8,128)} collective-permute-done((f32[320,128]{1,0:T(8,128)S(1)}, f32[320,128]{1,0:T(8,128)}, u32[]{:S(2)}, u32[]{:S(2)}) %collective-permute-start.4) | collective-permute-done | bytes 163872 | tf_op jit(solution)/shard_map/ppermute | solution.py:349
  35.7 1.2 %collective-permute-start.7 = (f32[320,128]{1,0:T(8,128)}, f32[320,128]{1,0:T(8,128)}, u32[]{:S(2)}, u32[]{:S(2)}) collective-permute-start(f32[320,128]{1,0:T(8,128)} %collective-permute-done.4.refs_3_.refs_1_), channel_id=1, source_target_pairs={{0,2},{1,3},{2,0},{3,1},{4,6},{5,7},{6,4},{7,5},{8,10},{9,11},{10,... | collective-permute-start | bytes 491528 | tf_op jit(solution)/shard_map/ppermute | solution.py:368
  36.9 8.4 %polar.2 = (bf16[512,512]{1,0:T(8,128)(2,1)S(1)}, bf16[512,512]{1,0:T(8,128)(2,1)S(1)}) custom-call(s32[4]{0:T(128)S(1)} %pad_add_fusion.1.refs_0_, f32[640,128]{1,0:T(8,128)S(1)} %get-tuple-element.21.refs_1_, f32[640,128]{1,0:T(8,128)S(1)} %collective-permute-done.3.refs_2_, f32[320,128]{1,0:T(8,128)} %collective-permute-done.4.refs_3_.refs_1_, ...), custom_call_target="tpu_custom_call" | custom-call | flops 999999995904 | tf_op jit(solution)/shard_map/polar/pallas_call | solution.py:32
  45.4 2.0 %turn.3.refs_3_ = f32[1056,256]{1,0:T(8,128)} custom-call(bf16[512,512]{1,0:T(8,128)(2,1)S(1)} %get-tuple-element.23.refs_0_.refs_2_, bf16[512,512]{1,0:T(8,128)(2,1)S(1)} %get-tuple-element.24.refs_1_.refs_3_, f32[1056,512]{1,0:T(8,128)S(1)} %copy-done), custom_call_target="tpu_custom_call" | custom-call | tf_op jit(solution)/shard_map/turn/pallas_call | solution.py:32
  48.4 1.2 %merge.1.refs_1_ = f32[640,128]{1,0:T(8,128)S(1)} custom-call(s32[1]{0:T(128)} %bitcast.7.refs_0_, f32[320,128]{1,0:T(8,128)} %collective-permute-done.4.refs_3_.refs_1_, f32[320,128]{1,0:T(8,128)} %collective-permute-done.7.refs_2_, f32[528,256]{1,0:T(8,128)S(1)} %get-tuple-element.26.refs_3_), custom_call_target="tpu_custom_call" | custom-call | tf_op jit(solution)/shard_map/merge/pallas_call | solution.py:32
  50.4 1.6 %collective-permute-start.8 = (f32[640,128]{1,0:T(8,128)S(1)}, f32[640,128]{1,0:T(8,128)S(1)}, u32[]{:S(2)}, u32[]{:S(2)}) collective-permute-start(f32[640,128]{1,0:T(8,128)S(1)} %merge.1.refs_1_), channel_id=1, source_target_pairs={{0,1},{1,0},{2,3},{3,2},{4,5},{5,4},{6,7},{7,6},{8,9},{9,8},{10,11... | collective-permute-start | bytes 983048 | tf_op jit(solution)/shard_map/ppermute | solution.py:370
  52.4 1.6 %collective-permute-done.9.refs_3_.refs_4_ = f32[416,512]{1,0:T(8,128)} collective-permute-done((f32[416,512]{1,0:T(8,128)}, f32[416,512]{1,0:T(8,128)}, u32[]{:S(2)}, u32[]{:S(2)}) %collective-permute-start.9) | collective-permute-done | bytes 852000 | tf_op jit(solution)/shard_map/ppermute | solution.py:334
  54.0 8.2 %polar.3 = (bf16[512,512]{1,0:T(8,128)(2,1)S(1)}, bf16[512,512]{1,0:T(8,128)(2,1)S(1)}) custom-call(s32[4]{0:T(128)S(1)} %pad_add_fusion.2.refs_0_, f32[640,128]{1,0:T(8,128)S(1)} %merge.1.refs_1_, f32[640,128]{1,0:T(8,128)S(1)} %collective-permute-done.8.refs_2_, f32[416,512]{1,0:T(8,128)} %collective-permute-done.9.refs_3_.refs_4_), custom_call_target="tpu_custom_call" | custom-call | flops 999999995904 | tf_op jit(solution)/shard_map/polar/pallas_call | solution.py:32
  62.2 3.0 %turn.5 = (f32[992,256]{1,0:T(8,128)S(1)}, f32[992,256]{1,0:T(8,128)S(1)}) custom-call(bf16[512,512]{1,0:T(8,128)(2,1)S(1)} %get-tuple-element.28.refs_0_, bf16[512,512]{1,0:T(8,128)(2,1)S(1)} %get-tuple-element.29.refs_1_, f32[192,512]{1,0:T(8,128)} %collective-permute-done.1.refs_2_.refs_4_, f32[384,512]{1,0:T(8,128)S(1)} %copy-done.11, ...), custom_call_target="tpu_custom_call" | custom-call | tf_op jit(solution)/shard_map/turn/pallas_call | solution.py:32
  66.1 3.2 %collective-permute-start.10 = (f32[992,256]{1,0:T(8,128)S(1)}, f32[992,256]{1,0:T(8,128)}, u32[]{:S(2)}, u32[]{:S(2)}) collective-permute-start(f32[992,256]{1,0:T(8,128)S(1)} %get-tuple-element.30.refs_4_), channel_id=1, source_target_pairs={{12,4},{20,12},{28,20},{0,8},{8,16},{16,24},{13,5},{21,13},{29,21}... | collective-permute-start | bytes 3047432 | tf_op jit(solution)/shard_map/ppermute | solution.py:378
  69.4 1.9 %collective-permute-start.12 = (f32[528,256]{1,0:T(8,128)S(1)}, f32[528,256]{1,0:T(8,128)}, u32[]{:S(2)}, u32[]{:S(2)}) collective-permute-start(f32[528,256]{1,0:T(8,128)S(1)} %get-tuple-element.31.refs_5_), channel_id=1, source_target_pairs={{8,4},{16,12},{24,20},{4,8},{12,16},{20,24},{9,5},{17,13},{25,21},... | collective-permute-start | bytes 1622024 | tf_op jit(solution)/shard_map/ppermute | solution.py:366
  71.3 4.3 %collective-permute-start.11 = (f32[528,256]{1,0:T(8,128)S(1)}, f32[528,256]{1,0:T(8,128)}, u32[]{:S(2)}, u32[]{:S(2)}) collective-permute-start(f32[528,256]{1,0:T(8,128)S(1)} %copy-done.7), channel_id=1, source_target_pairs={{8,4},{16,12},{24,20},{4,8},{12,16},{20,24},{9,5},{17,13},{25,21},... | collective-permute-start | bytes 1622024 | tf_op jit(solution)/shard_map/ppermute | solution.py:366
  75.7 2.2 %copy-done.1 = f32[2048,512]{1,0:T(8,128)S(1)} copy-done((f32[2048,512]{1,0:T(8,128)S(1)}, f32[2048,512]{1,0:T(8,128)}, u32[]{:S(2)}) %copy-start.1) | copy-done | bytes 4194328
  79.1 1.5 %join.3.refs_0_.refs_6_ = f32[2048,512]{1,0:T(8,128)} custom-call(s32[2]{0:T(128)S(1)} %pad_add_fusion.refs_0_, f32[992,256]{1,0:T(8,128)S(1)} %copy-done.9, f32[992,256]{1,0:T(8,128)S(1)} %own.1.refs_2_), custom_call_target="tpu_custom_call" | custom-call | tf_op jit(solution)/shard_map/join/pallas_call | solution.py:32
  81.2 3.8 %collective-permute-done.12.refs_4_ = f32[528,256]{1,0:T(8,128)} collective-permute-done((f32[528,256]{1,0:T(8,128)S(1)}, f32[528,256]{1,0:T(8,128)}, u32[]{:S(2)}, u32[]{:S(2)}) %collective-permute-start.12) | collective-permute-done | bytes 540704 | tf_op jit(solution)/shard_map/ppermute | solution.py:366
  85.0 11.6 %collective-permute-done.11.refs_2_ = f32[528,256]{1,0:T(8,128)} collective-permute-done((f32[528,256]{1,0:T(8,128)S(1)}, f32[528,256]{1,0:T(8,128)}, u32[]{:S(2)}, u32[]{:S(2)}) %collective-permute-start.11) | collective-permute-done | bytes 540704 | tf_op jit(solution)/shard_map/ppermute | solution.py:366
  96.6 3.2 %join.4.refs_0_.refs_2_ = f32[2048,512]{1,0:T(8,128)} custom-call(s32[2]{0:T(128)} %copy-done.14, f32[992,256]{1,0:T(8,128)} %collective-permute-done.10.refs_1_, f32[528,256]{1,0:T(8,128)} %collective-permute-done.11.refs_2_, f32[528,256]{1,0:T(8,128)} %copy-done.6, f32[528,256]{1,0:T(8,128)} %collective-permute-done.12.refs_4_, ...), custom_call_target="tpu_custom_call", output_to_operand_aliasing={{}: (6, {})} | custom-call | tf_op jit(solution)/shard_map/join/pallas_call | solution.py:32
  101.1 2.2 %join.5 = f32[2048,512]{1,0:T(8,128)} custom-call(s32[2]{0:T(128)} %copy-done.14, f32[1056,256]{1,0:T(8,128)} %collective-permute-done.6.refs_1_, f32[2048,512]{1,0:T(8,128)} %join.4.refs_0_.refs_2_, f32[8,128]{1,0:T(8,128)} %mark.3.refs_3_), custom_call_target="tpu_custom_call", output_to_operand_aliasing={{}: (2, {})} | custom-call | tf_op jit(solution)/shard_map/join/pallas_call | solution.py:32
  (54 shorter events, 12.7 us)
Async XLA Ops:
  1.8 12.6 %collective-permute-start.1 = (f32[192,512]{1,0:T(8,128)}, f32[192,512]{1,0:T(8,128)}, u32[]{:S(2)}, u32[]{:S(2)}) collective-permute-start(f32[192,512]{1,0:T(8,128)} %slice.6.refs_2_), channel_id=1, source_target_pairs={{0,4},{4,0},{8,12},{12,8},{16,20},{20,16},{24,28},{28,24},{1,5},{5... | collective-permute-start | bytes 1179656 | tf_op jit(solution)/shard_map/ppermute | solution.py:334
  5.1 7.9 %copy-start.15 = (f32[384,512]{1,0:T(8,128)S(1)}, f32[384,512]{1,0:T(8,128)}, u32[]{:S(2)}) copy-start(f32[384,512]{1,0:T(8,128)} %slice.7.refs_3_) | copy-start | bytes 2359300
  11.9 2.5 %collective-permute-start = (f32[640,128]{1,0:T(8,128)}, f32[640,128]{1,0:T(8,128)S(1)}, u32[]{:S(2)}, u32[]{:S(2)}) collective-permute-start(f32[640,128]{1,0:T(8,128)} %get-tuple-element.20), channel_id=1, source_target_pairs={{0,1},{1,0},{2,3},{3,2},{4,5},{5,4},{6,7},{7,6},{8,9},{9,8},{10,11... | collective-permute-start | bytes 983048 | tf_op jit(solution)/shard_map/ppermute | solution.py:344
  13.0 24.0 %collective-permute-start.5 = (f32[384,512]{1,0:T(8,128)S(1)}, f32[384,512]{1,0:T(8,128)S(1)}, u32[]{:S(2)}, u32[]{:S(2)}) collective-permute-start(f32[384,512]{1,0:T(8,128)S(1)} %copy-done.15), channel_id=1, source_target_pairs={{0,4},{4,0},{8,12},{12,8},{16,20},{20,16},{24,28},{28,24},{1,5},{5... | collective-permute-start | bytes 2359304 | tf_op jit(solution)/shard_map/ppermute | solution.py:334
  15.4 9.0 %collective-permute-start.2 = (f32[640,128]{1,0:T(8,128)S(1)}, f32[640,128]{1,0:T(8,128)S(1)}, u32[]{:S(2)}, u32[]{:S(2)}) collective-permute-start(f32[640,128]{1,0:T(8,128)S(1)} %add.68.refs_1_), channel_id=1, source_target_pairs={{0,2},{1,3},{2,0},{3,1},{4,6},{5,7},{6,4},{7,5},{8,10},{9,11},{10,... | collective-permute-start | bytes 983048 | tf_op jit(solution)/shard_map/ppermute | solution.py:345
  24.5 12.4 %collective-permute-start.3 = (f32[640,128]{1,0:T(8,128)S(1)}, f32[640,128]{1,0:T(8,128)S(1)}, u32[]{:S(2)}, u32[]{:S(2)}) collective-permute-start(f32[640,128]{1,0:T(8,128)S(1)} %get-tuple-element.21.refs_1_), channel_id=1, source_target_pairs={{0,1},{1,0},{2,3},{3,2},{4,5},{5,4},{6,7},{7,6},{8,9},{9,8},{10,11... | collective-permute-start | bytes 983048 | tf_op jit(solution)/shard_map/ppermute | solution.py:348
  25.8 9.9 %collective-permute-start.4 = (f32[320,128]{1,0:T(8,128)S(1)}, f32[320,128]{1,0:T(8,128)}, u32[]{:S(2)}, u32[]{:S(2)}) collective-permute-start(f32[320,128]{1,0:T(8,128)S(1)} %get-tuple-element.22), channel_id=1, source_target_pairs={{0,4},{4,0},{8,12},{12,8},{16,20},{20,16},{24,28},{28,24},{1,5},{5... | collective-permute-start | bytes 491528 | tf_op jit(solution)/shard_map/ppermute | solution.py:349
  26.0 27.9 %collective-permute-start.9 = (f32[416,512]{1,0:T(8,128)}, f32[416,512]{1,0:T(8,128)}, u32[]{:S(2)}, u32[]{:S(2)}) collective-permute-start(f32[416,512]{1,0:T(8,128)} %get-tuple-element.27), channel_id=1, source_target_pairs={{0,4},{4,0},{8,12},{12,8},{16,20},{20,16},{24,28},{28,24},{1,5},{5... | collective-permute-start | bytes 2555912 | tf_op jit(solution)/shard_map/ppermute | solution.py:334
  35.7 12.7 %collective-permute-start.7 = (f32[320,128]{1,0:T(8,128)}, f32[320,128]{1,0:T(8,128)}, u32[]{:S(2)}, u32[]{:S(2)}) collective-permute-start(f32[320,128]{1,0:T(8,128)} %collective-permute-done.4.refs_3_.refs_1_), channel_id=1, source_target_pairs={{0,2},{1,3},{2,0},{3,1},{4,6},{5,7},{6,4},{7,5},{8,10},{9,11},{10,... | collective-permute-start | bytes 491528 | tf_op jit(solution)/shard_map/ppermute | solution.py:368
  36.9 8.4 %copy-start.10 = (f32[384,512]{1,0:T(8,128)}, f32[384,512]{1,0:T(8,128)S(1)}, u32[]{:S(2)}) copy-start(f32[384,512]{1,0:T(8,128)S(1)} %collective-permute-done.5.refs_5_.refs_3_) | copy-start | bytes 2359300
  36.9 8.4 %copy-start = (f32[1056,512]{1,0:T(8,128)S(1)}, f32[1056,512]{1,0:T(8,128)}, u32[]{:S(2)}) copy-start(f32[1056,512]{1,0:T(8,128)} %get-tuple-element.25.refs_2_) | copy-start | bytes 6488068
  45.3 3.0 %copy-start.2 = (bf16[512,512]{1,0:T(8,128)(2,1)}, bf16[512,512]{1,0:T(8,128)(2,1)S(1)}, u32[]{:S(2)}) copy-start(bf16[512,512]{1,0:T(8,128)(2,1)S(1)} %get-tuple-element.23.refs_0_.refs_2_) | copy-start | bytes 1572868
  45.3 3.0 %copy-start.4 = (bf16[512,512]{1,0:T(8,128)(2,1)}, bf16[512,512]{1,0:T(8,128)(2,1)S(1)}, u32[]{:S(2)}) copy-start(bf16[512,512]{1,0:T(8,128)(2,1)S(1)} %get-tuple-element.24.refs_1_.refs_3_) | copy-start | bytes 1572868
  48.4 21.0 %copy-start.12 = (f32[528,256]{1,0:T(8,128)}, f32[528,256]{1,0:T(8,128)S(1)}, u32[]{:S(2)}) copy-start(f32[528,256]{1,0:T(8,128)S(1)} %get-tuple-element.31.refs_5_) | copy-start | bytes 1622020
  50.4 3.5 %collective-permute-start.8 = (f32[640,128]{1,0:T(8,128)S(1)}, f32[640,128]{1,0:T(8,128)S(1)}, u32[]{:S(2)}, u32[]{:S(2)}) collective-permute-start(f32[640,128]{1,0:T(8,128)S(1)} %merge.1.refs_1_), channel_id=1, source_target_pairs={{0,1},{1,0},{2,3},{3,2},{4,5},{5,4},{6,7},{7,6},{8,9},{9,8},{10,11... | collective-permute-start | bytes 983048 | tf_op jit(solution)/shard_map/ppermute | solution.py:370
  52.1 49.0 %collective-permute-start.6 = (f32[1056,256]{1,0:T(8,128)}, f32[1056,256]{1,0:T(8,128)}, u32[]{:S(2)}, u32[]{:S(2)}) collective-permute-start(f32[1056,256]{1,0:T(8,128)} %turn.3.refs_3_), channel_id=1, source_target_pairs={{0,4},{4,0},{8,12},{12,8},{16,20},{20,16},{24,28},{28,24},{1,5},{5... | collective-permute-start | bytes 3244040 | tf_op jit(solution)/shard_map/ppermute | solution.py:363
  53.9 8.2 %copy-start.11 = (f32[384,512]{1,0:T(8,128)S(1)}, f32[384,512]{1,0:T(8,128)}, u32[]{:S(2)}) copy-start(f32[384,512]{1,0:T(8,128)} %copy-done.10) | copy-start | bytes 2359300
  53.9 17.3 %copy-start.7 = (f32[528,256]{1,0:T(8,128)S(1)}, f32[528,256]{1,0:T(8,128)}, u32[]{:S(2)}) copy-start(f32[528,256]{1,0:T(8,128)} %copy-done.6) | copy-start | bytes 1622020
  53.9 21.7 %copy-start.3 = (bf16[512,512]{1,0:T(8,128)(2,1)S(1)}, bf16[512,512]{1,0:T(8,128)(2,1)}, u32[]{:S(2)}) copy-start(bf16[512,512]{1,0:T(8,128)(2,1)} %copy-done.2) | copy-start | bytes 1572868
  54.0 21.7 %copy-start.5 = (bf16[512,512]{1,0:T(8,128)(2,1)S(1)}, bf16[512,512]{1,0:T(8,128)(2,1)}, u32[]{:S(2)}) copy-start(bf16[512,512]{1,0:T(8,128)(2,1)} %copy-done.4) | copy-start | bytes 1572868
  66.1 30.4 %collective-permute-start.10 = (f32[992,256]{1,0:T(8,128)S(1)}, f32[992,256]{1,0:T(8,128)}, u32[]{:S(2)}, u32[]{:S(2)}) collective-permute-start(f32[992,256]{1,0:T(8,128)S(1)} %get-tuple-element.30.refs_4_), channel_id=1, source_target_pairs={{12,4},{20,12},{28,20},{0,8},{8,16},{16,24},{13,5},{21,13},{29,21}... | collective-permute-start | bytes 3047432 | tf_op jit(solution)/shard_map/ppermute | solution.py:378
  69.4 15.6 %collective-permute-start.12 = (f32[528,256]{1,0:T(8,128)S(1)}, f32[528,256]{1,0:T(8,128)}, u32[]{:S(2)}, u32[]{:S(2)}) collective-permute-start(f32[528,256]{1,0:T(8,128)S(1)} %get-tuple-element.31.refs_5_), channel_id=1, source_target_pairs={{8,4},{16,12},{24,20},{4,8},{12,16},{20,24},{9,5},{17,13},{25,21},... | collective-permute-start | bytes 1622024 | tf_op jit(solution)/shard_map/ppermute | solution.py:366
  71.3 25.3 %collective-permute-start.11 = (f32[528,256]{1,0:T(8,128)S(1)}, f32[528,256]{1,0:T(8,128)}, u32[]{:S(2)}, u32[]{:S(2)}) collective-permute-start(f32[528,256]{1,0:T(8,128)S(1)} %copy-done.7), channel_id=1, source_target_pairs={{8,4},{16,12},{24,20},{4,8},{12,16},{20,24},{9,5},{17,13},{25,21},... | collective-permute-start | bytes 1622024 | tf_op jit(solution)/shard_map/ppermute | solution.py:366
  75.7 4.9 %copy-start.14 = (s32[2]{0:T(128)}, s32[2]{0:T(128)S(1)}, u32[]{:S(2)}) copy-start(s32[2]{0:T(128)S(1)} %pad_add_fusion.refs_0_) | copy-start | bytes 28
  (5 other events, 6.1 us)

commit v5 on v4

--- a/solution.py
+++ b/solution.py
@@ -12,7 +12,7 @@
 epsilon = 1e-06
 
 PLAN = ((0, (6, 12, 13)), (4, (33,)))
-FIRST = 2
+FIRST, LAST = 2, 6
 
 MIB = 1 << 20
 LONG = 10**12
@@ -359,11 +359,12 @@
     late_near, late_far = {}, {}
     for k in kept:
         count = groups[k][1]
-        (a,) = turn([kept[k]], w, [(0, 0, count)], spec=IN_VMEM)
-        late_near[k] = a, lax.ppermute(a, "pair", to_partner[k])
+        cut = count - rows * LAST // 64
+        two = turn([kept[k]], w, [(0, 0, cut), (0, cut, count)], spec=IN_VMEM)
+        late_near[k] = [(at, a.shape[0], lax.ppermute(a, "pair", to_partner[k])) for at, a in zip((0, cut), two)]
         cut = count // 32 * 16
-        both = turn([kept[k]], w, [(1, 0, cut), (1, cut, count)], [a], IN_VMEM)
-        late_far[k] = [(at, a, lax.ppermute(a, "pair", onward[k])) for at, a in zip((0, cut), both)]
+        two = turn([kept[k]], w, [(1, 0, cut), (1, cut, count)], two[:1], IN_VMEM)
+        late_far[k] = [(at, a, lax.ppermute(a, "pair", onward[k])) for at, a in zip((0, cut), two)]
 
     part_2 = lax.ppermute(part, "tm", swap_rows)
     mine_q = merge(second, part, part_2, [late_far[k][0][1] for k in kept])
@@ -372,19 +373,23 @@
     w_q = polar(jnp.stack([core, *ids(partner), flag_q]), mine_q, other_q, width, from_partner[FIRST:])
     at_end = jnp.stack([first | last]).astype(jnp.int32)
     begin, count, threshold = groups[e]
-    near, far = turn(from_partner, w_q, [(0, 0, count), (1, 0, count)])
+    cut = sum(a.shape[0] for a in from_partner[:FIRST])
+    near, *far = turn(from_partner, w_q, [(0, 0, count), (1, 0, cut), (1, cut, count)])
     passes = [(p ^ 1, p - 1) for p in range(2, pairs, 2) if is_early(p, threshold)]
     passes += [(p ^ 1, p + 1) for p in range(1, pairs - 1, 2) if is_early(p, threshold)]
-    passed = lax.ppermute(far, "pair", passes)
-    alone = own(at_end, history, begin, count, w, (far,))
+    passed = [(at, a.shape[0], lax.ppermute(a, "pair", passes)) for at, a in zip((0, cut), far)]
+    alone = own(at_end, history, begin, count, w, far[:1])
 
     choice = jnp.stack([jnp.where(even, 1 + first, 0), jnp.where(even, 0, 1 + last)]).astype(jnp.int32)
-    parts = [[(begin, count, (near, None, alone))], [(begin, count, (None, passed, None))], []]
+    parts = [[(begin, count, (near, None, alone))], [], [], []]
+    for at, size, a in passed:
+        parts[1].append((begin + at, size, (None, a, None)))
     for k in kept:
         begin, count = groups[k][:2]
         for at, a, from_far in late_far[k]:
             parts[1].append((begin + at, a.shape[0], (None, from_far, a)))
-        parts[2].append((begin, count, (late_near[k][1], None, None)))
+        for part, (at, size, a) in zip(parts[2:], late_near[k]):
+            part.append((begin + at, size, (a, None, None)))
     joined = join(choice, parts[0], rows, width)
     for part in parts[1:]:
         joined = join(choice, part, rows, width, joined, mark(joined), 56)

time: 105 us -> 104 us (level)
  waiting for transfers between devices: 34.2 us -> 29.4 us
  Pallas kernels: 38.8 us -> 42.4 us
  starting transfers between devices: 19 us -> 22.4 us
  local copies, waits for them, and re-layouts: 10 us -> 7.91 us
    ppermute x2, waiting for transfers between devices: 15.4 us -> 4.96 us  [shards(): lax.ppermute(a, 'pair', onward[k])]
    ppermute x2 -> x4, waiting for transfers between devices: 0.73 us -> 7.89 us  [the longest x2 6.29 us: shards(): lax.ppermute(a, 'pair', passes)]
    ppermute x2 -> x4, starting transfers between devices: 3.45 us -> 8.06 us  [the longest x2 6.53 us: shards(): lax.ppermute(a, 'pair', passes)]
    pallas_call x15 -> x17, Pallas kernels: 38.8 us -> 42.4 us  [call(): pl.pallas_call(body, in_specs=[*in_specs, *[after_spec] * late], out_spec...]
    unnamed x32 -> x26, local copies, waits for them, and re-layouts: 6.15 us -> 4.02 us
    ppermute x3, waiting for transfers between devices: 1.57 us -> 0.01 us  [sent_early(): lax.ppermute(rows_of_k, 'pair', [(p, p ^ 1) for p in range(pairs) if is_e...]
    ppermute x2, starting transfers between devices: 6.18 us -> 4.91 us  [shards(): lax.ppermute(a, 'pair', onward[k])]
  transfers between devices with their start and end apart: 13 -> 15, of which waited for: 7 -> 7; matrix products, arithmetic and copies ran while one was open for 2% -> 2% of each run, Pallas kernels for 35% -> 39%
where the time goes in v5:
time: 104 us; the launch traced here: 103 us
  Pallas kernels  42.4 us (41%)
  waiting for transfers between devices  29.4 us (28%)
  starting transfers between devices  22.4 us (22%)
  local copies, waits for them, and re-layouts  7.91 us (8%)
  between operations  1.14 us (1%)
    pallas_call x17, Pallas kernels, call(): pl.pallas_call(body, in_specs=[*in_specs, *[after_spec] * late], out_spec...  42.4 us
    ppermute x1, waiting for transfers between devices, shards(): from_row = lax.ppermute(summed, 'tm', swap_rows)  7.69 us
    ppermute x1, waiting for transfers between devices, shards(): part = lax.ppermute(part, 'pair', swap_pairs)  7.67 us
    ppermute x2, starting transfers between devices, shards(): lax.ppermute(a, 'pair', passes)  6.53 us
    ppermute x2, waiting for transfers between devices, shards(): lax.ppermute(a, 'pair', passes)  6.29 us
    ppermute x2, waiting for transfers between devices, shards(): lax.ppermute(a, 'pair', onward[k])  4.96 us
    ppermute x2, starting transfers between devices, shards(): lax.ppermute(a, 'pair', onward[k])  4.91 us
    unnamed x26, local copies, waits for them, and re-layouts  4.02 us
  transfers between devices with their start and end apart: 15, of which 7 were waited for; matrix products, arithmetic and copies ran while one was open for 2% of the time, Pallas kernels for 39%

profile of v5, /device:TPU:9, one launch (start us, length us, event | category | flops | bytes accessed | tf_op | source)
XLA Modules:
  0.0 103.4 jit_solution(4369307781687518686)
XLA Ops:
  0.0 1.8 %slice.6.refs_2_ = f32[192,512]{1,0:T(8,128)} slice(f32[2048,512]{1,0:T(8,128)} %refs_1_.3), slice={[0:192], [0:512]} | slice | bytes 786432 | tf_op jit(solution)/shard_map/slice | solution.py:337
  3.0 2.1 %slice.7.refs_3_ = f32[384,512]{1,0:T(8,128)} slice(f32[2048,512]{1,0:T(8,128)} %refs_1_.3), slice={[192:576], [0:512]} | slice | bytes 1572864 | tf_op jit(solution)/shard_map/slice | solution.py:337
  5.1 6.8 %gram.1 = (f32[640,128]{1,0:T(8,128)}, f32[640,128]{1,0:T(8,128)}, f32[416,512]{1,0:T(8,128)}, f32[1056,512]{1,0:T(8,128)}) custom-call(s32[1]{0:T(128)} %bitcast.2.refs_0_, f32[2048,512]{1,0:T(8,128)} %refs_1_.3, f32[192,512]{1,0:T(8,128)} %slice.6.refs_2_, f32[384,512]{1,0:T(8,128)} %slice.7.refs_3_), custom_call_target="tpu_custom_call" | custom-call | flops 999999995904 | tf_op jit(solution)/shard_map/gram/pallas_call | solution.py:32
  15.4 1.3 %collective-permute-start.2 = (f32[640,128]{1,0:T(8,128)S(1)}, f32[640,128]{1,0:T(8,128)S(1)}, u32[]{:S(2)}, u32[]{:S(2)}) collective-permute-start(f32[640,128]{1,0:T(8,128)S(1)} %add.68.refs_1_), channel_id=1, source_target_pairs={{0,2},{1,3},{2,0},{3,1},{4,6},{5,7},{6,4},{7,5},{8,10},{9,11},{10,... | collective-permute-start | bytes 983048 | tf_op jit(solution)/shard_map/ppermute | solution.py:345
  16.7 7.7 %collective-permute-done.2.refs_2_ = f32[640,128]{1,0:T(8,128)S(1)} collective-permute-done((f32[640,128]{1,0:T(8,128)S(1)}, f32[640,128]{1,0:T(8,128)S(1)}, u32[]{:S(2)}, u32[]{:S(2)}) %collective-permute-start.2) | collective-permute-done | bytes 327712 | tf_op jit(solution)/shard_map/ppermute | solution.py:345
  28.0 7.7 %collective-permute-done.4.refs_3_.refs_1_ = f32[320,128]{1,0:T(8,128)} collective-permute-done((f32[320,128]{1,0:T(8,128)S(1)}, f32[320,128]{1,0:T(8,128)}, u32[]{:S(2)}, u32[]{:S(2)}) %collective-permute-start.4) | collective-permute-done | bytes 163872 | tf_op jit(solution)/shard_map/ppermute | solution.py:349
  36.9 8.4 %polar.2 = (bf16[512,512]{1,0:T(8,128)(2,1)S(1)}, bf16[512,512]{1,0:T(8,128)(2,1)S(1)}) custom-call(s32[4]{0:T(128)S(1)} %pad_add_fusion.1.refs_0_, f32[640,128]{1,0:T(8,128)S(1)} %get-tuple-element.24.refs_1_, f32[640,128]{1,0:T(8,128)S(1)} %collective-permute-done.3.refs_2_, f32[320,128]{1,0:T(8,128)} %collective-permute-done.4.refs_3_.refs_1_, ...), custom_call_target="tpu_custom_call" | custom-call | flops 999999995904 | tf_op jit(solution)/shard_map/polar/pallas_call | solution.py:32
  45.4 1.9 %turn.3 = (f32[864,256]{1,0:T(8,128)}, f32[192,256]{1,0:T(8,128)S(1)}) custom-call(bf16[512,512]{1,0:T(8,128)(2,1)S(1)} %get-tuple-element.26.refs_0_.refs_2_, bf16[512,512]{1,0:T(8,128)(2,1)S(1)} %get-tuple-element.27.refs_1_.refs_3_, f32[1056,512]{1,0:T(8,128)S(1)} %copy-done), custom_call_target="tpu_custom_call" | custom-call | tf_op jit(solution)/shard_map/turn/pallas_call | solution.py:32
  47.3 1.8 %turn.4 = (f32[528,256]{1,0:T(8,128)S(1)}, f32[528,256]{1,0:T(8,128)}) custom-call(bf16[512,512]{1,0:T(8,128)(2,1)S(1)} %get-tuple-element.26.refs_0_.refs_2_, bf16[512,512]{1,0:T(8,128)(2,1)S(1)} %get-tuple-element.27.refs_1_.refs_3_, f32[1056,512]{1,0:T(8,128)S(1)} %copy-done, f32[864,256]{1,0:T(8,128)} %get-tuple-element.30.refs_3_), custom_call_target="tpu_custom_call" | custom-call | tf_op jit(solution)/shard_map/turn/pallas_call | solution.py:32
  51.0 1.6 %collective-permute-start.9 = (f32[640,128]{1,0:T(8,128)S(1)}, f32[640,128]{1,0:T(8,128)S(1)}, u32[]{:S(2)}, u32[]{:S(2)}) collective-permute-start(f32[640,128]{1,0:T(8,128)S(1)} %merge.1.refs_1_), channel_id=1, source_target_pairs={{0,1},{1,0},{2,3},{3,2},{4,5},{5,4},{6,7},{7,6},{8,9},{9,8},{10,11... | collective-permute-start | bytes 983048 | tf_op jit(solution)/shard_map/ppermute | solution.py:371
  52.9 3.0 %collective-permute-start.14 = (f32[528,256]{1,0:T(8,128)}, f32[528,256]{1,0:T(8,128)}, u32[]{:S(2)}, u32[]{:S(2)}) collective-permute-start(f32[528,256]{1,0:T(8,128)} %get-tuple-element.37.refs_6_), channel_id=1, source_target_pairs={{8,4},{16,12},{24,20},{4,8},{12,16},{20,24},{9,5},{17,13},{25,21},... | collective-permute-start | bytes 1622024 | tf_op jit(solution)/shard_map/ppermute | solution.py:367
  56.0 8.2 %polar.3 = (bf16[512,512]{1,0:T(8,128)(2,1)S(1)}, bf16[512,512]{1,0:T(8,128)(2,1)S(1)}) custom-call(s32[4]{0:T(128)S(1)} %pad_add_fusion.2.refs_0_, f32[640,128]{1,0:T(8,128)S(1)} %merge.1.refs_1_, f32[640,128]{1,0:T(8,128)S(1)} %collective-permute-done.9.refs_2_, f32[416,512]{1,0:T(8,128)} %collective-permute-done.10.refs_3_.refs_4_), custom_call_target="tpu_custom_call" | custom-call | flops 999999995904 | tf_op jit(solution)/shard_map/polar/pallas_call | solution.py:32
  64.2 3.9 %turn.5 = (f32[992,256]{1,0:T(8,128)S(1)}, f32[576,256]{1,0:T(8,128)S(1)}, f32[416,256]{1,0:T(8,128)}) custom-call(bf16[512,512]{1,0:T(8,128)(2,1)S(1)} %get-tuple-element.33.refs_0_, bf16[512,512]{1,0:T(8,128)(2,1)S(1)} %get-tuple-element.34.refs_1_, f32[192,512]{1,0:T(8,128)} %collective-permute-done.1.refs_2_.refs_4_, f32[384,512]{1,0:T(8,128)S(1)} %copy-done.9, ...), custom_call_target="tpu_custom_call" | custom-call | tf_op jit(solution)/shard_map/turn/pallas_call | solution.py:32
  68.1 3.2 %collective-permute-start.11 = (f32[576,256]{1,0:T(8,128)S(1)}, f32[576,256]{1,0:T(8,128)}, u32[]{:S(2)}, u32[]{:S(2)}) collective-permute-start(f32[576,256]{1,0:T(8,128)S(1)} %get-tuple-element.35.refs_4_), channel_id=1, source_target_pairs={{12,4},{20,12},{28,20},{0,8},{8,16},{16,24},{13,5},{21,13},{29,21}... | collective-permute-start | bytes 1769480 | tf_op jit(solution)/shard_map/ppermute | solution.py:380
  71.3 1.9 %collective-permute-start.13 = (f32[528,256]{1,0:T(8,128)S(1)}, f32[528,256]{1,0:T(8,128)}, u32[]{:S(2)}, u32[]{:S(2)}) collective-permute-start(f32[528,256]{1,0:T(8,128)S(1)} %copy-done.7), channel_id=1, source_target_pairs={{8,4},{16,12},{24,20},{4,8},{12,16},{20,24},{9,5},{17,13},{25,21},... | collective-permute-start | bytes 1622024 | tf_op jit(solution)/shard_map/ppermute | solution.py:367
  73.2 3.3 %collective-permute-start.12 = (f32[416,256]{1,0:T(8,128)}, f32[416,256]{1,0:T(8,128)}, u32[]{:S(2)}, u32[]{:S(2)}) collective-permute-start(f32[416,256]{1,0:T(8,128)} %get-tuple-element.36), channel_id=1, source_target_pairs={{12,4},{20,12},{28,20},{0,8},{8,16},{16,24},{13,5},{21,13},{29,21}... | collective-permute-start | bytes 1277960 | tf_op jit(solution)/shard_map/ppermute | solution.py:380
  78.0 2.2 %copy-done.1 = f32[2048,512]{1,0:T(8,128)S(1)} copy-done((f32[2048,512]{1,0:T(8,128)S(1)}, f32[2048,512]{1,0:T(8,128)}, u32[]{:S(2)}) %copy-start.1) | copy-done | bytes 4194328
  80.2 1.5 %join.4.refs_0_.refs_7_ = f32[2048,512]{1,0:T(8,128)} custom-call(s32[2]{0:T(128)S(1)} %pad_add_fusion.refs_0_, f32[992,256]{1,0:T(8,128)S(1)} %get-tuple-element.38.refs_1_, f32[992,256]{1,0:T(8,128)S(1)} %own.1.refs_2_), custom_call_target="tpu_custom_call" | custom-call | tf_op jit(solution)/shard_map/join/pallas_call | solution.py:32
  82.3 5.0 %collective-permute-done.13.refs_3_ = f32[528,256]{1,0:T(8,128)} collective-permute-done((f32[528,256]{1,0:T(8,128)S(1)}, f32[528,256]{1,0:T(8,128)}, u32[]{:S(2)}, u32[]{:S(2)}) %collective-permute-start.13) | collective-permute-done | bytes 540704 | tf_op jit(solution)/shard_map/ppermute | solution.py:367
  87.2 6.3 %collective-permute-done.12.refs_2_ = f32[416,256]{1,0:T(8,128)} collective-permute-done((f32[416,256]{1,0:T(8,128)}, f32[416,256]{1,0:T(8,128)}, u32[]{:S(2)}, u32[]{:S(2)}) %collective-permute-start.12) | collective-permute-done | bytes 426016 | tf_op jit(solution)/shard_map/ppermute | solution.py:380
  93.5 3.2 %join.5.refs_0_.refs_2_ = f32[2048,512]{1,0:T(8,128)} custom-call(s32[2]{0:T(128)} %copy-done.11, f32[576,256]{1,0:T(8,128)} %collective-permute-done.11.refs_1_, f32[416,256]{1,0:T(8,128)} %collective-permute-done.12.refs_2_, f32[528,256]{1,0:T(8,128)} %collective-permute-done.13.refs_3_, f32[528,256]{1,0:T(8,128)} %copy-done.6, ...), custom_call_target="tpu_custom_call", output_to_operand_aliasing={{}: (7, {})} | custom-call | tf_op jit(solution)/shard_map/join/pallas_call | solution.py:32
  97.4 2.1 %join.6.refs_0_.refs_2_ = f32[2048,512]{1,0:T(8,128)} custom-call(s32[2]{0:T(128)} %copy-done.11, f32[864,256]{1,0:T(8,128)} %collective-permute-done.7.refs_1_, f32[2048,512]{1,0:T(8,128)} %join.5.refs_0_.refs_2_, f32[8,128]{1,0:T(8,128)} %mark.4.refs_3_), custom_call_target="tpu_custom_call", output_to_operand_aliasing={{}: (2, {})} | custom-call | tf_op jit(solution)/shard_map/join/pallas_call | solution.py:32
  100.1 1.5 %collective-permute-done.6.refs_1_ = f32[192,256]{1,0:T(8,128)} collective-permute-done((f32[192,256]{1,0:T(8,128)S(1)}, f32[192,256]{1,0:T(8,128)}, u32[]{:S(2)}, u32[]{:S(2)}) %collective-permute-start.6) | collective-permute-done | bytes 196640 | tf_op jit(solution)/shard_map/ppermute | solution.py:364
  101.6 1.6 %join.7 = f32[2048,512]{1,0:T(8,128)} custom-call(s32[2]{0:T(128)} %copy-done.11, f32[192,256]{1,0:T(8,128)} %collective-permute-done.6.refs_1_, f32[2048,512]{1,0:T(8,128)} %join.6.refs_0_.refs_2_, f32[8,128]{1,0:T(8,128)} %mark.5.refs_3_), custom_call_target="tpu_custom_call", output_to_operand_aliasing={{}: (2, {})} | custom-call | tf_op jit(solution)/shard_map/join/pallas_call | solution.py:32
  (54 shorter events, 14.3 us)
Async XLA Ops:
  1.8 12.6 %collective-permute-start.1 = (f32[192,512]{1,0:T(8,128)}, f32[192,512]{1,0:T(8,128)}, u32[]{:S(2)}, u32[]{:S(2)}) collective-permute-start(f32[192,512]{1,0:T(8,128)} %slice.6.refs_2_), channel_id=1, source_target_pairs={{0,4},{4,0},{8,12},{12,8},{16,20},{20,16},{24,28},{28,24},{1,5},{5... | collective-permute-start | bytes 1179656 | tf_op jit(solution)/shard_map/ppermute | solution.py:334
  5.1 7.9 %copy-start.12 = (f32[384,512]{1,0:T(8,128)S(1)}, f32[384,512]{1,0:T(8,128)}, u32[]{:S(2)}) copy-start(f32[384,512]{1,0:T(8,128)} %slice.7.refs_3_) | copy-start | bytes 2359300
  11.9 2.5 %collective-permute-start = (f32[640,128]{1,0:T(8,128)}, f32[640,128]{1,0:T(8,128)S(1)}, u32[]{:S(2)}, u32[]{:S(2)}) collective-permute-start(f32[640,128]{1,0:T(8,128)} %get-tuple-element.23), channel_id=1, source_target_pairs={{0,1},{1,0},{2,3},{3,2},{4,5},{5,4},{6,7},{7,6},{8,9},{9,8},{10,11... | collective-permute-start | bytes 983048 | tf_op jit(solution)/shard_map/ppermute | solution.py:344
  13.0 24.0 %collective-permute-start.5 = (f32[384,512]{1,0:T(8,128)S(1)}, f32[384,512]{1,0:T(8,128)S(1)}, u32[]{:S(2)}, u32[]{:S(2)}) collective-permute-start(f32[384,512]{1,0:T(8,128)S(1)} %copy-done.12), channel_id=1, source_target_pairs={{0,4},{4,0},{8,12},{12,8},{16,20},{20,16},{24,28},{28,24},{1,5},{5... | collective-permute-start | bytes 2359304 | tf_op jit(solution)/shard_map/ppermute | solution.py:334
  15.4 9.0 %collective-permute-start.2 = (f32[640,128]{1,0:T(8,128)S(1)}, f32[640,128]{1,0:T(8,128)S(1)}, u32[]{:S(2)}, u32[]{:S(2)}) collective-permute-start(f32[640,128]{1,0:T(8,128)S(1)} %add.68.refs_1_), channel_id=1, source_target_pairs={{0,2},{1,3},{2,0},{3,1},{4,6},{5,7},{6,4},{7,5},{8,10},{9,11},{10,... | collective-permute-start | bytes 983048 | tf_op jit(solution)/shard_map/ppermute | solution.py:345
  24.5 12.4 %collective-permute-start.3 = (f32[640,128]{1,0:T(8,128)S(1)}, f32[640,128]{1,0:T(8,128)S(1)}, u32[]{:S(2)}, u32[]{:S(2)}) collective-permute-start(f32[640,128]{1,0:T(8,128)S(1)} %get-tuple-element.24.refs_1_), channel_id=1, source_target_pairs={{0,1},{1,0},{2,3},{3,2},{4,5},{5,4},{6,7},{7,6},{8,9},{9,8},{10,11... | collective-permute-start | bytes 983048 | tf_op jit(solution)/shard_map/ppermute | solution.py:348
  25.8 9.9 %collective-permute-start.4 = (f32[320,128]{1,0:T(8,128)S(1)}, f32[320,128]{1,0:T(8,128)}, u32[]{:S(2)}, u32[]{:S(2)}) collective-permute-start(f32[320,128]{1,0:T(8,128)S(1)} %get-tuple-element.25), channel_id=1, source_target_pairs={{0,4},{4,0},{8,12},{12,8},{16,20},{20,16},{24,28},{28,24},{1,5},{5... | collective-permute-start | bytes 491528 | tf_op jit(solution)/shard_map/ppermute | solution.py:349
  26.0 29.9 %collective-permute-start.10 = (f32[416,512]{1,0:T(8,128)}, f32[416,512]{1,0:T(8,128)}, u32[]{:S(2)}, u32[]{:S(2)}) collective-permute-start(f32[416,512]{1,0:T(8,128)} %get-tuple-element.32), channel_id=1, source_target_pairs={{0,4},{4,0},{8,12},{12,8},{16,20},{20,16},{24,28},{28,24},{1,5},{5... | collective-permute-start | bytes 2555912 | tf_op jit(solution)/shard_map/ppermute | solution.py:334
  35.7 13.4 %collective-permute-start.8 = (f32[320,128]{1,0:T(8,128)}, f32[320,128]{1,0:T(8,128)}, u32[]{:S(2)}, u32[]{:S(2)}) collective-permute-start(f32[320,128]{1,0:T(8,128)} %collective-permute-done.4.refs_3_.refs_1_), channel_id=1, source_target_pairs={{0,2},{1,3},{2,0},{3,1},{4,6},{5,7},{6,4},{7,5},{8,10},{9,11},{10,... | collective-permute-start | bytes 491528 | tf_op jit(solution)/shard_map/ppermute | solution.py:369
  36.9 8.4 %copy-start.8 = (f32[384,512]{1,0:T(8,128)}, f32[384,512]{1,0:T(8,128)S(1)}, u32[]{:S(2)}) copy-start(f32[384,512]{1,0:T(8,128)S(1)} %collective-permute-done.5.refs_5_.refs_3_) | copy-start | bytes 2359300
  36.9 8.4 %copy-start = (f32[1056,512]{1,0:T(8,128)S(1)}, f32[1056,512]{1,0:T(8,128)}, u32[]{:S(2)}) copy-start(f32[1056,512]{1,0:T(8,128)} %get-tuple-element.28.refs_2_) | copy-start | bytes 6488068
  45.3 4.8 %copy-start.2 = (bf16[512,512]{1,0:T(8,128)(2,1)}, bf16[512,512]{1,0:T(8,128)(2,1)S(1)}, u32[]{:S(2)}) copy-start(bf16[512,512]{1,0:T(8,128)(2,1)S(1)} %get-tuple-element.26.refs_0_.refs_2_) | copy-start | bytes 1572868
  45.3 4.8 %copy-start.4 = (bf16[512,512]{1,0:T(8,128)(2,1)}, bf16[512,512]{1,0:T(8,128)(2,1)S(1)}, u32[]{:S(2)}) copy-start(bf16[512,512]{1,0:T(8,128)(2,1)S(1)} %get-tuple-element.27.refs_1_.refs_3_) | copy-start | bytes 1572868
  51.0 4.9 %collective-permute-start.9 = (f32[640,128]{1,0:T(8,128)S(1)}, f32[640,128]{1,0:T(8,128)S(1)}, u32[]{:S(2)}, u32[]{:S(2)}) collective-permute-start(f32[640,128]{1,0:T(8,128)S(1)} %merge.1.refs_1_), channel_id=1, source_target_pairs={{0,1},{1,0},{2,3},{3,2},{4,5},{5,4},{6,7},{7,6},{8,9},{9,8},{10,11... | collective-permute-start | bytes 983048 | tf_op jit(solution)/shard_map/ppermute | solution.py:371
  52.7 44.8 %collective-permute-start.7 = (f32[864,256]{1,0:T(8,128)}, f32[864,256]{1,0:T(8,128)}, u32[]{:S(2)}, u32[]{:S(2)}) collective-permute-start(f32[864,256]{1,0:T(8,128)} %get-tuple-element.30.refs_3_), channel_id=1, source_target_pairs={{0,4},{4,0},{8,12},{12,8},{16,20},{20,16},{24,28},{28,24},{1,5},{5... | collective-permute-start | bytes 2654216 | tf_op jit(solution)/shard_map/ppermute | solution.py:364
  52.9 23.7 %collective-permute-start.14 = (f32[528,256]{1,0:T(8,128)}, f32[528,256]{1,0:T(8,128)}, u32[]{:S(2)}, u32[]{:S(2)}) collective-permute-start(f32[528,256]{1,0:T(8,128)} %get-tuple-element.37.refs_6_), channel_id=1, source_target_pairs={{8,4},{16,12},{24,20},{4,8},{12,16},{20,24},{9,5},{17,13},{25,21},... | collective-permute-start | bytes 1622024 | tf_op jit(solution)/shard_map/ppermute | solution.py:367
  55.9 8.2 %copy-start.9 = (f32[384,512]{1,0:T(8,128)S(1)}, f32[384,512]{1,0:T(8,128)}, u32[]{:S(2)}) copy-start(f32[384,512]{1,0:T(8,128)} %copy-done.8) | copy-start | bytes 2359300
  56.0 15.3 %copy-start.7 = (f32[528,256]{1,0:T(8,128)S(1)}, f32[528,256]{1,0:T(8,128)}, u32[]{:S(2)}) copy-start(f32[528,256]{1,0:T(8,128)} %copy-done.6) | copy-start | bytes 1622020
  56.0 22.0 %copy-start.3 = (bf16[512,512]{1,0:T(8,128)(2,1)S(1)}, bf16[512,512]{1,0:T(8,128)(2,1)}, u32[]{:S(2)}) copy-start(bf16[512,512]{1,0:T(8,128)(2,1)} %copy-done.2) | copy-start | bytes 1572868
  56.0 22.0 %copy-start.5 = (bf16[512,512]{1,0:T(8,128)(2,1)S(1)}, bf16[512,512]{1,0:T(8,128)(2,1)}, u32[]{:S(2)}) copy-start(bf16[512,512]{1,0:T(8,128)(2,1)} %copy-done.4) | copy-start | bytes 1572868
  68.1 25.4 %collective-permute-start.11 = (f32[576,256]{1,0:T(8,128)S(1)}, f32[576,256]{1,0:T(8,128)}, u32[]{:S(2)}, u32[]{:S(2)}) collective-permute-start(f32[576,256]{1,0:T(8,128)S(1)} %get-tuple-element.35.refs_4_), channel_id=1, source_target_pairs={{12,4},{20,12},{28,20},{0,8},{8,16},{16,24},{13,5},{21,13},{29,21}... | collective-permute-start | bytes 1769480 | tf_op jit(solution)/shard_map/ppermute | solution.py:380
  71.3 15.9 %collective-permute-start.13 = (f32[528,256]{1,0:T(8,128)S(1)}, f32[528,256]{1,0:T(8,128)}, u32[]{:S(2)}, u32[]{:S(2)}) collective-permute-start(f32[528,256]{1,0:T(8,128)S(1)} %copy-done.7), channel_id=1, source_target_pairs={{8,4},{16,12},{24,20},{4,8},{12,16},{20,24},{9,5},{17,13},{25,21},... | collective-permute-start | bytes 1622024 | tf_op jit(solution)/shard_map/ppermute | solution.py:367
  73.2 20.3 %collective-permute-start.12 = (f32[416,256]{1,0:T(8,128)}, f32[416,256]{1,0:T(8,128)}, u32[]{:S(2)}, u32[]{:S(2)}) collective-permute-start(f32[416,256]{1,0:T(8,128)} %get-tuple-element.36), channel_id=1, source_target_pairs={{12,4},{20,12},{28,20},{0,8},{8,16},{16,24},{13,5},{21,13},{29,21}... | collective-permute-start | bytes 1277960 | tf_op jit(solution)/shard_map/ppermute | solution.py:380
  76.6 25.1 %collective-permute-start.6 = (f32[192,256]{1,0:T(8,128)S(1)}, f32[192,256]{1,0:T(8,128)}, u32[]{:S(2)}, u32[]{:S(2)}) collective-permute-start(f32[192,256]{1,0:T(8,128)S(1)} %get-tuple-element.29), channel_id=1, source_target_pairs={{0,4},{4,0},{8,12},{12,8},{16,20},{20,16},{24,28},{28,24},{1,5},{5... | collective-permute-start | bytes 589832 | tf_op jit(solution)/shard_map/ppermute | solution.py:364
  (4 other events, 7.7 us)

commit v6 on v5

--- a/solution.py
+++ b/solution.py
@@ -11,7 +11,7 @@
 
 epsilon = 1e-06
 
-PLAN = ((0, (6, 12, 13)), (4, (33,)))
+PLAN = ((0, (6, 11, 14)), (4, (33,)))
 FIRST, LAST = 2, 6
 
 MIB = 1 << 20
@@ -59,16 +59,28 @@
     return lax.dot_general(a, b, (((0,), (0,)), ((), ())), preferred_element_type=F32)
 
 
-def upper_tiles(width):
+def packing(width):
     n = width // TILE
-    at = [slice(i * TILE, (i + 1) * TILE) for i in range(n)]
-    return list(enumerate((at[i], at[j]) for i in range(n) for j in range(i, n)))
+    above = [(i, j) for i in range(n) for j in range(i + 1, n)]
+    shared = [(i, i + 1) for i in range(0, n, 2)]
+    return [(above[h::2], shared[h::2]) for h in (0, 1)]
+
+
+def packed_rows(width):
+    above, shared = packing(width)[0]
+    return (len(above) + len(shared)) * TILE + 16
+
+
+def tile_at(i, j):
+    return slice(i * TILE, (i + 1) * TILE), slice(j * TILE, (j + 1) * TILE)
+
+
+def tile_indices():
+    return (lax.broadcasted_iota(jnp.int32, (TILE, TILE), axis) for axis in (0, 1))
 
 
 def gram(core, b, pieces, kept, after, parts=4):
     rows, width = b.shape
-    tiles = upper_tiles(width)
-    half = len(tiles) // 2
 
     def kernel(core_ref, b_ref, *refs):
         mine_ref, other_ref, *copies = refs[:-5]
@@ -91,19 +103,35 @@
         for store in stores:
             store.start()
 
+        def tile(i, j):
+            there, mirrored = tile_at(i, j), tile_at(j, i)
+            total = sum(high_ref[(p, *there)] + cross_ref[(p, *there)] for p in range(parts))
+            return total + sum(cross_ref[(p, *mirrored)] for p in range(parts)).T
+
+        row, column = tile_indices()
         for flag, outs in enumerate(((mine_ref, other_ref), (other_ref, mine_ref))):
 
             @pl.when(core_ref[0] == flag)
             def _():
-                for k, (i, j) in tiles:
-                    tile = sum(high_ref[p, i, j] + cross_ref[p, i, j] for p in range(parts))
-                    at = slice(k % half * TILE, (k % half + 1) * TILE)
-                    outs[k // half][at, :] = tile + sum(cross_ref[p, j, i] for p in range(parts)).T
+                for out_ref, (above, shared) in zip(outs, packing(width)):
+                    at = 0
+                    for i, j in above:
+                        out_ref[at : at + TILE, :] = tile(i, j)
+                        at += TILE
+                    diagonals = []
+                    for i, j in shared:
+                        one = tile(i, i)
+                        out_ref[at : at + TILE, :] = jnp.where(row < column, one, tile(j, j))
+                        diagonals.append(jnp.sum(jnp.where(row == column, one, 0.0), axis=0, keepdims=True))
+                        at += TILE
+                    out_ref[at:, :] = jnp.zeros_like(out_ref[at:, :])
+                    for k, diagonal in enumerate(diagonals):
+                        out_ref[at + k : at + k + 1, :] = diagonal
 
         for store in stores:
             store.wait()
 
-    outs = [shape(half * TILE, TILE)] * 2 + [shape(count, width) for _, count in (*pieces, *kept)]
+    outs = [shape(packed_rows(width), TILE)] * 2 + [shape(count, width) for _, count in (*pieces, *kept)]
     scratch = [
         pltpu.VMEM((rows, width), F32),
         *[pltpu.VMEM((parts, width, width), F32)] * 2,
@@ -156,14 +184,29 @@
     width = x_ref.shape[0]
     half = width // 2
     core, top_id, bottom_id, swapped = (at_ref[i] for i in range(4))
-    tiles = upper_tiles(width)
-    for k, (i, j) in tiles:
-        per = len(tiles) // 2
-        at = slice(k % per * TILE, (k % per + 1) * TILE)
-        tile = jnp.where(core == k // per, mine_ref[at], other_ref[at])
-        one_ref[i, j] = tile
-        if i != j:
-            one_ref[j, i] = tile.T
+    tile_row, tile_column = tile_indices()
+    for h, (above, shared) in enumerate(packing(width)):
+        at = 0
+
+        def taken(size):
+            rows = slice(at, at + size)
+            return jnp.where(core == h, mine_ref[rows, :], other_ref[rows, :])
+
+        for i, j in above:
+            tile = taken(TILE)
+            one_ref[tile_at(i, j)] = tile
+            one_ref[tile_at(j, i)] = tile.T
+            at += TILE
+        tiles = []
+        for _ in shared:
+            tiles.append(taken(TILE))
+            at += TILE
+        diagonals = taken(16)
+        for k, ((i, j), tile) in enumerate(zip(shared, tiles)):
+            mirrored = tile.T
+            lower = jnp.where(tile_row > tile_column, mirrored, diagonals[k : k + 1, :])
+            one_ref[tile_at(i, i)] = jnp.where(tile_row < tile_column, tile, lower)
+            one_ref[tile_at(j, j)] = jnp.where(tile_row < tile_column, mirrored, tile)
     row = lax.broadcasted_iota(jnp.int32, (width, width), 0)
     column = lax.broadcasted_iota(jnp.int32, (width, width), 1)
     on_diagonal = row == column
@@ -373,7 +416,7 @@
     w_q = polar(jnp.stack([core, *ids(partner), flag_q]), mine_q, other_q, width, from_partner[FIRST:])
     at_end = jnp.stack([first | last]).astype(jnp.int32)
     begin, count, threshold = groups[e]
-    cut = sum(a.shape[0] for a in from_partner[:FIRST])
+    cut = count * 3 // 5 // 32 * 32
     near, *far = turn(from_partner, w_q, [(0, 0, count), (1, 0, cut), (1, cut, count)])
     passes = [(p ^ 1, p - 1) for p in range(2, pairs, 2) if is_early(p, threshold)]
     passes += [(p ^ 1, p + 1) for p in range(1, pairs - 1, 2) if is_early(p, threshold)]

time: 104 us -> 102 us (0.981)
  waiting for transfers between devices: 29.4 us -> 27.2 us
    ppermute x1, waiting for transfers between devices: 7.69 us -> 6.46 us  [shards(): from_row = lax.ppermute(summed, 'tm', swap_rows)]
  transfers between devices with their start and end apart: 15 -> 15, of which waited for: 7 -> 6; matrix products, arithmetic and copies ran while one was open for 2% -> 2% of each run, Pallas kernels for 39% -> 40%
where the time goes in v6:
time: 102 us; the launch traced here: 101 us
  Pallas kernels  42.5 us (42%)
  waiting for transfers between devices  27.2 us (27%)
  starting transfers between devices  22.4 us (22%)
  local copies, waits for them, and re-layouts  7.8 us (8%)
  between operations  1.14 us (1%)
    pallas_call x17, Pallas kernels, call(): pl.pallas_call(body, in_specs=[*in_specs, *[after_spec] * late], out_spec...  42.5 us
    ppermute x1, waiting for transfers between devices, shards(): part = lax.ppermute(part, 'pair', swap_pairs)  6.99 us
    ppermute x2, starting transfers between devices, shards(): lax.ppermute(a, 'pair', passes)  6.52 us
    ppermute x1, waiting for transfers between devices, shards(): from_row = lax.ppermute(summed, 'tm', swap_rows)  6.46 us
    ppermute x2, waiting for transfers between devices, shards(): lax.ppermute(a, 'pair', passes)  6.28 us
    ppermute x2, waiting for transfers between devices, shards(): lax.ppermute(a, 'pair', onward[k])  4.98 us
    ppermute x2, starting transfers between devices, shards(): lax.ppermute(a, 'pair', onward[k])  4.92 us
    unnamed x26, local copies, waits for them, and re-layouts  3.99 us
  transfers between devices with their start and end apart: 15, of which 6 were waited for; matrix products, arithmetic and copies ran while one was open for 2% of the time, Pallas kernels for 40%

profile of v6, /device:TPU:9, one launch (start us, length us, event | category | flops | bytes accessed | tf_op | source)
XLA Modules:
  0.0 101.3 jit_solution(147203381712384755)
XLA Ops:
  0.0 1.8 %slice.6.refs_2_ = f32[192,512]{1,0:T(8,128)} slice(f32[2048,512]{1,0:T(8,128)} %refs_1_.3), slice={[0:192], [0:512]} | slice | bytes 786432 | tf_op jit(solution)/shard_map/slice | solution.py:380
  3.0 2.0 %slice.7.refs_3_ = f32[352,512]{1,0:T(8,128)} slice(f32[2048,512]{1,0:T(8,128)} %refs_1_.3), slice={[192:544], [0:512]} | slice | bytes 1441792 | tf_op jit(solution)/shard_map/slice | solution.py:380
  5.0 6.6 %gram.1 = (f32[528,128]{1,0:T(8,128)}, f32[528,128]{1,0:T(8,128)}, f32[448,512]{1,0:T(8,128)}, f32[1056,512]{1,0:T(8,128)}) custom-call(s32[1]{0:T(128)} %bitcast.2.refs_0_, f32[2048,512]{1,0:T(8,128)} %refs_1_.3, f32[192,512]{1,0:T(8,128)} %slice.6.refs_2_, f32[352,512]{1,0:T(8,128)} %slice.7.refs_3_), custom_call_target="tpu_custom_call" | custom-call | flops 999999995904 | tf_op jit(solution)/shard_map/gram/pallas_call | solution.py:32
  15.0 1.3 %collective-permute-start.2 = (f32[528,128]{1,0:T(8,128)S(1)}, f32[528,128]{1,0:T(8,128)S(1)}, u32[]{:S(2)}, u32[]{:S(2)}) collective-permute-start(f32[528,128]{1,0:T(8,128)S(1)} %add.68.refs_1_), channel_id=1, source_target_pairs={{0,2},{1,3},{2,0},{3,1},{4,6},{5,7},{6,4},{7,5},{8,10},{9,11},{10,... | collective-permute-start | bytes 811016 | tf_op jit(solution)/shard_map/ppermute | solution.py:388
  16.3 6.5 %collective-permute-done.2.refs_2_ = f32[528,128]{1,0:T(8,128)S(1)} collective-permute-done((f32[528,128]{1,0:T(8,128)S(1)}, f32[528,128]{1,0:T(8,128)S(1)}, u32[]{:S(2)}, u32[]{:S(2)}) %collective-permute-start.2) | collective-permute-done | bytes 270368 | tf_op jit(solution)/shard_map/ppermute | solution.py:388
  26.4 7.0 %collective-permute-done.4.refs_3_.refs_1_ = f32[264,128]{1,0:T(8,128)} collective-permute-done((f32[264,128]{1,0:T(8,128)S(1)}, f32[264,128]{1,0:T(8,128)}, u32[]{:S(2)}, u32[]{:S(2)}) %collective-permute-start.4) | collective-permute-done | bytes 135200 | tf_op jit(solution)/shard_map/ppermute | solution.py:392
  34.6 8.5 %polar.2 = (bf16[512,512]{1,0:T(8,128)(2,1)S(1)}, bf16[512,512]{1,0:T(8,128)(2,1)S(1)}) custom-call(s32[4]{0:T(128)S(1)} %pad_add_fusion.1.refs_0_, f32[528,128]{1,0:T(8,128)S(1)} %get-tuple-element.24.refs_1_, f32[528,128]{1,0:T(8,128)S(1)} %collective-permute-done.3.refs_2_, f32[264,128]{1,0:T(8,128)} %collective-permute-done.4.refs_3_.refs_1_, ...), custom_call_target="tpu_custom_call" | custom-call | flops 999999995904 | tf_op jit(solution)/shard_map/polar/pallas_call | solution.py:32
  43.1 2.0 %turn.3 = (f32[864,256]{1,0:T(8,128)}, f32[192,256]{1,0:T(8,128)S(1)}) custom-call(bf16[512,512]{1,0:T(8,128)(2,1)S(1)} %get-tuple-element.26.refs_0_.refs_2_, bf16[512,512]{1,0:T(8,128)(2,1)S(1)} %get-tuple-element.27.refs_1_.refs_3_, f32[1056,512]{1,0:T(8,128)S(1)} %copy-done), custom_call_target="tpu_custom_call" | custom-call | tf_op jit(solution)/shard_map/turn/pallas_call | solution.py:32
  45.1 1.8 %turn.4 = (f32[528,256]{1,0:T(8,128)S(1)}, f32[528,256]{1,0:T(8,128)}) custom-call(bf16[512,512]{1,0:T(8,128)(2,1)S(1)} %get-tuple-element.26.refs_0_.refs_2_, bf16[512,512]{1,0:T(8,128)(2,1)S(1)} %get-tuple-element.27.refs_1_.refs_3_, f32[1056,512]{1,0:T(8,128)S(1)} %copy-done, f32[864,256]{1,0:T(8,128)} %get-tuple-element.30.refs_3_), custom_call_target="tpu_custom_call" | custom-call | tf_op jit(solution)/shard_map/turn/pallas_call | solution.py:32
  48.8 1.6 %collective-permute-start.9 = (f32[528,128]{1,0:T(8,128)S(1)}, f32[528,128]{1,0:T(8,128)S(1)}, u32[]{:S(2)}, u32[]{:S(2)}) collective-permute-start(f32[528,128]{1,0:T(8,128)S(1)} %merge.1.refs_1_), channel_id=1, source_target_pairs={{0,1},{1,0},{2,3},{3,2},{4,5},{5,4},{6,7},{7,6},{8,9},{9,8},{10,11... | collective-permute-start | bytes 811016 | tf_op jit(solution)/shard_map/ppermute | solution.py:414
  50.7 3.0 %collective-permute-start.14 = (f32[528,256]{1,0:T(8,128)}, f32[528,256]{1,0:T(8,128)}, u32[]{:S(2)}, u32[]{:S(2)}) collective-permute-start(f32[528,256]{1,0:T(8,128)} %get-tuple-element.37.refs_6_), channel_id=1, source_target_pairs={{8,4},{16,12},{24,20},{4,8},{12,16},{20,24},{9,5},{17,13},{25,21},... | collective-permute-start | bytes 1622024 | tf_op jit(solution)/shard_map/ppermute | solution.py:410
  53.8 8.3 %polar.3 = (bf16[512,512]{1,0:T(8,128)(2,1)S(1)}, bf16[512,512]{1,0:T(8,128)(2,1)S(1)}) custom-call(s32[4]{0:T(128)S(1)} %pad_add_fusion.2.refs_0_, f32[528,128]{1,0:T(8,128)S(1)} %merge.1.refs_1_, f32[528,128]{1,0:T(8,128)S(1)} %collective-permute-done.9.refs_2_, f32[448,512]{1,0:T(8,128)} %collective-permute-done.10.refs_3_.refs_4_), custom_call_target="tpu_custom_call" | custom-call | flops 999999995904 | tf_op jit(solution)/shard_map/polar/pallas_call | solution.py:32
  62.1 4.1 %turn.5 = (f32[992,256]{1,0:T(8,128)S(1)}, f32[576,256]{1,0:T(8,128)S(1)}, f32[416,256]{1,0:T(8,128)}) custom-call(bf16[512,512]{1,0:T(8,128)(2,1)S(1)} %get-tuple-element.33.refs_0_, bf16[512,512]{1,0:T(8,128)(2,1)S(1)} %get-tuple-element.34.refs_1_, f32[192,512]{1,0:T(8,128)} %collective-permute-done.1.refs_2_.refs_4_, f32[352,512]{1,0:T(8,128)S(1)} %copy-done.9, ...), custom_call_target="tpu_custom_call" | custom-call | tf_op jit(solution)/shard_map/turn/pallas_call | solution.py:32
  66.1 3.2 %collective-permute-start.11 = (f32[576,256]{1,0:T(8,128)S(1)}, f32[576,256]{1,0:T(8,128)}, u32[]{:S(2)}, u32[]{:S(2)}) collective-permute-start(f32[576,256]{1,0:T(8,128)S(1)} %get-tuple-element.35.refs_4_), channel_id=1, source_target_pairs={{12,4},{20,12},{28,20},{0,8},{8,16},{16,24},{13,5},{21,13},{29,21}... | collective-permute-start | bytes 1769480 | tf_op jit(solution)/shard_map/ppermute | solution.py:423
  69.3 1.9 %collective-permute-start.13 = (f32[528,256]{1,0:T(8,128)S(1)}, f32[528,256]{1,0:T(8,128)}, u32[]{:S(2)}, u32[]{:S(2)}) collective-permute-start(f32[528,256]{1,0:T(8,128)S(1)} %copy-done.7), channel_id=1, source_target_pairs={{8,4},{16,12},{24,20},{4,8},{12,16},{20,24},{9,5},{17,13},{25,21},... | collective-permute-start | bytes 1622024 | tf_op jit(solution)/shard_map/ppermute | solution.py:410
  71.3 3.3 %collective-permute-start.12 = (f32[416,256]{1,0:T(8,128)}, f32[416,256]{1,0:T(8,128)}, u32[]{:S(2)}, u32[]{:S(2)}) collective-permute-start(f32[416,256]{1,0:T(8,128)} %get-tuple-element.36), channel_id=1, source_target_pairs={{12,4},{20,12},{28,20},{0,8},{8,16},{16,24},{13,5},{21,13},{29,21}... | collective-permute-start | bytes 1277960 | tf_op jit(solution)/shard_map/ppermute | solution.py:423
  76.0 2.2 %copy-done.1 = f32[2048,512]{1,0:T(8,128)S(1)} copy-done((f32[2048,512]{1,0:T(8,128)S(1)}, f32[2048,512]{1,0:T(8,128)}, u32[]{:S(2)}) %copy-start.1) | copy-done | bytes 4194328
  78.2 1.5 %join.4.refs_0_.refs_7_ = f32[2048,512]{1,0:T(8,128)} custom-call(s32[2]{0:T(128)S(1)} %pad_add_fusion.refs_0_, f32[992,256]{1,0:T(8,128)S(1)} %get-tuple-element.38.refs_1_, f32[992,256]{1,0:T(8,128)S(1)} %own.1.refs_2_), custom_call_target="tpu_custom_call" | custom-call | tf_op jit(solution)/shard_map/join/pallas_call | solution.py:32
  80.3 5.0 %collective-permute-done.13.refs_3_ = f32[528,256]{1,0:T(8,128)} collective-permute-done((f32[528,256]{1,0:T(8,128)S(1)}, f32[528,256]{1,0:T(8,128)}, u32[]{:S(2)}, u32[]{:S(2)}) %collective-permute-start.13) | collective-permute-done | bytes 540704 | tf_op jit(solution)/shard_map/ppermute | solution.py:410
  85.3 6.3 %collective-permute-done.12.refs_2_ = f32[416,256]{1,0:T(8,128)} collective-permute-done((f32[416,256]{1,0:T(8,128)}, f32[416,256]{1,0:T(8,128)}, u32[]{:S(2)}, u32[]{:S(2)}) %collective-permute-start.12) | collective-permute-done | bytes 426016 | tf_op jit(solution)/shard_map/ppermute | solution.py:423
  91.6 3.2 %join.5.refs_0_.refs_2_ = f32[2048,512]{1,0:T(8,128)} custom-call(s32[2]{0:T(128)} %copy-done.11, f32[576,256]{1,0:T(8,128)} %collective-permute-done.11.refs_1_, f32[416,256]{1,0:T(8,128)} %collective-permute-done.12.refs_2_, f32[528,256]{1,0:T(8,128)} %collective-permute-done.13.refs_3_, f32[528,256]{1,0:T(8,128)} %copy-done.6, ...), custom_call_target="tpu_custom_call", output_to_operand_aliasing={{}: (7, {})} | custom-call | tf_op jit(solution)/shard_map/join/pallas_call | solution.py:32
  95.4 2.1 %join.6.refs_0_.refs_2_ = f32[2048,512]{1,0:T(8,128)} custom-call(s32[2]{0:T(128)} %copy-done.11, f32[864,256]{1,0:T(8,128)} %collective-permute-done.7.refs_1_, f32[2048,512]{1,0:T(8,128)} %join.5.refs_0_.refs_2_, f32[8,128]{1,0:T(8,128)} %mark.4.refs_3_), custom_call_target="tpu_custom_call", output_to_operand_aliasing={{}: (2, {})} | custom-call | tf_op jit(solution)/shard_map/join/pallas_call | solution.py:32
  98.1 1.4 %collective-permute-done.6.refs_1_ = f32[192,256]{1,0:T(8,128)} collective-permute-done((f32[192,256]{1,0:T(8,128)S(1)}, f32[192,256]{1,0:T(8,128)}, u32[]{:S(2)}, u32[]{:S(2)}) %collective-permute-start.6) | collective-permute-done | bytes 196640 | tf_op jit(solution)/shard_map/ppermute | solution.py:407
  99.5 1.6 %join.7 = f32[2048,512]{1,0:T(8,128)} custom-call(s32[2]{0:T(128)} %copy-done.11, f32[192,256]{1,0:T(8,128)} %collective-permute-done.6.refs_1_, f32[2048,512]{1,0:T(8,128)} %join.6.refs_0_.refs_2_, f32[8,128]{1,0:T(8,128)} %mark.5.refs_3_), custom_call_target="tpu_custom_call", output_to_operand_aliasing={{}: (2, {})} | custom-call | tf_op jit(solution)/shard_map/join/pallas_call | solution.py:32
  (54 shorter events, 14.0 us)
Async XLA Ops:
  1.8 12.3 %collective-permute-start.1 = (f32[192,512]{1,0:T(8,128)}, f32[192,512]{1,0:T(8,128)}, u32[]{:S(2)}, u32[]{:S(2)}) collective-permute-start(f32[192,512]{1,0:T(8,128)} %slice.6.refs_2_), channel_id=1, source_target_pairs={{0,4},{4,0},{8,12},{12,8},{16,20},{20,16},{24,28},{28,24},{1,5},{5... | collective-permute-start | bytes 1179656 | tf_op jit(solution)/shard_map/ppermute | solution.py:377
  5.0 7.6 %copy-start.12 = (f32[352,512]{1,0:T(8,128)S(1)}, f32[352,512]{1,0:T(8,128)}, u32[]{:S(2)}) copy-start(f32[352,512]{1,0:T(8,128)} %slice.7.refs_3_) | copy-start | bytes 2162692
  11.7 2.4 %collective-permute-start = (f32[528,128]{1,0:T(8,128)}, f32[528,128]{1,0:T(8,128)S(1)}, u32[]{:S(2)}, u32[]{:S(2)}) collective-permute-start(f32[528,128]{1,0:T(8,128)} %get-tuple-element.23), channel_id=1, source_target_pairs={{0,1},{1,0},{2,3},{3,2},{4,5},{5,4},{6,7},{7,6},{8,9},{9,8},{10,11... | collective-permute-start | bytes 811016 | tf_op jit(solution)/shard_map/ppermute | solution.py:387
  12.7 21.9 %collective-permute-start.5 = (f32[352,512]{1,0:T(8,128)S(1)}, f32[352,512]{1,0:T(8,128)S(1)}, u32[]{:S(2)}, u32[]{:S(2)}) collective-permute-start(f32[352,512]{1,0:T(8,128)S(1)} %copy-done.12), channel_id=1, source_target_pairs={{0,4},{4,0},{8,12},{12,8},{16,20},{20,16},{24,28},{28,24},{1,5},{5... | collective-permute-start | bytes 2162696 | tf_op jit(solution)/shard_map/ppermute | solution.py:377
  15.0 7.8 %collective-permute-start.2 = (f32[528,128]{1,0:T(8,128)S(1)}, f32[528,128]{1,0:T(8,128)S(1)}, u32[]{:S(2)}, u32[]{:S(2)}) collective-permute-start(f32[528,128]{1,0:T(8,128)S(1)} %add.68.refs_1_), channel_id=1, source_target_pairs={{0,2},{1,3},{2,0},{3,1},{4,6},{5,7},{6,4},{7,5},{8,10},{9,11},{10,... | collective-permute-start | bytes 811016 | tf_op jit(solution)/shard_map/ppermute | solution.py:388
  22.9 11.8 %collective-permute-start.3 = (f32[528,128]{1,0:T(8,128)S(1)}, f32[528,128]{1,0:T(8,128)S(1)}, u32[]{:S(2)}, u32[]{:S(2)}) collective-permute-start(f32[528,128]{1,0:T(8,128)S(1)} %get-tuple-element.24.refs_1_), channel_id=1, source_target_pairs={{0,1},{1,0},{2,3},{3,2},{4,5},{5,4},{6,7},{7,6},{8,9},{9,8},{10,11... | collective-permute-start | bytes 811016 | tf_op jit(solution)/shard_map/ppermute | solution.py:391
  24.1 9.2 %collective-permute-start.4 = (f32[264,128]{1,0:T(8,128)S(1)}, f32[264,128]{1,0:T(8,128)}, u32[]{:S(2)}, u32[]{:S(2)}) collective-permute-start(f32[264,128]{1,0:T(8,128)S(1)} %get-tuple-element.25), channel_id=1, source_target_pairs={{0,4},{4,0},{8,12},{12,8},{16,20},{20,16},{24,28},{28,24},{1,5},{5... | collective-permute-start | bytes 405512 | tf_op jit(solution)/shard_map/ppermute | solution.py:392
  24.4 29.3 %collective-permute-start.10 = (f32[448,512]{1,0:T(8,128)}, f32[448,512]{1,0:T(8,128)}, u32[]{:S(2)}, u32[]{:S(2)}) collective-permute-start(f32[448,512]{1,0:T(8,128)} %get-tuple-element.32), channel_id=1, source_target_pairs={{0,4},{4,0},{8,12},{12,8},{16,20},{20,16},{24,28},{28,24},{1,5},{5... | collective-permute-start | bytes 2752520 | tf_op jit(solution)/shard_map/ppermute | solution.py:377
  33.4 13.5 %collective-permute-start.8 = (f32[264,128]{1,0:T(8,128)}, f32[264,128]{1,0:T(8,128)}, u32[]{:S(2)}, u32[]{:S(2)}) collective-permute-start(f32[264,128]{1,0:T(8,128)} %collective-permute-done.4.refs_3_.refs_1_), channel_id=1, source_target_pairs={{0,2},{1,3},{2,0},{3,1},{4,6},{5,7},{6,4},{7,5},{8,10},{9,11},{10,... | collective-permute-start | bytes 405512 | tf_op jit(solution)/shard_map/ppermute | solution.py:412
  34.6 8.5 %copy-start.8 = (f32[352,512]{1,0:T(8,128)}, f32[352,512]{1,0:T(8,128)S(1)}, u32[]{:S(2)}) copy-start(f32[352,512]{1,0:T(8,128)S(1)} %collective-permute-done.5.refs_5_.refs_3_) | copy-start | bytes 2162692
  34.6 8.5 %copy-start = (f32[1056,512]{1,0:T(8,128)S(1)}, f32[1056,512]{1,0:T(8,128)}, u32[]{:S(2)}) copy-start(f32[1056,512]{1,0:T(8,128)} %get-tuple-element.28.refs_2_) | copy-start | bytes 6488068
  43.1 4.8 %copy-start.2 = (bf16[512,512]{1,0:T(8,128)(2,1)}, bf16[512,512]{1,0:T(8,128)(2,1)S(1)}, u32[]{:S(2)}) copy-start(bf16[512,512]{1,0:T(8,128)(2,1)S(1)} %get-tuple-element.26.refs_0_.refs_2_) | copy-start | bytes 1572868
  43.1 4.8 %copy-start.4 = (bf16[512,512]{1,0:T(8,128)(2,1)}, bf16[512,512]{1,0:T(8,128)(2,1)S(1)}, u32[]{:S(2)}) copy-start(bf16[512,512]{1,0:T(8,128)(2,1)S(1)} %get-tuple-element.27.refs_1_.refs_3_) | copy-start | bytes 1572868
  48.8 4.9 %collective-permute-start.9 = (f32[528,128]{1,0:T(8,128)S(1)}, f32[528,128]{1,0:T(8,128)S(1)}, u32[]{:S(2)}, u32[]{:S(2)}) collective-permute-start(f32[528,128]{1,0:T(8,128)S(1)} %merge.1.refs_1_), channel_id=1, source_target_pairs={{0,1},{1,0},{2,3},{3,2},{4,5},{5,4},{6,7},{7,6},{8,9},{9,8},{10,11... | collective-permute-start | bytes 811016 | tf_op jit(solution)/shard_map/ppermute | solution.py:414
  50.4 45.0 %collective-permute-start.7 = (f32[864,256]{1,0:T(8,128)}, f32[864,256]{1,0:T(8,128)}, u32[]{:S(2)}, u32[]{:S(2)}) collective-permute-start(f32[864,256]{1,0:T(8,128)} %get-tuple-element.30.refs_3_), channel_id=1, source_target_pairs={{0,4},{4,0},{8,12},{12,8},{16,20},{20,16},{24,28},{28,24},{1,5},{5... | collective-permute-start | bytes 2654216 | tf_op jit(solution)/shard_map/ppermute | solution.py:407
  50.7 23.9 %collective-permute-start.14 = (f32[528,256]{1,0:T(8,128)}, f32[528,256]{1,0:T(8,128)}, u32[]{:S(2)}, u32[]{:S(2)}) collective-permute-start(f32[528,256]{1,0:T(8,128)} %get-tuple-element.37.refs_6_), channel_id=1, source_target_pairs={{8,4},{16,12},{24,20},{4,8},{12,16},{20,24},{9,5},{17,13},{25,21},... | collective-permute-start | bytes 1622024 | tf_op jit(solution)/shard_map/ppermute | solution.py:410
  53.7 8.3 %copy-start.9 = (f32[352,512]{1,0:T(8,128)S(1)}, f32[352,512]{1,0:T(8,128)}, u32[]{:S(2)}) copy-start(f32[352,512]{1,0:T(8,128)} %copy-done.8) | copy-start | bytes 2162692
  53.7 15.6 %copy-start.7 = (f32[528,256]{1,0:T(8,128)S(1)}, f32[528,256]{1,0:T(8,128)}, u32[]{:S(2)}) copy-start(f32[528,256]{1,0:T(8,128)} %copy-done.6) | copy-start | bytes 1622020
  53.7 22.2 %copy-start.3 = (bf16[512,512]{1,0:T(8,128)(2,1)S(1)}, bf16[512,512]{1,0:T(8,128)(2,1)}, u32[]{:S(2)}) copy-start(bf16[512,512]{1,0:T(8,128)(2,1)} %copy-done.2) | copy-start | bytes 1572868
  53.8 22.2 %copy-start.5 = (bf16[512,512]{1,0:T(8,128)(2,1)S(1)}, bf16[512,512]{1,0:T(8,128)(2,1)}, u32[]{:S(2)}) copy-start(bf16[512,512]{1,0:T(8,128)(2,1)} %copy-done.4) | copy-start | bytes 1572868
  66.1 25.4 %collective-permute-start.11 = (f32[576,256]{1,0:T(8,128)S(1)}, f32[576,256]{1,0:T(8,128)}, u32[]{:S(2)}, u32[]{:S(2)}) collective-permute-start(f32[576,256]{1,0:T(8,128)S(1)} %get-tuple-element.35.refs_4_), channel_id=1, source_target_pairs={{12,4},{20,12},{28,20},{0,8},{8,16},{16,24},{13,5},{21,13},{29,21}... | collective-permute-start | bytes 1769480 | tf_op jit(solution)/shard_map/ppermute | solution.py:423
  69.3 16.0 %collective-permute-start.13 = (f32[528,256]{1,0:T(8,128)S(1)}, f32[528,256]{1,0:T(8,128)}, u32[]{:S(2)}, u32[]{:S(2)}) collective-permute-start(f32[528,256]{1,0:T(8,128)S(1)} %copy-done.7), channel_id=1, source_target_pairs={{8,4},{16,12},{24,20},{4,8},{12,16},{20,24},{9,5},{17,13},{25,21},... | collective-permute-start | bytes 1622024 | tf_op jit(solution)/shard_map/ppermute | solution.py:410
  71.3 20.3 %collective-permute-start.12 = (f32[416,256]{1,0:T(8,128)}, f32[416,256]{1,0:T(8,128)}, u32[]{:S(2)}, u32[]{:S(2)}) collective-permute-start(f32[416,256]{1,0:T(8,128)} %get-tuple-element.36), channel_id=1, source_target_pairs={{12,4},{20,12},{28,20},{0,8},{8,16},{16,24},{13,5},{21,13},{29,21}... | collective-permute-start | bytes 1277960 | tf_op jit(solution)/shard_map/ppermute | solution.py:423
  74.6 24.9 %collective-permute-start.6 = (f32[192,256]{1,0:T(8,128)S(1)}, f32[192,256]{1,0:T(8,128)}, u32[]{:S(2)}, u32[]{:S(2)}) collective-permute-start(f32[192,256]{1,0:T(8,128)S(1)} %get-tuple-element.29), channel_id=1, source_target_pairs={{0,4},{4,0},{8,12},{12,8},{16,20},{20,16},{24,28},{28,24},{1,5},{5... | collective-permute-start | bytes 589832 | tf_op jit(solution)/shard_map/ppermute | solution.py:407
  (4 other events, 7.7 us)

commit v7 on v6

--- a/solution.py
+++ b/solution.py
@@ -11,7 +11,7 @@
 
 epsilon = 1e-06
 
-PLAN = ((0, (6, 11, 14)), (4, (33,)))
+PLAN = ((0, (6, 10, 15)), (4, (33,)))
 FIRST, LAST = 2, 6
 
 MIB = 1 << 20
@@ -139,7 +139,7 @@
         pltpu.SemaphoreType.DMA((len(outs) - 2,)),
     ]
     specs = [IN_VMEM] * 2 + [ANYWHERE] * len(pieces) + [IN_VMEM] * len(kept)
-    return call(kernel, "gram", (core, b), [IN_SMEM, ANYWHERE], outs, specs, scratch, after, 57, LONG)
+    return call(kernel, "gram", (core, b), [IN_SMEM, IN_HBM], outs, specs, scratch, after, 32, LONG)
 
 
 def add(a, b, after):
@@ -289,7 +289,7 @@
             load.wait()
             out_ref[...] = times(rows_ref[...], high_ref[:, half:], low_ref[:, half:])
 
-    specs = [IN_SMEM, ANYWHERE, WHOLE, WHOLE]
+    specs = [IN_SMEM, IN_HBM, WHOLE, WHOLE]
     scratch = [pltpu.VMEM((count, width), F32), pltpu.SemaphoreType.DMA]
     return call(kernel, "own", (at_end, b, *w), specs, shape(count, half), IN_VMEM, scratch, after, 24)
 

time: 102 us -> 101 us (level)
    unnamed x26 -> x22, local copies, waits for them, and re-layouts: 3.99 us -> 5.88 us
    ppermute x2, waiting for transfers between devices: 1.41 us -> 2.67 us  [shards(): lax.ppermute(a, 'pair', to_partner[k])]
  transfers between devices with their start and end apart: 15 -> 15, of which waited for: 6 -> 8; matrix products, arithmetic and copies ran while one was open for 2% -> 1% of each run, Pallas kernels for 40% -> 40%
where the time goes in v7:
time: 101 us
  Pallas kernels  41.5 us (41%)
  waiting for transfers between devices  26.7 us (26%)
  starting transfers between devices  22.5 us (22%)
  local copies, waits for them, and re-layouts  8.79 us (9%)
  between operations  1.09 us (1%)
    pallas_call x17, Pallas kernels, call(): pl.pallas_call(body, in_specs=[*in_specs, *[after_spec] * late], out_spec...  41.5 us
    ppermute x2, starting transfers between devices, shards(): lax.ppermute(a, 'pair', passes)  6.39 us
    ppermute x2, waiting for transfers between devices, shards(): lax.ppermute(a, 'pair', passes)  6.26 us
    ppermute x1, waiting for transfers between devices, shards(): from_row = lax.ppermute(summed, 'tm', swap_rows)  6.18 us
    ppermute x1, waiting for transfers between devices, shards(): part = lax.ppermute(part, 'pair', swap_pairs)  6.11 us
    unnamed x22, local copies, waits for them, and re-layouts  5.88 us
    ppermute x2, starting transfers between devices, shards(): lax.ppermute(a, 'pair', onward[k])  4.92 us
    ppermute x2, waiting for transfers between devices, shards(): lax.ppermute(a, 'pair', onward[k])  4.2 us
  transfers between devices with their start and end apart: 15, of which 8 were waited for; matrix products, arithmetic and copies ran while one was open for 1% of the time, Pallas kernels for 40%

profile of v7, /device:TPU:9, one launch (start us, length us, event | category | flops | bytes accessed | tf_op | source)
XLA Modules:
  0.0 100.8 jit_solution(2275542947059800702)
XLA Ops:
  0.0 1.8 %slice.6.refs_2_ = f32[192,512]{1,0:T(8,128)} slice(f32[2048,512]{1,0:T(8,128)} %refs_1_.3), slice={[0:192], [0:512]} | slice | bytes 786432 | tf_op jit(solution)/shard_map/slice | solution.py:380
  4.1 2.2 %copy-done = f32[2048,512]{1,0:T(8,128)S(1)} copy-done((f32[2048,512]{1,0:T(8,128)S(1)}, f32[2048,512]{1,0:T(8,128)}, u32[]{:S(2)}) %copy-start) | copy-done | bytes 4194328
  6.3 4.4 %gram.1 = (f32[528,128]{1,0:T(8,128)S(1)}, f32[528,128]{1,0:T(8,128)S(1)}, f32[480,512]{1,0:T(8,128)S(1)}, f32[1056,512]{1,0:T(8,128)S(1)}) custom-call(s32[1]{0:T(128)} %bitcast.2.refs_0_, f32[2048,512]{1,0:T(8,128)S(1)} %copy-done, f32[192,512]{1,0:T(8,128)} %slice.6.refs_2_, f32[320,512]{1,0:T(8,128)S(1)} %slice.7.refs_3_), custom_call_target="tpu_custom_call" | custom-call | flops 999999995904 | tf_op jit(solution)/shard_map/gram/pallas_call | solution.py:32
  14.3 6.2 %collective-permute-done.2.refs_2_ = f32[528,128]{1,0:T(8,128)S(1)} collective-permute-done((f32[528,128]{1,0:T(8,128)S(1)}, f32[528,128]{1,0:T(8,128)S(1)}, u32[]{:S(2)}, u32[]{:S(2)}) %collective-permute-start.2) | collective-permute-done | bytes 270368 | tf_op jit(solution)/shard_map/ppermute | solution.py:388
  21.2 1.5 %collective-permute-start.3 = (f32[528,128]{1,0:T(8,128)}, f32[528,128]{1,0:T(8,128)S(1)}, u32[]{:S(2)}, u32[]{:S(2)}) collective-permute-start(f32[528,128]{1,0:T(8,128)} %get-tuple-element.24.refs_1_), channel_id=1, source_target_pairs={{0,1},{1,0},{2,3},{3,2},{4,5},{5,4},{6,7},{7,6},{8,9},{9,8},{10,11... | collective-permute-start | bytes 811016 | tf_op jit(solution)/shard_map/ppermute | solution.py:391
  25.0 6.1 %collective-permute-done.4.refs_3_.refs_1_ = f32[264,128]{1,0:T(8,128)} collective-permute-done((f32[264,128]{1,0:T(8,128)S(1)}, f32[264,128]{1,0:T(8,128)}, u32[]{:S(2)}, u32[]{:S(2)}) %collective-permute-start.4) | collective-permute-done | bytes 135200 | tf_op jit(solution)/shard_map/ppermute | solution.py:392
  32.3 8.9 %polar.2 = (bf16[512,512]{1,0:T(8,128)(2,1)S(1)}, bf16[512,512]{1,0:T(8,128)(2,1)S(1)}) custom-call(s32[4]{0:T(128)S(1)} %pad_add_fusion.1.refs_0_, f32[528,128]{1,0:T(8,128)} %get-tuple-element.24.refs_1_, f32[528,128]{1,0:T(8,128)S(1)} %collective-permute-done.3.refs_2_, f32[264,128]{1,0:T(8,128)} %collective-permute-done.4.refs_3_.refs_1_, ...), custom_call_target="tpu_custom_call" | custom-call | flops 999999995904 | tf_op jit(solution)/shard_map/polar/pallas_call | solution.py:32
  41.2 2.0 %turn.3 = (f32[864,256]{1,0:T(8,128)}, f32[192,256]{1,0:T(8,128)}) custom-call(bf16[512,512]{1,0:T(8,128)(2,1)S(1)} %get-tuple-element.26.refs_0_.refs_2_, bf16[512,512]{1,0:T(8,128)(2,1)S(1)} %get-tuple-element.27.refs_1_.refs_3_, f32[1056,512]{1,0:T(8,128)S(1)} %get-tuple-element.28.refs_2_), custom_call_target="tpu_custom_call" | custom-call | tf_op jit(solution)/shard_map/turn/pallas_call | solution.py:32
  43.2 1.8 %turn.4 = (f32[528,256]{1,0:T(8,128)S(1)}, f32[528,256]{1,0:T(8,128)}) custom-call(bf16[512,512]{1,0:T(8,128)(2,1)S(1)} %get-tuple-element.26.refs_0_.refs_2_, bf16[512,512]{1,0:T(8,128)(2,1)S(1)} %get-tuple-element.27.refs_1_.refs_3_, f32[1056,512]{1,0:T(8,128)S(1)} %get-tuple-element.28.refs_2_, f32[864,256]{1,0:T(8,128)} %get-tuple-element.30.refs_3_), custom_call_target="tpu_custom_call" | custom-call | tf_op jit(solution)/shard_map/turn/pallas_call | solution.py:32
  46.9 1.6 %collective-permute-start.9 = (f32[528,128]{1,0:T(8,128)S(1)}, f32[528,128]{1,0:T(8,128)S(1)}, u32[]{:S(2)}, u32[]{:S(2)}) collective-permute-start(f32[528,128]{1,0:T(8,128)S(1)} %merge.1.refs_1_), channel_id=1, source_target_pairs={{0,1},{1,0},{2,3},{3,2},{4,5},{5,4},{6,7},{7,6},{8,9},{9,8},{10,11... | collective-permute-start | bytes 811016 | tf_op jit(solution)/shard_map/ppermute | solution.py:414
  48.8 3.0 %collective-permute-start.14 = (f32[528,256]{1,0:T(8,128)}, f32[528,256]{1,0:T(8,128)}, u32[]{:S(2)}, u32[]{:S(2)}) collective-permute-start(f32[528,256]{1,0:T(8,128)} %get-tuple-element.37.refs_6_), channel_id=1, source_target_pairs={{8,4},{16,12},{24,20},{4,8},{12,16},{20,24},{9,5},{17,13},{25,21},... | collective-permute-start | bytes 1622024 | tf_op jit(solution)/shard_map/ppermute | solution.py:410
  52.1 8.3 %polar.3 = (bf16[512,512]{1,0:T(8,128)(2,1)S(1)}, bf16[512,512]{1,0:T(8,128)(2,1)S(1)}) custom-call(s32[4]{0:T(128)S(1)} %pad_add_fusion.2.refs_0_, f32[528,128]{1,0:T(8,128)S(1)} %merge.1.refs_1_, f32[528,128]{1,0:T(8,128)S(1)} %collective-permute-done.9.refs_2_, f32[480,512]{1,0:T(8,128)} %collective-permute-done.10.refs_3_.refs_4_), custom_call_target="tpu_custom_call" | custom-call | flops 999999995904 | tf_op jit(solution)/shard_map/polar/pallas_call | solution.py:32
  60.4 4.1 %turn.5 = (f32[992,256]{1,0:T(8,128)S(1)}, f32[576,256]{1,0:T(8,128)S(1)}, f32[416,256]{1,0:T(8,128)}) custom-call(bf16[512,512]{1,0:T(8,128)(2,1)S(1)} %get-tuple-element.33.refs_0_, bf16[512,512]{1,0:T(8,128)(2,1)S(1)} %get-tuple-element.34.refs_1_, f32[192,512]{1,0:T(8,128)} %collective-permute-done.1.refs_2_.refs_4_, ...), custom_call_target="tpu_custom_call" | custom-call | tf_op jit(solution)/shard_map/turn/pallas_call | solution.py:32
  64.5 3.2 %collective-permute-start.11 = (f32[576,256]{1,0:T(8,128)S(1)}, f32[576,256]{1,0:T(8,128)}, u32[]{:S(2)}, u32[]{:S(2)}) collective-permute-start(f32[576,256]{1,0:T(8,128)S(1)} %get-tuple-element.35.refs_4_), channel_id=1, source_target_pairs={{12,4},{20,12},{28,20},{0,8},{8,16},{16,24},{13,5},{21,13},{29,21}... | collective-permute-start | bytes 1769480 | tf_op jit(solution)/shard_map/ppermute | solution.py:423
  67.7 1.9 %collective-permute-start.13 = (f32[528,256]{1,0:T(8,128)S(1)}, f32[528,256]{1,0:T(8,128)}, u32[]{:S(2)}, u32[]{:S(2)}) collective-permute-start(f32[528,256]{1,0:T(8,128)S(1)} %copy-done.7), channel_id=1, source_target_pairs={{8,4},{16,12},{24,20},{4,8},{12,16},{20,24},{9,5},{17,13},{25,21},... | collective-permute-start | bytes 1622024 | tf_op jit(solution)/shard_map/ppermute | solution.py:410
  69.7 3.2 %collective-permute-start.12 = (f32[416,256]{1,0:T(8,128)}, f32[416,256]{1,0:T(8,128)}, u32[]{:S(2)}, u32[]{:S(2)}) collective-permute-start(f32[416,256]{1,0:T(8,128)} %get-tuple-element.36), channel_id=1, source_target_pairs={{12,4},{20,12},{28,20},{0,8},{8,16},{16,24},{13,5},{21,13},{29,21}... | collective-permute-start | bytes 1277960 | tf_op jit(solution)/shard_map/ppermute | solution.py:423
  72.9 1.4 %collective-permute-start.6 = (f32[192,256]{1,0:T(8,128)}, f32[192,256]{1,0:T(8,128)S(1)}, u32[]{:S(2)}, u32[]{:S(2)}) collective-permute-start(f32[192,256]{1,0:T(8,128)} %get-tuple-element.29), channel_id=1, source_target_pairs={{0,4},{4,0},{8,12},{12,8},{16,20},{20,16},{24,28},{28,24},{1,5},{5... | collective-permute-start | bytes 589832 | tf_op jit(solution)/shard_map/ppermute | solution.py:407
  74.4 2.2 %copy-done.1 = f32[2048,512]{1,0:T(8,128)S(1)} copy-done((f32[2048,512]{1,0:T(8,128)S(1)}, f32[2048,512]{1,0:T(8,128)}, u32[]{:S(2)}) %copy-start.1) | copy-done | bytes 4194328
  76.6 1.5 %join.4.refs_0_.refs_7_ = f32[2048,512]{1,0:T(8,128)} custom-call(s32[2]{0:T(128)S(1)} %pad_add_fusion.refs_0_, f32[992,256]{1,0:T(8,128)S(1)} %get-tuple-element.38.refs_1_, f32[992,256]{1,0:T(8,128)S(1)} %own.1.refs_2_), custom_call_target="tpu_custom_call" | custom-call | tf_op jit(solution)/shard_map/join/pallas_call | solution.py:32
  78.7 4.2 %collective-permute-done.13.refs_3_ = f32[528,256]{1,0:T(8,128)} collective-permute-done((f32[528,256]{1,0:T(8,128)S(1)}, f32[528,256]{1,0:T(8,128)}, u32[]{:S(2)}, u32[]{:S(2)}) %collective-permute-start.13) | collective-permute-done | bytes 540704 | tf_op jit(solution)/shard_map/ppermute | solution.py:410
  82.9 6.3 %collective-permute-done.12.refs_2_ = f32[416,256]{1,0:T(8,128)} collective-permute-done((f32[416,256]{1,0:T(8,128)}, f32[416,256]{1,0:T(8,128)}, u32[]{:S(2)}, u32[]{:S(2)}) %collective-permute-start.12) | collective-permute-done | bytes 426016 | tf_op jit(solution)/shard_map/ppermute | solution.py:423
  89.2 3.2 %join.5.refs_0_.refs_2_ = f32[2048,512]{1,0:T(8,128)} custom-call(s32[2]{0:T(128)} %copy-done.8, f32[576,256]{1,0:T(8,128)} %collective-permute-done.11.refs_1_, f32[416,256]{1,0:T(8,128)} %collective-permute-done.12.refs_2_, f32[528,256]{1,0:T(8,128)} %collective-permute-done.13.refs_3_, f32[528,256]{1,0:T(8,128)} %copy-done.6, ...), custom_call_target="tpu_custom_call", output_to_operand_aliasing={{}: (7, {})} | custom-call | tf_op jit(solution)/shard_map/join/pallas_call | solution.py:32
  94.3 2.1 %join.6.refs_0_.refs_2_ = f32[2048,512]{1,0:T(8,128)} custom-call(s32[2]{0:T(128)} %copy-done.8, f32[864,256]{1,0:T(8,128)} %collective-permute-done.7.refs_1_, f32[2048,512]{1,0:T(8,128)} %join.5.refs_0_.refs_2_, f32[8,128]{1,0:T(8,128)} %mark.4.refs_3_), custom_call_target="tpu_custom_call", output_to_operand_aliasing={{}: (2, {})} | custom-call | tf_op jit(solution)/shard_map/join/pallas_call | solution.py:32
  99.0 1.6 %join.7 = f32[2048,512]{1,0:T(8,128)} custom-call(s32[2]{0:T(128)} %copy-done.8, f32[192,256]{1,0:T(8,128)} %copy-done.10, f32[2048,512]{1,0:T(8,128)} %join.6.refs_0_.refs_2_, f32[8,128]{1,0:T(8,128)} %mark.5.refs_3_), custom_call_target="tpu_custom_call", output_to_operand_aliasing={{}: (2, {})} | custom-call | tf_op jit(solution)/shard_map/join/pallas_call | solution.py:32
  (50 shorter events, 17.1 us)
Async XLA Ops:
  1.8 11.2 %collective-permute-start.1 = (f32[192,512]{1,0:T(8,128)}, f32[192,512]{1,0:T(8,128)}, u32[]{:S(2)}, u32[]{:S(2)}) collective-permute-start(f32[192,512]{1,0:T(8,128)} %slice.6.refs_2_), channel_id=1, source_target_pairs={{0,4},{4,0},{8,12},{12,8},{16,20},{20,16},{24,28},{28,24},{1,5},{5... | collective-permute-start | bytes 1179656 | tf_op jit(solution)/shard_map/ppermute | solution.py:377
  4.1 2.2 %copy-start = (f32[2048,512]{1,0:T(8,128)S(1)}, f32[2048,512]{1,0:T(8,128)}, u32[]{:S(2)}) copy-start(f32[2048,512]{1,0:T(8,128)} %refs_1_.3) | copy-start | bytes 12582916
  10.7 2.2 %copy-start.9 = (f32[480,512]{1,0:T(8,128)}, f32[480,512]{1,0:T(8,128)S(1)}, u32[]{:S(2)}) copy-start(f32[480,512]{1,0:T(8,128)S(1)} %get-tuple-element.32) | copy-start | bytes 2949124
  10.7 2.2 %collective-permute-start = (f32[528,128]{1,0:T(8,128)S(1)}, f32[528,128]{1,0:T(8,128)S(1)}, u32[]{:S(2)}, u32[]{:S(2)}) collective-permute-start(f32[528,128]{1,0:T(8,128)S(1)} %get-tuple-element.23), channel_id=1, source_target_pairs={{0,1},{1,0},{2,3},{3,2},{4,5},{5,4},{6,7},{7,6},{8,9},{9,8},{10,11... | collective-permute-start | bytes 811016 | tf_op jit(solution)/shard_map/ppermute | solution.py:387
  11.8 20.6 %collective-permute-start.5 = (f32[320,512]{1,0:T(8,128)S(1)}, f32[320,512]{1,0:T(8,128)}, u32[]{:S(2)}, u32[]{:S(2)}) collective-permute-start(f32[320,512]{1,0:T(8,128)S(1)} %slice.7.refs_3_), channel_id=1, source_target_pairs={{0,4},{4,0},{8,12},{12,8},{16,20},{20,16},{24,28},{28,24},{1,5},{5... | collective-permute-start | bytes 1966088 | tf_op jit(solution)/shard_map/ppermute | solution.py:377
  13.0 7.5 %collective-permute-start.2 = (f32[528,128]{1,0:T(8,128)S(1)}, f32[528,128]{1,0:T(8,128)S(1)}, u32[]{:S(2)}, u32[]{:S(2)}) collective-permute-start(f32[528,128]{1,0:T(8,128)S(1)} %add.68.refs_1_), channel_id=1, source_target_pairs={{0,2},{1,3},{2,0},{3,1},{4,6},{5,7},{6,4},{7,5},{8,10},{9,11},{10,... | collective-permute-start | bytes 811016 | tf_op jit(solution)/shard_map/ppermute | solution.py:388
  21.2 11.1 %collective-permute-start.3 = (f32[528,128]{1,0:T(8,128)}, f32[528,128]{1,0:T(8,128)S(1)}, u32[]{:S(2)}, u32[]{:S(2)}) collective-permute-start(f32[528,128]{1,0:T(8,128)} %get-tuple-element.24.refs_1_), channel_id=1, source_target_pairs={{0,1},{1,0},{2,3},{3,2},{4,5},{5,4},{6,7},{7,6},{8,9},{9,8},{10,11... | collective-permute-start | bytes 811016 | tf_op jit(solution)/shard_map/ppermute | solution.py:391
  22.7 8.4 %collective-permute-start.4 = (f32[264,128]{1,0:T(8,128)S(1)}, f32[264,128]{1,0:T(8,128)}, u32[]{:S(2)}, u32[]{:S(2)}) collective-permute-start(f32[264,128]{1,0:T(8,128)S(1)} %get-tuple-element.25), channel_id=1, source_target_pairs={{0,4},{4,0},{8,12},{12,8},{16,20},{20,16},{24,28},{28,24},{1,5},{5... | collective-permute-start | bytes 405512 | tf_op jit(solution)/shard_map/ppermute | solution.py:392
  23.1 29.1 %collective-permute-start.10 = (f32[480,512]{1,0:T(8,128)}, f32[480,512]{1,0:T(8,128)}, u32[]{:S(2)}, u32[]{:S(2)}) collective-permute-start(f32[480,512]{1,0:T(8,128)} %copy-done.9), channel_id=1, source_target_pairs={{0,4},{4,0},{8,12},{12,8},{16,20},{20,16},{24,28},{28,24},{1,5},{5... | collective-permute-start | bytes 2949128 | tf_op jit(solution)/shard_map/ppermute | solution.py:377
  31.1 14.0 %collective-permute-start.8 = (f32[264,128]{1,0:T(8,128)}, f32[264,128]{1,0:T(8,128)}, u32[]{:S(2)}, u32[]{:S(2)}) collective-permute-start(f32[264,128]{1,0:T(8,128)} %collective-permute-done.4.refs_3_.refs_1_), channel_id=1, source_target_pairs={{0,2},{1,3},{2,0},{3,1},{4,6},{5,7},{6,4},{7,5},{8,10},{9,11},{10,... | collective-permute-start | bytes 405512 | tf_op jit(solution)/shard_map/ppermute | solution.py:412
  41.2 4.9 %copy-start.2 = (bf16[512,512]{1,0:T(8,128)(2,1)}, bf16[512,512]{1,0:T(8,128)(2,1)S(1)}, u32[]{:S(2)}) copy-start(bf16[512,512]{1,0:T(8,128)(2,1)S(1)} %get-tuple-element.26.refs_0_.refs_2_) | copy-start | bytes 1572868
  41.2 4.9 %copy-start.4 = (bf16[512,512]{1,0:T(8,128)(2,1)}, bf16[512,512]{1,0:T(8,128)(2,1)S(1)}, u32[]{:S(2)}) copy-start(bf16[512,512]{1,0:T(8,128)(2,1)S(1)} %get-tuple-element.27.refs_1_.refs_3_) | copy-start | bytes 1572868
  46.9 5.2 %collective-permute-start.9 = (f32[528,128]{1,0:T(8,128)S(1)}, f32[528,128]{1,0:T(8,128)S(1)}, u32[]{:S(2)}, u32[]{:S(2)}) collective-permute-start(f32[528,128]{1,0:T(8,128)S(1)} %merge.1.refs_1_), channel_id=1, source_target_pairs={{0,1},{1,0},{2,3},{3,2},{4,5},{5,4},{6,7},{7,6},{8,9},{9,8},{10,11... | collective-permute-start | bytes 811016 | tf_op jit(solution)/shard_map/ppermute | solution.py:414
  48.6 45.7 %collective-permute-start.7 = (f32[864,256]{1,0:T(8,128)}, f32[864,256]{1,0:T(8,128)}, u32[]{:S(2)}, u32[]{:S(2)}) collective-permute-start(f32[864,256]{1,0:T(8,128)} %get-tuple-element.30.refs_3_), channel_id=1, source_target_pairs={{0,4},{4,0},{8,12},{12,8},{16,20},{20,16},{24,28},{28,24},{1,5},{5... | collective-permute-start | bytes 2654216 | tf_op jit(solution)/shard_map/ppermute | solution.py:407
  48.8 24.1 %collective-permute-start.14 = (f32[528,256]{1,0:T(8,128)}, f32[528,256]{1,0:T(8,128)}, u32[]{:S(2)}, u32[]{:S(2)}) collective-permute-start(f32[528,256]{1,0:T(8,128)} %get-tuple-element.37.refs_6_), channel_id=1, source_target_pairs={{8,4},{16,12},{24,20},{4,8},{12,16},{20,24},{9,5},{17,13},{25,21},... | collective-permute-start | bytes 1622024 | tf_op jit(solution)/shard_map/ppermute | solution.py:410
  52.1 15.6 %copy-start.7 = (f32[528,256]{1,0:T(8,128)S(1)}, f32[528,256]{1,0:T(8,128)}, u32[]{:S(2)}) copy-start(f32[528,256]{1,0:T(8,128)} %copy-done.6) | copy-start | bytes 1622020
  52.1 22.2 %copy-start.3 = (bf16[512,512]{1,0:T(8,128)(2,1)S(1)}, bf16[512,512]{1,0:T(8,128)(2,1)}, u32[]{:S(2)}) copy-start(bf16[512,512]{1,0:T(8,128)(2,1)} %copy-done.2) | copy-start | bytes 1572868
  52.1 22.2 %copy-start.5 = (bf16[512,512]{1,0:T(8,128)(2,1)S(1)}, bf16[512,512]{1,0:T(8,128)(2,1)}, u32[]{:S(2)}) copy-start(bf16[512,512]{1,0:T(8,128)(2,1)} %copy-done.4) | copy-start | bytes 1572868
  64.5 24.6 %collective-permute-start.11 = (f32[576,256]{1,0:T(8,128)S(1)}, f32[576,256]{1,0:T(8,128)}, u32[]{:S(2)}, u32[]{:S(2)}) collective-permute-start(f32[576,256]{1,0:T(8,128)S(1)} %get-tuple-element.35.refs_4_), channel_id=1, source_target_pairs={{12,4},{20,12},{28,20},{0,8},{8,16},{16,24},{13,5},{21,13},{29,21}... | collective-permute-start | bytes 1769480 | tf_op jit(solution)/shard_map/ppermute | solution.py:423
  67.7 15.2 %collective-permute-start.13 = (f32[528,256]{1,0:T(8,128)S(1)}, f32[528,256]{1,0:T(8,128)}, u32[]{:S(2)}, u32[]{:S(2)}) collective-permute-start(f32[528,256]{1,0:T(8,128)S(1)} %copy-done.7), channel_id=1, source_target_pairs={{8,4},{16,12},{24,20},{4,8},{12,16},{20,24},{9,5},{17,13},{25,21},... | collective-permute-start | bytes 1622024 | tf_op jit(solution)/shard_map/ppermute | solution.py:410
  69.7 19.5 %collective-permute-start.12 = (f32[416,256]{1,0:T(8,128)}, f32[416,256]{1,0:T(8,128)}, u32[]{:S(2)}, u32[]{:S(2)}) collective-permute-start(f32[416,256]{1,0:T(8,128)} %get-tuple-element.36), channel_id=1, source_target_pairs={{12,4},{20,12},{28,20},{0,8},{8,16},{16,24},{13,5},{21,13},{29,21}... | collective-permute-start | bytes 1277960 | tf_op jit(solution)/shard_map/ppermute | solution.py:423
  72.9 25.5 %collective-permute-start.6 = (f32[192,256]{1,0:T(8,128)}, f32[192,256]{1,0:T(8,128)S(1)}, u32[]{:S(2)}, u32[]{:S(2)}) collective-permute-start(f32[192,256]{1,0:T(8,128)} %get-tuple-element.29), channel_id=1, source_target_pairs={{0,4},{4,0},{8,12},{12,8},{16,20},{20,16},{24,28},{28,24},{1,5},{5... | collective-permute-start | bytes 589832 | tf_op jit(solution)/shard_map/ppermute | solution.py:407
  74.4 3.7 %copy-start.8 = (s32[2]{0:T(128)}, s32[2]{0:T(128)S(1)}, u32[]{:S(2)}) copy-start(s32[2]{0:T(128)S(1)} %pad_add_fusion.refs_0_) | copy-start | bytes 28
  74.4 2.2 %copy-start.1 = (f32[2048,512]{1,0:T(8,128)S(1)}, f32[2048,512]{1,0:T(8,128)}, u32[]{:S(2)}) copy-start(f32[2048,512]{1,0:T(8,128)} %refs_1_.3) | copy-start | bytes 12582916
  (2 other events, 1.5 us)

commit v8 on v7

--- a/solution.py
+++ b/solution.py
@@ -11,7 +11,7 @@
 
 epsilon = 1e-06
 
-PLAN = ((0, (6, 10, 15)), (4, (33,)))
+PLAN = ((0, (6, 10, 14)), (4, (34,)))
 FIRST, LAST = 2, 6
 
 MIB = 1 << 20

time: 101 us -> 102 us (level)
    ppermute x2, waiting for transfers between devices: 4.2 us -> 5.34 us  [shards(): lax.ppermute(a, 'pair', onward[k])]
    ppermute x2, waiting for transfers between devices: 6.26 us -> 5.2 us  [shards(): lax.ppermute(a, 'pair', passes)]
  transfers between devices with their start and end apart: 15 -> 15, of which waited for: 8 -> 7; matrix products, arithmetic and copies ran while one was open for 1% -> 1% of each run, Pallas kernels for 40% -> 39%
where the time goes in v8:
time: 102 us; the launch traced here: 101 us
  Pallas kernels  41.6 us (41%)
  waiting for transfers between devices  27.1 us (27%)
  starting transfers between devices  22.6 us (22%)
  local copies, waits for them, and re-layouts  8.76 us (9%)
  between operations  1.13 us (1%)
    pallas_call x17, Pallas kernels, call(): pl.pallas_call(body, in_specs=[*in_specs, *[after_spec] * late], out_spec...  41.6 us
    ppermute x2, starting transfers between devices, shards(): lax.ppermute(a, 'pair', passes)  6.53 us
    ppermute x1, waiting for transfers between devices, shards(): from_row = lax.ppermute(summed, 'tm', swap_rows)  6.18 us
    ppermute x1, waiting for transfers between devices, shards(): part = lax.ppermute(part, 'pair', swap_pairs)  6.07 us
    unnamed x22, local copies, waits for them, and re-layouts  5.88 us
    ppermute x2, waiting for transfers between devices, shards(): lax.ppermute(a, 'pair', onward[k])  5.34 us
    ppermute x2, waiting for transfers between devices, shards(): lax.ppermute(a, 'pair', passes)  5.2 us
    ppermute x2, starting transfers between devices, shards(): lax.ppermute(a, 'pair', onward[k])  4.91 us
  transfers between devices with their start and end apart: 15, of which 7 were waited for; matrix products, arithmetic and copies ran while one was open for 1% of the time, Pallas kernels for 39%

profile of v8, /device:TPU:9, one launch (start us, length us, event | category | flops | bytes accessed | tf_op | source)
XLA Modules:
  0.0 101.3 jit_solution(9978475148459938960)
XLA Ops:
  0.0 1.8 %slice.6.refs_2_ = f32[192,512]{1,0:T(8,128)} slice(f32[2048,512]{1,0:T(8,128)} %refs_1_.3), slice={[0:192], [0:512]} | slice | bytes 786432 | tf_op jit(solution)/shard_map/slice | solution.py:380
  4.1 2.2 %copy-done = f32[2048,512]{1,0:T(8,128)S(1)} copy-done((f32[2048,512]{1,0:T(8,128)S(1)}, f32[2048,512]{1,0:T(8,128)}, u32[]{:S(2)}) %copy-start) | copy-done | bytes 4194328
  6.3 4.4 %gram.1 = (f32[528,128]{1,0:T(8,128)S(1)}, f32[528,128]{1,0:T(8,128)S(1)}, f32[448,512]{1,0:T(8,128)S(1)}, f32[1088,512]{1,0:T(8,128)S(1)}) custom-call(s32[1]{0:T(128)} %bitcast.2.refs_0_, f32[2048,512]{1,0:T(8,128)S(1)} %copy-done, f32[192,512]{1,0:T(8,128)} %slice.6.refs_2_, f32[320,512]{1,0:T(8,128)S(1)} %slice.7.refs_3_), custom_call_target="tpu_custom_call" | custom-call | flops 999999995904 | tf_op jit(solution)/shard_map/gram/pallas_call | solution.py:32
  14.3 6.2 %collective-permute-done.2.refs_2_ = f32[528,128]{1,0:T(8,128)S(1)} collective-permute-done((f32[528,128]{1,0:T(8,128)S(1)}, f32[528,128]{1,0:T(8,128)S(1)}, u32[]{:S(2)}, u32[]{:S(2)}) %collective-permute-start.2) | collective-permute-done | bytes 270368 | tf_op jit(solution)/shard_map/ppermute | solution.py:388
  21.3 1.5 %collective-permute-start.3 = (f32[528,128]{1,0:T(8,128)}, f32[528,128]{1,0:T(8,128)S(1)}, u32[]{:S(2)}, u32[]{:S(2)}) collective-permute-start(f32[528,128]{1,0:T(8,128)} %get-tuple-element.24.refs_1_), channel_id=1, source_target_pairs={{0,1},{1,0},{2,3},{3,2},{4,5},{5,4},{6,7},{7,6},{8,9},{9,8},{10,11... | collective-permute-start | bytes 811016 | tf_op jit(solution)/shard_map/ppermute | solution.py:391
  25.0 6.1 %collective-permute-done.4.refs_3_.refs_1_ = f32[264,128]{1,0:T(8,128)} collective-permute-done((f32[264,128]{1,0:T(8,128)}, f32[264,128]{1,0:T(8,128)}, u32[]{:S(2)}, u32[]{:S(2)}) %collective-permute-start.4) | collective-permute-done | bytes 135200 | tf_op jit(solution)/shard_map/ppermute | solution.py:392
  32.3 8.9 %polar.2 = (bf16[512,512]{1,0:T(8,128)(2,1)S(1)}, bf16[512,512]{1,0:T(8,128)(2,1)S(1)}) custom-call(s32[4]{0:T(128)S(1)} %pad_add_fusion.1.refs_0_, f32[528,128]{1,0:T(8,128)} %get-tuple-element.24.refs_1_, f32[528,128]{1,0:T(8,128)S(1)} %collective-permute-done.3.refs_2_, f32[264,128]{1,0:T(8,128)} %collective-permute-done.4.refs_3_.refs_1_, ...), custom_call_target="tpu_custom_call" | custom-call | flops 999999995904 | tf_op jit(solution)/shard_map/polar/pallas_call | solution.py:32
  41.2 2.1 %turn.3 = (f32[896,256]{1,0:T(8,128)}, f32[192,256]{1,0:T(8,128)}) custom-call(bf16[512,512]{1,0:T(8,128)(2,1)S(1)} %get-tuple-element.26.refs_0_.refs_2_, bf16[512,512]{1,0:T(8,128)(2,1)S(1)} %get-tuple-element.27.refs_1_.refs_3_, f32[1088,512]{1,0:T(8,128)S(1)} %get-tuple-element.28.refs_2_), custom_call_target="tpu_custom_call" | custom-call | tf_op jit(solution)/shard_map/turn/pallas_call | solution.py:32
  43.3 1.8 %turn.4 = (f32[544,256]{1,0:T(8,128)S(1)}, f32[544,256]{1,0:T(8,128)}) custom-call(bf16[512,512]{1,0:T(8,128)(2,1)S(1)} %get-tuple-element.26.refs_0_.refs_2_, bf16[512,512]{1,0:T(8,128)(2,1)S(1)} %get-tuple-element.27.refs_1_.refs_3_, f32[1088,512]{1,0:T(8,128)S(1)} %get-tuple-element.28.refs_2_, f32[896,256]{1,0:T(8,128)} %get-tuple-element.30.refs_3_), custom_call_target="tpu_custom_call" | custom-call | tf_op jit(solution)/shard_map/turn/pallas_call | solution.py:32
  46.9 1.6 %collective-permute-start.9 = (f32[528,128]{1,0:T(8,128)S(1)}, f32[528,128]{1,0:T(8,128)S(1)}, u32[]{:S(2)}, u32[]{:S(2)}) collective-permute-start(f32[528,128]{1,0:T(8,128)S(1)} %merge.1.refs_1_), channel_id=1, source_target_pairs={{0,1},{1,0},{2,3},{3,2},{4,5},{5,4},{6,7},{7,6},{8,9},{9,8},{10,11... | collective-permute-start | bytes 811016 | tf_op jit(solution)/shard_map/ppermute | solution.py:414
  48.9 3.0 %collective-permute-start.14 = (f32[544,256]{1,0:T(8,128)}, f32[544,256]{1,0:T(8,128)}, u32[]{:S(2)}, u32[]{:S(2)}) collective-permute-start(f32[544,256]{1,0:T(8,128)} %get-tuple-element.37.refs_6_), channel_id=1, source_target_pairs={{8,4},{16,12},{24,20},{4,8},{12,16},{20,24},{9,5},{17,13},{25,21},... | collective-permute-start | bytes 1671176 | tf_op jit(solution)/shard_map/ppermute | solution.py:410
  51.9 8.3 %polar.3 = (bf16[512,512]{1,0:T(8,128)(2,1)S(1)}, bf16[512,512]{1,0:T(8,128)(2,1)S(1)}) custom-call(s32[4]{0:T(128)S(1)} %pad_add_fusion.2.refs_0_, f32[528,128]{1,0:T(8,128)S(1)} %merge.1.refs_1_, f32[528,128]{1,0:T(8,128)S(1)} %collective-permute-done.9.refs_2_, f32[448,512]{1,0:T(8,128)} %collective-permute-done.10.refs_3_.refs_4_), custom_call_target="tpu_custom_call" | custom-call | flops 999999995904 | tf_op jit(solution)/shard_map/polar/pallas_call | solution.py:32
  60.2 4.0 %turn.5 = (f32[960,256]{1,0:T(8,128)S(1)}, f32[576,256]{1,0:T(8,128)S(1)}, f32[384,256]{1,0:T(8,128)}) custom-call(bf16[512,512]{1,0:T(8,128)(2,1)S(1)} %get-tuple-element.33.refs_0_, bf16[512,512]{1,0:T(8,128)(2,1)S(1)} %get-tuple-element.34.refs_1_, f32[192,512]{1,0:T(8,128)} %collective-permute-done.1.refs_2_.refs_4_, ...), custom_call_target="tpu_custom_call" | custom-call | tf_op jit(solution)/shard_map/turn/pallas_call | solution.py:32
  64.2 3.2 %collective-permute-start.11 = (f32[576,256]{1,0:T(8,128)S(1)}, f32[576,256]{1,0:T(8,128)}, u32[]{:S(2)}, u32[]{:S(2)}) collective-permute-start(f32[576,256]{1,0:T(8,128)S(1)} %get-tuple-element.35.refs_4_), channel_id=1, source_target_pairs={{12,4},{20,12},{28,20},{0,8},{8,16},{16,24},{13,5},{21,13},{29,21}... | collective-permute-start | bytes 1769480 | tf_op jit(solution)/shard_map/ppermute | solution.py:423
  67.5 1.9 %collective-permute-start.13 = (f32[544,256]{1,0:T(8,128)S(1)}, f32[544,256]{1,0:T(8,128)}, u32[]{:S(2)}, u32[]{:S(2)}) collective-permute-start(f32[544,256]{1,0:T(8,128)S(1)} %copy-done.7), channel_id=1, source_target_pairs={{8,4},{16,12},{24,20},{4,8},{12,16},{20,24},{9,5},{17,13},{25,21},... | collective-permute-start | bytes 1671176 | tf_op jit(solution)/shard_map/ppermute | solution.py:410
  69.4 3.3 %collective-permute-start.12 = (f32[384,256]{1,0:T(8,128)}, f32[384,256]{1,0:T(8,128)}, u32[]{:S(2)}, u32[]{:S(2)}) collective-permute-start(f32[384,256]{1,0:T(8,128)} %get-tuple-element.36), channel_id=1, source_target_pairs={{12,4},{20,12},{28,20},{0,8},{8,16},{16,24},{13,5},{21,13},{29,21}... | collective-permute-start | bytes 1179656 | tf_op jit(solution)/shard_map/ppermute | solution.py:423
  74.1 2.2 %copy-done.1 = f32[2048,512]{1,0:T(8,128)S(1)} copy-done((f32[2048,512]{1,0:T(8,128)S(1)}, f32[2048,512]{1,0:T(8,128)}, u32[]{:S(2)}) %copy-start.1) | copy-done | bytes 4194328
  76.3 1.5 %join.4.refs_0_.refs_7_ = f32[2048,512]{1,0:T(8,128)} custom-call(s32[2]{0:T(128)S(1)} %pad_add_fusion.refs_0_, f32[960,256]{1,0:T(8,128)S(1)} %get-tuple-element.38.refs_1_, f32[960,256]{1,0:T(8,128)S(1)} %own.1.refs_2_), custom_call_target="tpu_custom_call" | custom-call | tf_op jit(solution)/shard_map/join/pallas_call | solution.py:32
  78.4 5.3 %collective-permute-done.13.refs_3_ = f32[544,256]{1,0:T(8,128)} collective-permute-done((f32[544,256]{1,0:T(8,128)S(1)}, f32[544,256]{1,0:T(8,128)}, u32[]{:S(2)}, u32[]{:S(2)}) %collective-permute-start.13) | collective-permute-done | bytes 557088 | tf_op jit(solution)/shard_map/ppermute | solution.py:410
  83.8 5.2 %collective-permute-done.12.refs_2_ = f32[384,256]{1,0:T(8,128)} collective-permute-done((f32[384,256]{1,0:T(8,128)}, f32[384,256]{1,0:T(8,128)}, u32[]{:S(2)}, u32[]{:S(2)}) %collective-permute-start.12) | collective-permute-done | bytes 393248 | tf_op jit(solution)/shard_map/ppermute | solution.py:423
  89.0 3.2 %join.5.refs_0_.refs_2_ = f32[2048,512]{1,0:T(8,128)} custom-call(s32[2]{0:T(128)} %copy-done.8, f32[576,256]{1,0:T(8,128)} %collective-permute-done.11.refs_1_, f32[384,256]{1,0:T(8,128)} %collective-permute-done.12.refs_2_, f32[544,256]{1,0:T(8,128)} %collective-permute-done.13.refs_3_, f32[544,256]{1,0:T(8,128)} %copy-done.6, ...), custom_call_target="tpu_custom_call", output_to_operand_aliasing={{}: (7, {})} | custom-call | tf_op jit(solution)/shard_map/join/pallas_call | solution.py:32
  92.8 2.0 %collective-permute-done.7.refs_1_ = f32[896,256]{1,0:T(8,128)} collective-permute-done((f32[896,256]{1,0:T(8,128)}, f32[896,256]{1,0:T(8,128)}, u32[]{:S(2)}, u32[]{:S(2)}) %collective-permute-start.7) | collective-permute-done | bytes 917536 | tf_op jit(solution)/shard_map/ppermute | solution.py:407
  94.8 2.1 %join.6.refs_0_.refs_2_ = f32[2048,512]{1,0:T(8,128)} custom-call(s32[2]{0:T(128)} %copy-done.8, f32[896,256]{1,0:T(8,128)} %collective-permute-done.7.refs_1_, f32[2048,512]{1,0:T(8,128)} %join.5.refs_0_.refs_2_, f32[8,128]{1,0:T(8,128)} %mark.4.refs_3_), custom_call_target="tpu_custom_call", output_to_operand_aliasing={{}: (2, {})} | custom-call | tf_op jit(solution)/shard_map/join/pallas_call | solution.py:32
  99.6 1.6 %join.7 = f32[2048,512]{1,0:T(8,128)} custom-call(s32[2]{0:T(128)} %copy-done.8, f32[192,256]{1,0:T(8,128)} %copy-done.10, f32[2048,512]{1,0:T(8,128)} %join.6.refs_0_.refs_2_, f32[8,128]{1,0:T(8,128)} %mark.5.refs_3_), custom_call_target="tpu_custom_call", output_to_operand_aliasing={{}: (2, {})} | custom-call | tf_op jit(solution)/shard_map/join/pallas_call | solution.py:32
  (50 shorter events, 16.9 us)
Async XLA Ops:
  1.8 11.1 %collective-permute-start.1 = (f32[192,512]{1,0:T(8,128)}, f32[192,512]{1,0:T(8,128)}, u32[]{:S(2)}, u32[]{:S(2)}) collective-permute-start(f32[192,512]{1,0:T(8,128)} %slice.6.refs_2_), channel_id=1, source_target_pairs={{0,4},{4,0},{8,12},{12,8},{16,20},{20,16},{24,28},{28,24},{1,5},{5... | collective-permute-start | bytes 1179656 | tf_op jit(solution)/shard_map/ppermute | solution.py:377
  4.1 2.2 %copy-start = (f32[2048,512]{1,0:T(8,128)S(1)}, f32[2048,512]{1,0:T(8,128)}, u32[]{:S(2)}) copy-start(f32[2048,512]{1,0:T(8,128)} %refs_1_.3) | copy-start | bytes 12582916
  10.7 2.2 %copy-start.9 = (f32[448,512]{1,0:T(8,128)}, f32[448,512]{1,0:T(8,128)S(1)}, u32[]{:S(2)}) copy-start(f32[448,512]{1,0:T(8,128)S(1)} %get-tuple-element.32) | copy-start | bytes 2752516
  10.7 2.2 %collective-permute-start = (f32[528,128]{1,0:T(8,128)S(1)}, f32[528,128]{1,0:T(8,128)S(1)}, u32[]{:S(2)}, u32[]{:S(2)}) collective-permute-start(f32[528,128]{1,0:T(8,128)S(1)} %get-tuple-element.23), channel_id=1, source_target_pairs={{0,1},{1,0},{2,3},{3,2},{4,5},{5,4},{6,7},{7,6},{8,9},{9,8},{10,11... | collective-permute-start | bytes 811016 | tf_op jit(solution)/shard_map/ppermute | solution.py:387
  11.7 20.6 %collective-permute-start.5 = (f32[320,512]{1,0:T(8,128)S(1)}, f32[320,512]{1,0:T(8,128)}, u32[]{:S(2)}, u32[]{:S(2)}) collective-permute-start(f32[320,512]{1,0:T(8,128)S(1)} %slice.7.refs_3_), channel_id=1, source_target_pairs={{0,4},{4,0},{8,12},{12,8},{16,20},{20,16},{24,28},{28,24},{1,5},{5... | collective-permute-start | bytes 1966088 | tf_op jit(solution)/shard_map/ppermute | solution.py:377
  12.9 7.5 %collective-permute-start.2 = (f32[528,128]{1,0:T(8,128)S(1)}, f32[528,128]{1,0:T(8,128)S(1)}, u32[]{:S(2)}, u32[]{:S(2)}) collective-permute-start(f32[528,128]{1,0:T(8,128)S(1)} %add.68.refs_1_), channel_id=1, source_target_pairs={{0,2},{1,3},{2,0},{3,1},{4,6},{5,7},{6,4},{7,5},{8,10},{9,11},{10,... | collective-permute-start | bytes 811016 | tf_op jit(solution)/shard_map/ppermute | solution.py:388
  21.3 11.0 %collective-permute-start.3 = (f32[528,128]{1,0:T(8,128)}, f32[528,128]{1,0:T(8,128)S(1)}, u32[]{:S(2)}, u32[]{:S(2)}) collective-permute-start(f32[528,128]{1,0:T(8,128)} %get-tuple-element.24.refs_1_), channel_id=1, source_target_pairs={{0,1},{1,0},{2,3},{3,2},{4,5},{5,4},{6,7},{7,6},{8,9},{9,8},{10,11... | collective-permute-start | bytes 811016 | tf_op jit(solution)/shard_map/ppermute | solution.py:391
  22.7 8.3 %collective-permute-start.4 = (f32[264,128]{1,0:T(8,128)}, f32[264,128]{1,0:T(8,128)}, u32[]{:S(2)}, u32[]{:S(2)}) collective-permute-start(f32[264,128]{1,0:T(8,128)} %get-tuple-element.25), channel_id=1, source_target_pairs={{0,4},{4,0},{8,12},{12,8},{16,20},{20,16},{24,28},{28,24},{1,5},{5... | collective-permute-start | bytes 405512 | tf_op jit(solution)/shard_map/ppermute | solution.py:392
  23.1 28.8 %collective-permute-start.10 = (f32[448,512]{1,0:T(8,128)}, f32[448,512]{1,0:T(8,128)}, u32[]{:S(2)}, u32[]{:S(2)}) collective-permute-start(f32[448,512]{1,0:T(8,128)} %copy-done.9), channel_id=1, source_target_pairs={{0,4},{4,0},{8,12},{12,8},{16,20},{20,16},{24,28},{28,24},{1,5},{5... | collective-permute-start | bytes 2752520 | tf_op jit(solution)/shard_map/ppermute | solution.py:377
  31.0 14.1 %collective-permute-start.8 = (f32[264,128]{1,0:T(8,128)}, f32[264,128]{1,0:T(8,128)}, u32[]{:S(2)}, u32[]{:S(2)}) collective-permute-start(f32[264,128]{1,0:T(8,128)} %collective-permute-done.4.refs_3_.refs_1_), channel_id=1, source_target_pairs={{0,2},{1,3},{2,0},{3,1},{4,6},{5,7},{6,4},{7,5},{8,10},{9,11},{10,... | collective-permute-start | bytes 405512 | tf_op jit(solution)/shard_map/ppermute | solution.py:412
  41.2 4.9 %copy-start.2 = (bf16[512,512]{1,0:T(8,128)(2,1)}, bf16[512,512]{1,0:T(8,128)(2,1)S(1)}, u32[]{:S(2)}) copy-start(bf16[512,512]{1,0:T(8,128)(2,1)S(1)} %get-tuple-element.26.refs_0_.refs_2_) | copy-start | bytes 1572868
  41.2 4.9 %copy-start.4 = (bf16[512,512]{1,0:T(8,128)(2,1)}, bf16[512,512]{1,0:T(8,128)(2,1)S(1)}, u32[]{:S(2)}) copy-start(bf16[512,512]{1,0:T(8,128)(2,1)S(1)} %get-tuple-element.27.refs_1_.refs_3_) | copy-start | bytes 1572868
  46.9 4.9 %collective-permute-start.9 = (f32[528,128]{1,0:T(8,128)S(1)}, f32[528,128]{1,0:T(8,128)S(1)}, u32[]{:S(2)}, u32[]{:S(2)}) collective-permute-start(f32[528,128]{1,0:T(8,128)S(1)} %merge.1.refs_1_), channel_id=1, source_target_pairs={{0,1},{1,0},{2,3},{3,2},{4,5},{5,4},{6,7},{7,6},{8,9},{9,8},{10,11... | collective-permute-start | bytes 811016 | tf_op jit(solution)/shard_map/ppermute | solution.py:414
  48.6 46.2 %collective-permute-start.7 = (f32[896,256]{1,0:T(8,128)}, f32[896,256]{1,0:T(8,128)}, u32[]{:S(2)}, u32[]{:S(2)}) collective-permute-start(f32[896,256]{1,0:T(8,128)} %get-tuple-element.30.refs_3_), channel_id=1, source_target_pairs={{0,4},{4,0},{8,12},{12,8},{16,20},{20,16},{24,28},{28,24},{1,5},{5... | collective-permute-start | bytes 2752520 | tf_op jit(solution)/shard_map/ppermute | solution.py:407
  48.9 23.9 %collective-permute-start.14 = (f32[544,256]{1,0:T(8,128)}, f32[544,256]{1,0:T(8,128)}, u32[]{:S(2)}, u32[]{:S(2)}) collective-permute-start(f32[544,256]{1,0:T(8,128)} %get-tuple-element.37.refs_6_), channel_id=1, source_target_pairs={{8,4},{16,12},{24,20},{4,8},{12,16},{20,24},{9,5},{17,13},{25,21},... | collective-permute-start | bytes 1671176 | tf_op jit(solution)/shard_map/ppermute | solution.py:410
  51.9 15.6 %copy-start.7 = (f32[544,256]{1,0:T(8,128)S(1)}, f32[544,256]{1,0:T(8,128)}, u32[]{:S(2)}) copy-start(f32[544,256]{1,0:T(8,128)} %copy-done.6) | copy-start | bytes 1671172
  51.9 22.2 %copy-start.3 = (bf16[512,512]{1,0:T(8,128)(2,1)S(1)}, bf16[512,512]{1,0:T(8,128)(2,1)}, u32[]{:S(2)}) copy-start(bf16[512,512]{1,0:T(8,128)(2,1)} %copy-done.2) | copy-start | bytes 1572868
  51.9 22.2 %copy-start.5 = (bf16[512,512]{1,0:T(8,128)(2,1)S(1)}, bf16[512,512]{1,0:T(8,128)(2,1)}, u32[]{:S(2)}) copy-start(bf16[512,512]{1,0:T(8,128)(2,1)} %copy-done.4) | copy-start | bytes 1572868
  64.2 24.7 %collective-permute-start.11 = (f32[576,256]{1,0:T(8,128)S(1)}, f32[576,256]{1,0:T(8,128)}, u32[]{:S(2)}, u32[]{:S(2)}) collective-permute-start(f32[576,256]{1,0:T(8,128)S(1)} %get-tuple-element.35.refs_4_), channel_id=1, source_target_pairs={{12,4},{20,12},{28,20},{0,8},{8,16},{16,24},{13,5},{21,13},{29,21}... | collective-permute-start | bytes 1769480 | tf_op jit(solution)/shard_map/ppermute | solution.py:423
  67.5 16.3 %collective-permute-start.13 = (f32[544,256]{1,0:T(8,128)S(1)}, f32[544,256]{1,0:T(8,128)}, u32[]{:S(2)}, u32[]{:S(2)}) collective-permute-start(f32[544,256]{1,0:T(8,128)S(1)} %copy-done.7), channel_id=1, source_target_pairs={{8,4},{16,12},{24,20},{4,8},{12,16},{20,24},{9,5},{17,13},{25,21},... | collective-permute-start | bytes 1671176 | tf_op jit(solution)/shard_map/ppermute | solution.py:410
  69.4 19.6 %collective-permute-start.12 = (f32[384,256]{1,0:T(8,128)}, f32[384,256]{1,0:T(8,128)}, u32[]{:S(2)}, u32[]{:S(2)}) collective-permute-start(f32[384,256]{1,0:T(8,128)} %get-tuple-element.36), channel_id=1, source_target_pairs={{12,4},{20,12},{28,20},{0,8},{8,16},{16,24},{13,5},{21,13},{29,21}... | collective-permute-start | bytes 1179656 | tf_op jit(solution)/shard_map/ppermute | solution.py:423
  72.7 26.2 %collective-permute-start.6 = (f32[192,256]{1,0:T(8,128)}, f32[192,256]{1,0:T(8,128)S(1)}, u32[]{:S(2)}, u32[]{:S(2)}) collective-permute-start(f32[192,256]{1,0:T(8,128)} %get-tuple-element.29), channel_id=1, source_target_pairs={{0,4},{4,0},{8,12},{12,8},{16,20},{20,16},{24,28},{28,24},{1,5},{5... | collective-permute-start | bytes 589832 | tf_op jit(solution)/shard_map/ppermute | solution.py:407
  74.1 3.7 %copy-start.8 = (s32[2]{0:T(128)}, s32[2]{0:T(128)S(1)}, u32[]{:S(2)}) copy-start(s32[2]{0:T(128)S(1)} %pad_add_fusion.refs_0_) | copy-start | bytes 28
  74.1 2.2 %copy-start.1 = (f32[2048,512]{1,0:T(8,128)S(1)}, f32[2048,512]{1,0:T(8,128)}, u32[]{:S(2)}) copy-start(f32[2048,512]{1,0:T(8,128)} %refs_1_.3) | copy-start | bytes 12582916
  (2 other events, 1.5 us)
